TPU v7x, 128 devices: a whole 4x4x4 slice. The times are simulated.
128 devices in a mesh: group: 4 (over y), dev: 32 (over z, x, core).
Axes of the slice: x: 4, y: 4, z: 4, core: 2. Of those that a mesh axis runs over, the one named last changes fastest.
Arguments:
- atom_rows: float32 [4, 262144], P(None, ('group', 'dev')), may hold values from -0.5 to 0.5
- atom_owner: int32 [262144], P(('group', 'dev')), may hold values from 0 to 127, as said below
- atom_cell: int32 [262144], P(('group', 'dev')), may hold values from 0 to 1023
- need_cells: int32 [128, 128, 72], P(('group', 'dev')), may hold values from -1 to 1023, as said below
- list_entry: int32 [16, 131072], P(None, ('group', 'dev')), may hold values from 0 to 10239, as said below
- list_class: int32 [16, 131072], P(None, ('group', 'dev')), may hold values from 0 to 7
- basis_freq: float32 [121, 3], replicated, may hold values from -4 to 4
- basis_phase: float32 [121], replicated, may hold values from -3.140625 to 3.140625
- near_ops: float32 [8, 121, 121], replicated, may hold values from -0.125 to 0.125
- up_ops: float32 [8, 121, 121], replicated, may hold values from -0.046875 to 0.046875
- far_in: float32 [31, 121, 121], replicated, may hold values from -0.09375 to 0.09375
- far_out: float32 [3, 121, 121], replicated, may hold values from -0.046875 to 0.046875
- down_ops: float32 [8, 121, 121], replicated, may hold values from -0.5 to 0.5
Outputs:
- local_field: float32 [121, 131072], P(None, ('group', 'dev'))
- potential: float32 [327680], P(('group', 'dev'))
Inputs may be any that keep to these rules, and one draw needn't show every extreme that they name: `atom_owner`: an atom that changes device moves at most 2 positions along the curve. Of one device's rows, those sent to lower devices come first, the farther before the nearer, and those sent to higher devices come last, the nearer before the farther; the rest stay. At most 128 rows of one device name one other device, and for every offset some device sends exactly 128. `need_cells`: -1 marks an unused slot, and the used slots of a row come first. The cells asked of one device are consecutive cell numbers modulo 1024. No device asks itself; devices next to it on the curve (|s - t| = 1) are asked for exactly 72 cells, those two positions away for exactly 18, all others for 9 to 18. `list_entry`: each entry of a cell of device t is a column below 1024 or a column 1024 + s * 72 + j with need_cells[t, s, j] >= 0, and every such requested column appears in some entry of device t.
All inputs are finite; a program needn't handle non-finite values.
Results may differ from a plain program's by a relative error of at most 0.0003.
Values sent between devices are 32-bit elements; how exact they have to be, the bound alone decides.
No kernel may reach another device: no remote copies, remote signals or barrier semaphores. Data moves between devices by JAX's collectives and lax.ppermute only.
A program may use at most 64 MiB of HBM per device.

v0:
```python
import jax
import jax.numpy as jnp
from jax import lax
from jax.sharding import PartitionSpec as P

CELLS_DEV = 1024
REACH = 2
OCT = 8
CAP = 128


soften = 0.25
highest = lax.Precision.HIGHEST


def from_behind(value, axis, by):
    length = lax.axis_size(axis)
    pairs = [(i, i + by) for i in range(length) if 0 <= i + by < length]
    return lax.ppermute(value, axis, pairs)


def move_steps():
    return [step_by for step_by in range(-REACH, REACH + 1) if step_by != 0]


def outgoing(payload, offsets, step_by):
    chosen = (offsets == step_by).astype(jnp.int32)
    ranking = jnp.cumsum(chosen) - chosen
    slot_hot = (
        (ranking[None, :] == jnp.arange(CAP, dtype=jnp.int32)[:, None]) & (chosen[None, :] > 0)
    ).astype(jnp.float32)
    return lax.dot_general(payload, slot_hot, (((1,), (1,)), ((), ())), precision=highest)


def cell_index(arrived):
    return jnp.where(arrived[4] > 0.5, arrived[4] - 1.0, float(CELLS_DEV)).astype(jnp.int32)


def near_potential(arrived_dev):
    slot_count = arrived_dev.shape[1]
    block_rows = slot_count // max(1, slot_count // 512)

    def one_block(offset):
        picked = lax.dynamic_slice_in_dim(arrived_dev, offset, block_rows, 1)
        squared = jnp.zeros((block_rows, slot_count), jnp.float32)
        for axis_id in range(3):
            spacing = picked[axis_id][:, None] - arrived_dev[axis_id][None, :]
            squared = squared + spacing * spacing
        same_cell = picked[4][:, None] == arrived_dev[4][None, :]
        itself = (offset + jnp.arange(block_rows, dtype=jnp.int32))[:, None] == jnp.arange(
            slot_count, dtype=jnp.int32
        )[None, :]
        weights = jnp.where(
            same_cell & ~itself, arrived_dev[3][None, :] / jnp.sqrt(squared + soften), 0.0
        )
        return jnp.sum(weights, axis=1)

    starts = jnp.arange(slot_count // block_rows, dtype=jnp.int32) * block_rows
    return lax.map(one_block, starts).reshape(-1)


def near_apply(table_rows, entry_dev, class_dev, near_ops):
    coef_count = table_rows.shape[1]
    gathered = jnp.take(table_rows, entry_dev.reshape(-1), axis=0).reshape(
        entry_dev.shape[0], entry_dev.shape[1], coef_count
    )
    class_hot = (
        class_dev[None, :, :] == jnp.arange(near_ops.shape[0], dtype=jnp.int32)[:, None, None]
    ).astype(jnp.float32)
    by_class = jnp.einsum("lck,olc->ock", gathered, class_hot, precision=highest)
    return jnp.einsum("okj,ocj->kc", near_ops, by_class, precision=highest)


def far_terms(operators, sources, distance):
    op_count = operators.shape[0]
    chosen = (distance[:, None] == jnp.arange(op_count, dtype=jnp.int32)[None, :]).astype(
        jnp.float32
    )
    summed = jnp.einsum("bo,bj->oj", chosen, sources, precision=highest)
    return jnp.einsum("okj,oj->k", operators, summed, precision=highest)


def on_device(
    atom_rows,
    atom_owner,
    atom_cell,
    need_cells,
    list_entry,
    list_class,
    basis_freq,
    basis_phase,
    near_ops,
    up_ops,
    far_in,
    far_out,
    down_ops,
):
    members = lax.axis_size("dev")
    groups = lax.axis_size("group")
    cell_count = list_entry.shape[1]
    coef_count = basis_freq.shape[0]
    group_id = lax.axis_index("group")
    member_id = lax.axis_index("dev")
    my_index = group_id * members + member_id
    offsets = atom_owner - my_index
    payload = jnp.concatenate([atom_rows, (atom_cell + 1).astype(jnp.float32)[None, :]], axis=0)
    pieces = [jnp.where((offsets == 0)[None, :], payload, 0.0)]
    for step_by in move_steps():
        outbound = outgoing(payload, offsets, step_by)
        pieces.append(from_behind(outbound, ("group", "dev"), step_by))
    arrived = jnp.concatenate(pieces, axis=1)
    basis_vals = jnp.cos(
        jnp.dot(basis_freq, arrived[0:3], precision=highest) + basis_phase[:, None]
    )
    cell_ids = cell_index(arrived)
    cell_hot = (cell_ids[:, None] == jnp.arange(cell_count, dtype=jnp.int32)[None, :]).astype(
        jnp.float32
    )
    weighted = basis_vals * arrived[3][None, :]
    multipole = jnp.dot(weighted, cell_hot, precision=highest)
    pole_rows = jnp.concatenate([multipole.T, jnp.zeros((1, coef_count), jnp.float32)], axis=0)
    requests = need_cells[0]
    asked_cells = lax.all_to_all(
        requests, ("group", "dev"), split_axis=0, concat_axis=0, tiled=True
    )
    slot_ids = jnp.where(asked_cells >= 0, asked_cells, cell_count)
    rows_out = jnp.take(pole_rows, slot_ids.reshape(-1), axis=0).reshape(
        asked_cells.shape[0], asked_cells.shape[1], coef_count
    )
    picked = jnp.transpose(rows_out, (2, 0, 1))
    received = lax.all_to_all(
        picked, ("group", "dev"), split_axis=1, concat_axis=1, tiled=True
    ).reshape(coef_count, -1)
    table_rows = jnp.concatenate([multipole.T, received.T], axis=0)
    near_field = near_apply(table_rows, list_entry, list_class, near_ops)
    grouped = jnp.sum(multipole.reshape(coef_count, -1, OCT), axis=1)
    coarse = jnp.einsum("okj,jo->k", up_ops, grouped, precision=highest)
    all_coarse = lax.all_gather(coarse[None, :], ("group", "dev"), axis=0, tiled=True).reshape(
        groups, members, coef_count
    )
    own_group = lax.dynamic_index_in_dim(all_coarse, group_id, 0, keepdims=False)
    distance = jnp.abs(jnp.arange(members, dtype=jnp.int32) - member_id) - 1
    inner_field = far_terms(far_in, own_group, distance)
    group_sums = jnp.sum(all_coarse, axis=1)
    group_gap = jnp.abs(jnp.arange(groups, dtype=jnp.int32) - group_id) - 1
    far_field = inner_field + far_terms(far_out, group_sums, group_gap)
    down_terms = jnp.einsum("okj,j->ko", down_ops, far_field, precision=highest)
    local_field = near_field + jnp.tile(down_terms, (1, cell_count // OCT))
    local_at = lax.dot_general(local_field, cell_hot, (((1,), (1,)), ((), ())), precision=highest)
    far_part = jnp.sum(local_at * basis_vals, axis=0) * coef_count ** (-0.5)
    return (local_field, far_part + near_potential(arrived))


def solution(mesh):
    in_specs = (
        P(None, ("group", "dev")),
        P(("group", "dev")),
        P(("group", "dev")),
        P(("group", "dev"), None, None),
        P(None, ("group", "dev")),
        P(None, ("group", "dev")),
        P(),
        P(),
        P(),
        P(),
        P(),
        P(),
        P(),
    )
    out_specs = (P(None, ("group", "dev")), P(("group", "dev")))
    return jax.shard_map(
        on_device, mesh=mesh, in_specs=in_specs, out_specs=out_specs, check_vma=False
    )
```

profile of v0, /device:TPU:1, one launch (start us, length us, event | category | flops | bytes accessed | tf_op | source)
XLA Modules:
  0.0 316.4 jit_solution(14810940422108130440)
XLA Ops:
  0.7 0.8 convert_compare_fusion
  2.1 0.7 add_convert_fusion
  2.8 1.4 fusion.41
  4.2 1.3 collective-permute-start
  6.1 1.4 fusion.39
  7.5 3.3 %collective-permute-start.1 = (f32[5,128]{1,0:T(8,128)S(1)}, f32[5,128]{1,0:T(8,128)S(1)}, u32[]{:S(2)}, u32[]{:S(2)}) collective-permute-start(f32[5,128]{1,0:T(8,128)S(1)} %fusion.39), channel_id=1, source_target_pairs={{1,0},{2,1},{3,2},{4,3},{5,4},{6,5},{7,6},{8,7},{9,8},{10,9},{11,1... | collective-permute-start | bytes 7688 | tf_op jit(solution)/shard_map/ppermute | solution.py:19
  11.4 1.4 fusion.37
  12.8 4.2 %collective-permute-start.2 = (f32[5,128]{1,0:T(8,128)S(1)}, f32[5,128]{1,0:T(8,128)S(1)}, u32[]{:S(2)}, u32[]{:S(2)}) collective-permute-start(f32[5,128]{1,0:T(8,128)S(1)} %fusion.37), channel_id=1, source_target_pairs={{0,1},{1,2},{2,3},{3,4},{4,5},{5,6},{6,7},{7,8},{8,9},{9,10},{10,1... | collective-permute-start | bytes 7688 | tf_op jit(solution)/shard_map/ppermute | solution.py:19
  17.6 1.4 fusion.35
  18.9 3.2 %collective-permute-start.3 = (f32[5,128]{1,0:T(8,128)S(1)}, f32[5,128]{1,0:T(8,128)S(1)}, u32[]{:S(2)}, u32[]{:S(2)}) collective-permute-start(f32[5,128]{1,0:T(8,128)S(1)} %fusion.35), channel_id=1, source_target_pairs={{0,2},{1,3},{2,4},{3,5},{4,6},{5,7},{6,8},{7,9},{8,10},{9,11},{10,... | collective-permute-start | bytes 7688 | tf_op jit(solution)/shard_map/ppermute | solution.py:19
  22.1 1.5 copy.39
  23.6 14.0 %all-to-all-start = ((s32[128,1,72]{2,1,0:T(1,128)}), s32[128,1,72]{2,1,0:T(1,128)S(1)}, u32[]{:S(2)}, u32[]{:S(2)}) async-start(s32[128,1,72]{2,1,0:T(1,128)} %bitcast.17), calls=%async_computation | async-start | bytes 131072 | tf_op jit(solution)/shard_map/all_to_all | solution.py:123
  38.9 0.8 fusion.57
  39.6 0.9 compare_and_fusion.1
  40.5 0.9 copy.55
  41.5 1.8 copy.37
  43.9 6.0 %fusion.13 = f32[121,2560]{1,0:T(8,128)S(1)} fusion(f32[121,3]{0,1:T(4,128)} %param.21, f32[121]{0:T(128)} %param.22, f32[5,2560]{1,0:T(8,128)S(1)} %constant_dynamic-update-slice_fusion), kind=kOutput, calls=%fused_computation.30 | convolution fusion | flops 11461120 | bytes 1281936 | tf_op jit(solution)/shard_map/dot_general | solution.py:113
  49.9 1.0 copy-done.2
  50.9 3.8 %fusion.3 = f32[121,1024]{1,0:T(8,128)S(1)} fusion(s32[2560]{0:T(1024)S(1)} %fusion.63, f32[121,2560]{1,0:T(8,128)S(1)} %fusion.13, f32[2560]{0:T(1024)S(1)} %slice_reduce_fusion.5), kind=kOutput, calls=%fused_computation.15 | convolution fusion | flops 3809262080 | bytes 1755136 | tf_op jit(solution)/shard_map/dot_general | solution.py:120
  55.1 1.5 convolution_bitcast_fusion.3
  57.2 67.6 %all-reduce.1 = f32[15488]{0:T(1024)S(1)} all-reduce(f32[15488]{0:T(1024)S(1)} %dynamic-update-slice), channel_id=2, replica_groups=mesh['group'=4,'dev'=32] {'group','dev'}, use_global_device_ids=true, to_apply=%add.1 | all-reduce | flops 15488 | bytes 123904
  125.6 0.8 reduce.25
  126.7 31.0 %gather_fusion = f32[9216,121]{1,0:T(8,128)} fusion(f32[1025,121]{1,0:T(8,128)S(1)} %concatenate.14.clone, s32[9216]{0:T(1024)S(1)} %broadcast_clamp_fusion.1), kind=kCustom, calls=%fused_computation | custom fusion | bytes 8957952 | tf_op jit(solution)/shard_map/jit(_take)/gather | solution.py:127
  157.6 6.8 %select_bitcast_fusion = f32[121,128,72]{0,2,1:T(8,128)} fusion(f32[128,72,121]{2,1,0:T(8,128)} %bitcast.98, pred[128,72]{1,0:T(8,128)(4,1)S(1)} %compare_and_fusion), kind=kLoop, calls=%fused_computation.21 | loop fusion | flops 1115136 | bytes 8930304 | tf_op jit(solution)/shard_map/transpose | solution.py:130
  164.4 5.5 %all-to-all-start.1 = ((f32[121,128,72]{0,2,1:T(8,128)}), f32[121,128,72]{0,2,1:T(8,128)}, u32[]{:S(2)}, u32[]{:S(2)}) async-start(f32[121,128,72]{0,2,1:T(8,128)} %select_bitcast_fusion), calls=%async_computation.1 | async-start | bytes 9437184 | tf_op jit(solution)/shard_map/all_to_all | solution.py:131
  170.0 38.0 %while.10 = (s32[]{:T(128)}, f32[5,512]{1,0:T(8,128)S(1)}, s32[5]{0:T(128)S(1)}, f32[5,2560]{1,0:T(8,128)S(1)}, s32[]{:T(128)}, /*index=5*/s32[]{:T(128)}, s32[]{}, s32[]{:T(128)}, s32[]{}, s32[]{}) while((s32[]{:T(128)}, f32[5,512]{1,0:T(8,128)S(1)}, s32[5]{0:T(128)S(1)}, f32[5,2560]{1,0:T(8,128)S(1)}, s32[]{:T(128)}, ...), condition=%wide.region_13.14_spmd, body=%wide.region_11.13_spmd.sunk | while | flops 20971528 | bytes 188623 | solution.py:59
  170.1 0.6 dynamic_slice.17
  172.8 0.6 iota_add_fusion.2
  173.5 4.1 %select_reduce_fusion.2 = f32[512]{0:T(512)S(1)} fusion(f32[2560]{0:T(1024)S(1)} %get-tuple-element.99, f32[512]{0:T(512)S(1)} %bitcast.108, f32[2560]{0:T(1024)S(1)} %get-tuple-element.101, f32[512]{0:T(512)S(1)} %bitcast.106, f32[2560]{0:T(1024)S(1)} %get-tuple-element.103, f32[512]{0:T(512)S(1)} %bitcast.107, f32[2560]{0:T(1024)S(1)} %get-tuple-element.105, ...), kind=kLoop, calls=%fused_computation.2.clone.1 | loop fusion | flops 20971008 | bytes 63488 | tf_op jit(solution)/shard_map/while/body/eval_jaxpr/reduce_sum | solution.py:56
  177.6 0.6 dynamic_slice.17
  180.4 0.6 iota_add_fusion.2
  181.0 4.1 %select_reduce_fusion.2 = f32[512]{0:T(512)S(1)} fusion(f32[2560]{0:T(1024)S(1)} %get-tuple-element.99, f32[512]{0:T(512)S(1)} %bitcast.108, f32[2560]{0:T(1024)S(1)} %get-tuple-element.101, f32[512]{0:T(512)S(1)} %bitcast.106, f32[2560]{0:T(1024)S(1)} %get-tuple-element.103, f32[512]{0:T(512)S(1)} %bitcast.107, f32[2560]{0:T(1024)S(1)} %get-tuple-element.105, ...), kind=kLoop, calls=%fused_computation.2.clone.1 | loop fusion | flops 20971008 | bytes 63488 | tf_op jit(solution)/shard_map/while/body/eval_jaxpr/reduce_sum | solution.py:56
  185.2 0.6 dynamic_slice.17
  188.0 0.6 iota_add_fusion.2
  188.6 4.1 %select_reduce_fusion.2 = f32[512]{0:T(512)S(1)} fusion(f32[2560]{0:T(1024)S(1)} %get-tuple-element.99, f32[512]{0:T(512)S(1)} %bitcast.108, f32[2560]{0:T(1024)S(1)} %get-tuple-element.101, f32[512]{0:T(512)S(1)} %bitcast.106, f32[2560]{0:T(1024)S(1)} %get-tuple-element.103, f32[512]{0:T(512)S(1)} %bitcast.107, f32[2560]{0:T(1024)S(1)} %get-tuple-element.105, ...), kind=kLoop, calls=%fused_computation.2.clone.1 | loop fusion | flops 20971008 | bytes 63488 | tf_op jit(solution)/shard_map/while/body/eval_jaxpr/reduce_sum | solution.py:56
  192.8 0.6 dynamic_slice.17
  196.2 4.1 %select_reduce_fusion.2 = f32[512]{0:T(512)S(1)} fusion(f32[2560]{0:T(1024)S(1)} %get-tuple-element.99, f32[512]{0:T(512)S(1)} %bitcast.108, f32[2560]{0:T(1024)S(1)} %get-tuple-element.101, f32[512]{0:T(512)S(1)} %bitcast.106, f32[2560]{0:T(1024)S(1)} %get-tuple-element.103, f32[512]{0:T(512)S(1)} %bitcast.107, f32[2560]{0:T(1024)S(1)} %get-tuple-element.105, ...), kind=kLoop, calls=%fused_computation.2.clone.1 | loop fusion | flops 20971008 | bytes 63488 | tf_op jit(solution)/shard_map/while/body/eval_jaxpr/reduce_sum | solution.py:56
  200.4 0.6 dynamic_slice.17
  203.8 4.1 %select_reduce_fusion.2 = f32[512]{0:T(512)S(1)} fusion(f32[2560]{0:T(1024)S(1)} %get-tuple-element.99, f32[512]{0:T(512)S(1)} %bitcast.108, f32[2560]{0:T(1024)S(1)} %get-tuple-element.101, f32[512]{0:T(512)S(1)} %bitcast.106, f32[2560]{0:T(1024)S(1)} %get-tuple-element.103, f32[512]{0:T(512)S(1)} %bitcast.107, f32[2560]{0:T(1024)S(1)} %get-tuple-element.105, ...), kind=kLoop, calls=%fused_computation.2.clone.1 | loop fusion | flops 20971008 | bytes 63488 | tf_op jit(solution)/shard_map/while/body/eval_jaxpr/reduce_sum | solution.py:56
  208.6 2.5 fusion.26
  211.1 1.2 fusion.30
  213.0 15.4 %all-to-all-done.1 = f32[121,128,72]{0,2,1:T(8,128)} async-done(((f32[121,128,72]{0,2,1:T(8,128)}), f32[121,128,72]{0,2,1:T(8,128)}, u32[]{:S(2)}, u32[]{:S(2)}) %all-to-all-start.1) | async-done | bytes 4460576 | tf_op jit(solution)/shard_map/all_to_all | solution.py:131
  228.4 4.3 %pad_maximum_fusion = f32[10240,121]{1,0:T(8,128)} fusion(f32[9216,121]{1,0:T(8,128)} %bitcast.23, f32[1024,121]{1,0:T(8,128)S(1)} %copy.41), kind=kLoop, calls=%fused_computation.18 | loop fusion | flops 1239040 | bytes 9912320 | tf_op jit(solution)/shard_map/concatenate | solution.py:134
  232.7 57.0 %gather_fusion.1 = f32[16384,121]{1,0:T(8,128)} fusion(f32[10240,121]{1,0:T(8,128)} %pad_maximum_fusion, s32[16384]{0:T(1024)S(1)} %broadcast_clamp_fusion), kind=kCustom, calls=%fused_computation.1 | custom fusion | bytes 15925248 | tf_op jit(solution)/shard_map/jit(_take)/gather | solution.py:64
  289.6 15.2 %fusion.14 = f32[8,1024,121]{2,0,1:T(8,128)S(1)} fusion(f32[16,1024,121]{2,1,0:T(8,128)} %bitcast.97, pred[16,1024]{0,1:T(8,128)(4,1)S(1)} %copy.38, s32[16,1024]{0,1:T(8,128)S(1)} %copy-done.1), kind=kOutput, calls=%fused_computation.31 | convolution fusion | flops 192430080 | bytes 11976704 | tf_op jit(solution)/shard_map/lck,olc->ock/dot_general | solution.py:70
  304.9 3.7 %fusion.23 = f32[121,1024]{0,1:T(8,128)S(1)} fusion(f32[8,1024,121]{2,0,1:T(8,128)S(1)} %fusion.14, f32[8,121,121]{2,0,1:T(8,128)S(1)} %copy-done.4, f32[121,8]{0,1:T(8,128)S(1)} %bitcast.116), kind=kOutput, calls=%fused_computation.38 | convolution fusion | flops 1439392768 | bytes 4932928 | tf_op jit(solution)/shard_map/okj,ocj->kc/dot_general | solution.py:71
  308.6 6.3 %fusion.19 = f32[2560]{0:T(1024)S(1)} fusion(f32[121,2560]{1,0:T(8,128)S(1)} %copy-done.3, f32[121,1024]{0,1:T(8,128)S(1)} %fusion.23, s32[2560]{0:T(1024)S(1)} %copy-done.8), kind=kOutput, calls=%fused_computation.36 | convolution fusion | flops 3809569280 | bytes 1755136 | tf_op jit(solution)/shard_map/dot_general | solution.py:149
  314.8 1.0 copy.46
  (98 shorter events, 10.4 us)
Async XLA Ops:
  0.6 207.9 %copy-start = (f32[31,121,121]{2,0,1:T(8,128)S(1)}, f32[31,121,121]{2,0,1:T(8,128)}, u32[]{:S(2)}) copy-start(f32[31,121,121]{2,0,1:T(8,128)} %param.25) | copy-start | bytes 5446456
  4.2 39.5 %collective-permute-start = (f32[5,128]{1,0:T(8,128)S(1)}, f32[5,128]{1,0:T(8,128)S(1)}, u32[]{:S(2)}, u32[]{:S(2)}) collective-permute-start(f32[5,128]{1,0:T(8,128)S(1)} %fusion.41), channel_id=1, source_target_pairs={{2,0},{3,1},{4,2},{5,3},{6,4},{7,5},{8,6},{9,7},{10,8},{11,9},{12,... | collective-permute-start | bytes 7688 | tf_op jit(solution)/shard_map/ppermute | solution.py:19
  7.5 36.2 %collective-permute-start.1 = (f32[5,128]{1,0:T(8,128)S(1)}, f32[5,128]{1,0:T(8,128)S(1)}, u32[]{:S(2)}, u32[]{:S(2)}) collective-permute-start(f32[5,128]{1,0:T(8,128)S(1)} %fusion.39), channel_id=1, source_target_pairs={{1,0},{2,1},{3,2},{4,3},{5,4},{6,5},{7,6},{8,7},{9,8},{10,9},{11,1... | collective-permute-start | bytes 7688 | tf_op jit(solution)/shard_map/ppermute | solution.py:19
  12.8 30.9 %collective-permute-start.2 = (f32[5,128]{1,0:T(8,128)S(1)}, f32[5,128]{1,0:T(8,128)S(1)}, u32[]{:S(2)}, u32[]{:S(2)}) collective-permute-start(f32[5,128]{1,0:T(8,128)S(1)} %fusion.37), channel_id=1, source_target_pairs={{0,1},{1,2},{2,3},{3,4},{4,5},{5,6},{6,7},{7,8},{8,9},{9,10},{10,1... | collective-permute-start | bytes 7688 | tf_op jit(solution)/shard_map/ppermute | solution.py:19
  18.9 24.8 %collective-permute-start.3 = (f32[5,128]{1,0:T(8,128)S(1)}, f32[5,128]{1,0:T(8,128)S(1)}, u32[]{:S(2)}, u32[]{:S(2)}) collective-permute-start(f32[5,128]{1,0:T(8,128)S(1)} %fusion.35), channel_id=1, source_target_pairs={{0,2},{1,3},{2,4},{3,5},{4,6},{5,7},{6,8},{7,9},{8,10},{9,11},{10,... | collective-permute-start | bytes 7688 | tf_op jit(solution)/shard_map/ppermute | solution.py:19
  23.6 101.4 %all-to-all-start = ((s32[128,1,72]{2,1,0:T(1,128)}), s32[128,1,72]{2,1,0:T(1,128)S(1)}, u32[]{:S(2)}, u32[]{:S(2)}) async-start(s32[128,1,72]{2,1,0:T(1,128)} %bitcast.17), calls=%async_computation | async-start | bytes 131072 | tf_op jit(solution)/shard_map/all_to_all | solution.py:123
  43.8 13.1 %copy-start.7 = (s32[2560]{0:T(1024)}, s32[2560]{0:T(1024)S(1)}, u32[]{:S(2)}) copy-start(s32[2560]{0:T(1024)S(1)} %fusion.63) | copy-start | bytes 30724
  49.9 1.1 copy-start.2
  164.4 5.6 %copy-start.6 = (f32[5,512]{1,0:T(8,128)S(1)}, f32[5,512]{1,0:T(8,128)}, u32[]{:S(2)}) copy-start(f32[5,512]{1,0:T(8,128)} %custom-call.5) | copy-start | bytes 30724
  164.4 63.9 %all-to-all-start.1 = ((f32[121,128,72]{0,2,1:T(8,128)}), f32[121,128,72]{0,2,1:T(8,128)}, u32[]{:S(2)}, u32[]{:S(2)}) async-start(f32[121,128,72]{0,2,1:T(8,128)} %select_bitcast_fusion), calls=%async_computation.1 | async-start | bytes 9437184 | tf_op jit(solution)/shard_map/all_to_all | solution.py:131
  170.0 38.0 %copy-start.10 = (s32[32]{0:T(128)S(1)}, s32[32]{0:T(128)}, u32[]{:S(2)}) copy-start(s32[32]{0:T(128)} %abs_add_fusion.1) | copy-start | bytes 388
  170.0 38.3 %copy-start.9 = (s32[4]{0:T(128)S(1)}, s32[4]{0:T(128)}, u32[]{:S(2)}) copy-start(s32[4]{0:T(128)} %abs_add_fusion) | copy-start | bytes 52
  170.0 42.3 %copy-start.5 = (f32[8,121,121]{2,0,1:T(8,128)S(1)}, f32[8,121,121]{2,0,1:T(8,128)}, u32[]{:S(2)}) copy-start(f32[8,121,121]{2,0,1:T(8,128)} %param.27) | copy-start | bytes 1405540
  232.7 57.0 %copy-start.1 = (s32[16,1024]{0,1:T(8,128)S(1)}, s32[16,1024]{0,1:T(8,128)}, u32[]{:S(2)}) copy-start(s32[16,1024]{0,1:T(8,128)} %copy.37) | copy-start | bytes 196612
  289.6 15.2 %copy-start.4 = (f32[8,121,121]{2,0,1:T(8,128)S(1)}, f32[8,121,121]{2,0,1:T(8,128)}, u32[]{:S(2)}) copy-start(f32[8,121,121]{2,0,1:T(8,128)} %param.23) | copy-start | bytes 1405540
  304.8 3.7 %copy-start.3 = (f32[121,2560]{1,0:T(8,128)S(1)}, f32[121,2560]{1,0:T(8,128)}, u32[]{:S(2)}) copy-start(f32[121,2560]{1,0:T(8,128)} %copy-done.2) | copy-start | bytes 3717124
  304.8 3.7 %copy-start.8 = (s32[2560]{0:T(1024)S(1)}, s32[2560]{0:T(1024)}, u32[]{:S(2)}) copy-start(s32[2560]{0:T(1024)} %copy-done.7) | copy-start | bytes 30724
where the time goes:
time: 318 us; the launch traced here: 316 us
  local copies, waits for them, and re-layouts  102 us (32%)
  blocking collectives  67.6 us (21%)
  matrix products  46.8 us (15%)
  other arithmetic  42.6 us (13%)
  starting transfers between devices  31.6 us (10%)
  waiting for transfers between devices  15.4 us (5%)
  loops' own time  9.65 us (3%)
    unnamed x1, blocking collectives  67.6 us
    gather x1, local copies, waits for them, and re-layouts, near_apply(): jnp.take(table_rows, entry_dev.reshape(-1), axis=0)  57 us
    gather x1, local copies, waits for them, and re-layouts, on_device(): jnp.take(pole_rows, slot_ids.reshape(-1), axis=0)  31 us
    reduce_sum x5, other arithmetic, one_block(): return jnp.sum(weights, axis=1)  20.6 us
    all_to_all x1, waiting for transfers between devices, on_device(): lax.all_to_all(picked, ('group', 'dev'), split_axis=1, concat_axis=1, til...  15.4 us
    dot_general x1, matrix products, near_apply(): jnp.einsum('lck,olc->ock', gathered, class_hot, precision=highest)  15.2 us
    all_to_all x1, starting transfers between devices, on_device(): lax.all_to_all(requests, ('group', 'dev'), split_axis=0, concat_axis=0, t...  14 us
    ppermute x4, starting transfers between devices, from_behind(): return lax.ppermute(value, axis, pairs)  12 us
  transfers between devices with their start and end apart: 6, of which 1 were waited for; matrix products, arithmetic and copies ran while one was open for 19% of the time, Pallas kernels for 0%

commit v1 on v0

v1 whole, which is shorter than its diff:
```python
import math

import jax
import jax.numpy as jnp
from jax import lax
from jax.experimental import pallas as pl
from jax.experimental.pallas import tpu as pltpu
from jax.sharding import PartitionSpec as P

COEF = 121
LANES = 128
CELLS = 1024
STAY = 2048
CAP = 128
ARRIVE = 4 * CAP
SLOTS = STAY + ARRIVE
LIST = 16
OPS = 8
SLOT = 72
SHORT = 18
BLOCK = SHORT + 1
DEVICES = 128
MEMBERS = 32
GROUPS = 4
EXTRA = 56
FAR_ROWS = DEVICES * BLOCK
REMOTE = FAR_ROWS + 2 * EXTRA
WRAP = CELLS + 80
AXES = ("group", "dev")
MIB = 2**20
f32, bf16, i32 = jnp.float32, jnp.bfloat16, jnp.int32
SIN = [(-1) ** n * (2 * math.pi) ** (2 * n + 1) / math.factorial(2 * n + 1) for n in range(6)]

NT = (((1,), (1,)), ((), ()))
NN = (((1,), (0,)), ((), ()))


def shift(value, by):
    pairs = [(i, i + by) for i in range(DEVICES) if 0 <= i + by < DEVICES]
    return lax.ppermute(value, AXES, pairs)


def split(value):
    high = value.astype(bf16)
    return high, (value - high.astype(f32)).astype(bf16)


def basis_of(waves, atoms):
    turns = waves[:, 3:4] + waves[:, 0:1] * atoms[0:1, :]
    turns = turns + waves[:, 1:2] * atoms[1:2, :]
    turns = turns + waves[:, 2:3] * atoms[2:3, :]
    turns = turns - jnp.floor(turns + 0.5)
    base = 0.25 - jnp.abs(turns)
    square = base * base
    total = jnp.full_like(square, SIN[5])
    for factor in SIN[4::-1]:
        total = total * square + factor
    return base * total


def cell_hot(cell_row):
    ids = lax.broadcasted_iota(i32, (CELLS, cell_row.shape[1]), 0) + 1
    return jnp.where(ids == cell_row, 1.0, 0.0).astype(bf16)


def poles(basis, charge, hot):
    high, low = split(basis * charge)
    both = lax.dot_general(hot, jnp.concatenate([high, low], axis=0), NT, preferred_element_type=f32)
    return both[:, :LANES] + both[:, LANES:]


def pack_kernel(me_ref, owner_ref, rows_ref, cell_ref, m2_ref, m1_ref, p1_ref, p2_ref, buf):
    gap = owner_ref[...] - me_ref[0]

    def count(by):
        return jnp.sum(jnp.where(gap == by, 1.0, 0.0)).astype(i32)

    buf[...] = jnp.zeros_like(buf)
    for at, lo in ((0, 0), (256, STAY - 256)):
        buf[0:4, at : at + 256] = rows_ref[:, lo : lo + 256]
        buf[4:5, at : at + 256] = (cell_ref[:, lo : lo + 256] + 1).astype(f32)
    lane = lax.broadcasted_iota(i32, (8, CAP), 1)
    low2, low1, up1, up2 = count(-2), count(-1), count(1), count(2)
    m2_ref[...] = jnp.where(lane < low2, buf[:, :CAP], 0.0)
    ahead = pltpu.roll(buf[:, :256], lax.rem(256 - low2, 256), 1)
    m1_ref[...] = jnp.where(lane < low1, ahead[:, :CAP], 0.0)
    behind = pltpu.roll(buf[:, 256:], lax.rem(up1 + up2, 256), 1)
    p1_ref[...] = jnp.where(lane < up1, behind[:, :CAP], 0.0)
    last = pltpu.roll(buf[:, 256:], lax.rem(up2, 256), 1)
    p2_ref[...] = jnp.where(lane < up2, last[:, :CAP], 0.0)


def order_kernel(me_ref, entry_ref, class_ref, own_ref, far_ref, count_ref):
    entry, kind = entry_ref[...], class_ref[...]
    own_ref[...] = jnp.where(entry < CELLS, kind * CELLS + entry, OPS * CELLS)
    asked = jnp.maximum(entry - CELLS, 0)
    source = jnp.floor((asked.astype(f32) + 0.5) * (1.0 / SLOT)).astype(i32)
    slot = asked - source * SLOT
    side = jnp.where(source < me_ref[0], FAR_ROWS, FAR_ROWS + EXTRA)
    row = jnp.where(slot < SHORT, source * BLOCK + slot, side + slot - SHORT)
    key = jnp.where(entry < CELLS, -1, kind * REMOTE + row)
    keys = [key[l] for l in range(LIST)]
    used = keys[0] * 0
    for one in keys:
        used = used + jnp.where(one >= 0, 1, 0)
    step = 1
    while step < LIST:
        gap = step
        while gap >= 1:
            for base in range(gap % step, LIST - gap, 2 * gap):
                for i in range(min(gap, LIST - base - gap)):
                    a, b = base + i, base + i + gap
                    if a // (2 * step) == b // (2 * step):
                        keys[a], keys[b] = jnp.maximum(keys[a], keys[b]), jnp.minimum(keys[a], keys[b])
            gap //= 2
        step *= 2
    for l in range(LIST):
        far_ref[l] = jnp.where(keys[l] < 0, OPS * REMOTE, keys[l])
    count_ref[...] = jnp.max(used, axis=0, keepdims=True)


def stay_kernel(me_ref, owner_ref, rows_ref, cell_ref, waves_ref, atoms_ref, basis_ref, pole_ref):
    stays = owner_ref[...] == me_ref[0]
    atoms_ref[...] = jnp.zeros_like(atoms_ref)
    atoms_ref[0:4, :] = jnp.where(stays, rows_ref[...], 0.0)
    atoms_ref[4:5, :] = jnp.where(stays, (cell_ref[...] + 1).astype(f32), 0.0)
    width = 512
    for lo in range(0, STAY, width):
        atoms = atoms_ref[:, lo : lo + width]
        basis = basis_of(waves_ref[...], atoms)
        basis_ref[:, lo : lo + width] = basis
        part = poles(basis, atoms[3:4, :], cell_hot(atoms[4:5, :].astype(i32)))
        pole_ref[...] = part if lo == 0 else pole_ref[...] + part


def merge_kernel(
    me_ref, first_ref, m2_ref, m1_ref, p1_ref, p2_ref, waves_ref, stay_ref, up_ref,
    send_ref, low_ref, high_ref, pole_ref, basis_ref, atoms_ref, ring, turned,
):
    for at, ref in enumerate((m2_ref, m1_ref, p1_ref, p2_ref)):
        atoms_ref[:, at * CAP : (at + 1) * CAP] = ref[...]
    atoms = atoms_ref[...]
    basis = basis_of(waves_ref[...], atoms)
    basis_ref[...] = basis
    pole = stay_ref[...] + poles(basis, atoms[3:4, :], cell_hot(atoms[4:5, :].astype(i32)))
    pole_ref[...] = pole
    ring[0:CELLS, :] = pole
    ring[CELLS:WRAP, :] = pole[0 : WRAP - CELLS, :]
    grouped = jnp.sum(pole.reshape(CELLS // 8, 8, LANES), axis=0)
    raised = up_ref[...].reshape(COEF, OPS, COEF) * grouped[None, :, :COEF]
    turned[...] = jnp.zeros_like(turned)
    turned[0:COEF, 0:COEF] = jnp.sum(raised, axis=1)
    coarse = jnp.sum(turned[...].T, axis=0, keepdims=True)

    def one(t, _):
        start = jnp.maximum(first_ref[t], 0)
        send_ref[pl.ds(t * BLOCK, SHORT), :] = ring[pl.ds(start, SHORT), :]
        send_ref[pl.ds(t * BLOCK + SHORT, 1), :] = coarse
        return 0

    lax.fori_loop(0, DEVICES, one, 0, unroll=4)
    me = me_ref[0]
    below = jnp.maximum(first_ref[jnp.maximum(me - 1, 0)], 0)
    above = jnp.maximum(first_ref[jnp.minimum(me + 1, DEVICES - 1)], 0)
    low_ref[...] = ring[pl.ds(below + SHORT, EXTRA), :]
    high_ref[...] = ring[pl.ds(above + SHORT, EXTRA), :]


def load_ops(ops_ref, both, low):
    both[...] = jnp.zeros_like(both)
    low[...] = jnp.zeros_like(low)
    for o in range(OPS):
        one_high, one_low = split(ops_ref[pl.ds(o, COEF, stride=OPS), :])
        both[o * LANES : o * LANES + COEF, 0:COEF] = one_high
        both[o * LANES : o * LANES + COEF, LANES : LANES + COEF] = one_high
        low[o * LANES : o * LANES + COEF, 0:COEF] = one_low


def premultiply(rows, both, low):
    high, rest = split(rows)
    out = lax.dot_general(jnp.concatenate([high, rest], axis=1), both[...], NT, preferred_element_type=f32)
    return out + lax.dot_general(high, low[...], NT, preferred_element_type=f32)


def mid_kernel(own_ref, stay_ref, new_ref, pole_ref, ops_ref, sum_ref, pair_ref, table, both, low, cols, atoms_ref):
    atoms_ref[:, 0:STAY] = stay_ref[...]
    atoms_ref[:, STAY:] = new_ref[...]
    load_ops(ops_ref, both, low)
    width = 128

    def apply(i, _):
        lo = pl.multiple_of(i * width, width)
        out = premultiply(pole_ref[pl.ds(lo, width), :], both, low)
        for o in range(OPS):
            table[pl.ds(o * CELLS + lo, width), :] = out[:, o * LANES : (o + 1) * LANES]
        return 0

    lax.fori_loop(0, CELLS // width, apply, 0)
    table[OPS * CELLS :, :] = jnp.zeros((8, LANES), f32)

    def gather(g, _):
        for r in range(8):
            total = None
            for l in range(LIST):
                row = table[pl.ds(own_ref[l * CELLS + r * LANES + g], 1), :]
                total = row if total is None else total + row
            sum_ref[pl.ds(r * LANES + g, 1), :] = total
        return 0

    lax.fori_loop(0, LANES, gather, 0)

    for lo in range(0, SLOTS, LANES):
        cols[lo : lo + LANES, :] = atoms_ref[:, lo : lo + LANES].T
    pair_ref[...] = jnp.zeros_like(pair_ref)
    wide = 512
    for lo in range(0, SLOTS, wide):
        across = atoms_ref[:, lo : lo + wide]

        def pairs(i, total):
            down = cols[pl.ds(pl.multiple_of(i * 8, 8), 8), :]
            gap = down[:, 0:1] - across[0:1, :]
            far = gap * gap + 0.25
            gap = down[:, 1:2] - across[1:2, :]
            far = far + gap * gap
            gap = down[:, 2:3] - across[2:3, :]
            far = far + gap * gap
            charge = jnp.where(down[:, 4:5] == across[4:5, :], down[:, 3:4], 0.0)
            return total + charge * lax.rsqrt(far)

        total = lax.fori_loop(0, SLOTS // 8, pairs, jnp.zeros((8, wide), f32), unroll=8)
        itself = across[3:4, :] * lax.rsqrt(jnp.full((1, wide), 0.25, f32))
        pair_ref[:, lo : lo + wide] = jnp.sum(total, axis=0, keepdims=True) - itself


def last_kernel(
    me_ref, index_ref, count_ref, far_ref, below_ref, above_ref, ops_ref, sum_ref, inner_ref, outer_ref, down_ref,
    stay_ref, new_ref, stay_basis_ref, new_basis_ref, pair_ref, local_ref, pot_ref,
    table, both, low, rows, coarse,
):
    load_ops(ops_ref, both, low)

    def apply(rows_in, at):
        out = premultiply(rows_in, both, low)
        for o in range(OPS):
            table[pl.ds(o * REMOTE + at, rows_in.shape[0]), :] = out[:, o * LANES : (o + 1) * LANES]

    width = 128

    def step(i, _):
        lo = pl.multiple_of(i * width, width)
        apply(far_ref[pl.ds(lo, width), :], lo)
        return 0

    lax.fori_loop(0, FAR_ROWS // width, step, 0)
    apply(below_ref[...], FAR_ROWS)
    apply(above_ref[...], FAR_ROWS + EXTRA)
    table[OPS * REMOTE :, :] = jnp.zeros((8, LANES), f32)

    coarse[...] = far_ref[pl.ds(SHORT, DEVICES, stride=BLOCK), :]
    me = me_ref[0]
    group, member = me // MEMBERS, lax.rem(me, MEMBERS)
    who = lax.broadcasted_iota(i32, (40, DEVICES), 1)
    which = lax.broadcasted_iota(i32, (40, DEVICES), 0)
    its_group, its_member = who // MEMBERS, lax.rem(who, MEMBERS)
    near = (its_group == group) & (jnp.abs(its_member - member) - 1 == which) & (which < MEMBERS)
    away = (jnp.abs(its_group - group) - 1 == which - MEMBERS) & (which >= MEMBERS)
    chosen = jnp.where(near | away, 1.0, 0.0)
    sums = lax.dot_general(chosen, coarse[...], NN, precision=lax.Precision.HIGHEST, preferred_element_type=f32)
    field = jnp.sum(inner_ref[...] * sums[None, 0 : MEMBERS - 1, 0:COEF], axis=1)
    for o in range(GROUPS - 1):
        field = field + outer_ref[o] * sums[MEMBERS + o : MEMBERS + o + 1, 0:COEF]
    field = jnp.broadcast_to(jnp.sum(field, axis=1, keepdims=True), (COEF, LANES))
    child = lax.rem(lax.broadcasted_iota(i32, (COEF, LANES), 1), OPS)
    pattern = jnp.zeros((COEF, LANES), f32)
    for o in range(OPS):
        one = lax.dot_general(
            down_ref[pl.ds(o, COEF, stride=OPS), :], field, NN,
            precision=lax.Precision.HIGHEST, preferred_element_type=f32,
        )
        pattern = jnp.where(child == o, one, pattern)

    def gather(g, _):
        def more(l, totals):
            return tuple(
                totals[r] + table[pl.ds(index_ref[l * CELLS + r * LANES + g], 1), :] for r in range(8)
            )

        start = tuple(sum_ref[pl.ds(r * LANES + g, 1), :] for r in range(8))
        totals = lax.fori_loop(0, count_ref[g], more, start)
        for r in range(8):
            rows[pl.ds(r * LANES + g, 1), :] = totals[r]
        return 0

    lax.fori_loop(0, LANES, gather, 0)

    for lo in range(0, CELLS, LANES):
        local_ref[:, lo : lo + LANES] = rows[lo : lo + LANES, :].T[0:COEF, :] + pattern
    local = local_ref[...]
    high, rest = split(local)
    high = jnp.concatenate([high, jnp.zeros((LANES - COEF, CELLS), bf16)], axis=0)
    rest = jnp.concatenate([rest, jnp.zeros((LANES - COEF, CELLS), bf16)], axis=0)
    stacked = jnp.concatenate([high, rest], axis=0)
    wide = 512
    for lo in range(0, SLOTS, wide):
        if lo < STAY:
            cells, basis = stay_ref[4:5, lo : lo + wide], stay_basis_ref[:, lo : lo + wide]
        else:
            cells, basis = new_ref[4:5, :], new_basis_ref[...]
        at = lax.dot_general(stacked, cell_hot(cells.astype(i32)), NN, preferred_element_type=f32)
        read = jnp.sum((at[:LANES] + at[LANES:]) * basis, axis=0, keepdims=True)
        pot_ref[:, lo : lo + wide] = read * COEF**-0.5 + pair_ref[:, lo : lo + wide]


VM = pl.BlockSpec(memory_space=pltpu.VMEM)
SM = pl.BlockSpec(memory_space=pltpu.SMEM)


def call(kernel, name, ins, outs, scratch, limit, flops, *operands):
    cost = pl.CostEstimate(flops=flops, bytes_accessed=4 * MIB, transcendentals=0)
    return pl.pallas_call(
        kernel,
        name=name,
        in_specs=ins,
        out_specs=[VM] * len(outs),
        out_shape=[jax.ShapeDtypeStruct(shape, kind) for shape, kind in outs],
        scratch_shapes=scratch,
        cost_estimate=cost,
        compiler_params=pltpu.CompilerParams(vmem_limit_bytes=limit * MIB),
    )(*operands)


def on_device(
    atom_rows,
    atom_owner,
    atom_cell,
    need_cells,
    list_entry,
    list_class,
    basis_freq,
    basis_phase,
    near_ops,
    up_ops,
    far_in,
    far_out,
    down_ops,
):
    me = (lax.axis_index("group") * MEMBERS + lax.axis_index("dev")).reshape(1).astype(i32)
    first = lax.all_to_all(need_cells[0, :, 0].reshape(DEVICES, 1, 1), AXES, split_axis=0, concat_axis=0, tiled=True)
    first = first.reshape(DEVICES)
    waves = jnp.concatenate([basis_freq, basis_phase[:, None]], axis=1) * (0.5 / math.pi)
    waves = jnp.pad(waves, ((0, LANES - COEF), (0, 4)))
    owner_row, cell_row = atom_owner.reshape(1, STAY), atom_cell.reshape(1, STAY)
    by_row = [ops.transpose(1, 0, 2).reshape(COEF * OPS, COEF) for ops in (near_ops, up_ops, down_ops)]

    piece = ((8, CAP), f32)
    outbound = call(
        pack_kernel, "pack", [SM, VM, VM, VM], [piece] * 4, [pltpu.VMEM((8, 512), f32)], 16, 10**6,
        me, atom_owner.reshape(STAY // LANES, LANES), atom_rows, cell_row,
    )
    pieces = [shift(out, by) for out, by in zip(outbound, (-2, -1, 1, 2))]

    shape3 = (LIST, CELLS // LANES, LANES)
    own_index, far_index, counts = call(
        order_kernel, "order", [SM, VM, VM], [(shape3, i32), (shape3, i32), ((1, LANES), i32)], [], 16, 10**6,
        me, list_entry.reshape(shape3), list_class.reshape(shape3),
    )
    stay_atoms, stay_basis, stay_pole = call(
        stay_kernel, "stay", [SM, VM, VM, VM, VM],
        [((8, STAY), f32), ((LANES, STAY), f32), ((CELLS, LANES), f32)], [], 32, 4 * 10**9,
        me, owner_row, atom_rows, cell_row, waves,
    )
    send, low, high, pole, new_basis, new_atoms = call(
        merge_kernel, "merge", [SM, SM, VM, VM, VM, VM, VM, VM, VM],
        [((FAR_ROWS, LANES), f32), ((EXTRA, LANES), f32), ((EXTRA, LANES), f32), ((CELLS, LANES), f32),
         ((LANES, ARRIVE), f32), ((8, ARRIVE), f32)],
        [pltpu.VMEM((WRAP, LANES), f32), pltpu.VMEM((LANES, LANES), f32)], 32, 2 * 10**9,
        me, first, *pieces, waves, stay_pole, by_row[1],
    )
    below, above = shift(high, 1), shift(low, -1)
    far_rows = lax.all_to_all(send.reshape(DEVICES, 1, BLOCK * LANES), AXES, split_axis=0, concat_axis=0, tiled=True)
    far_rows = far_rows.reshape(FAR_ROWS, LANES)
    split_ops = [pltpu.VMEM((OPS * LANES, 2 * LANES), bf16), pltpu.VMEM((OPS * LANES, LANES), bf16)]
    own_sum, pair = call(
        mid_kernel, "mid", [SM, VM, VM, VM, VM], [((CELLS, LANES), f32), ((1, SLOTS), f32)],
        [pltpu.VMEM((OPS * CELLS + 8, LANES), f32), *split_ops, pltpu.VMEM((SLOTS, 8), f32), pltpu.VMEM((8, SLOTS), f32)],
        32, 20 * 10**9,
        own_index.reshape(-1), stay_atoms, new_atoms, pole, by_row[0],
    )
    local, pot = call(
        last_kernel, "last", [SM, SM, SM] + [VM] * 13, [((COEF, CELLS), f32), ((1, SLOTS), f32)],
        [pltpu.VMEM((OPS * REMOTE + 8, LANES), f32), *split_ops, pltpu.VMEM((CELLS, LANES), f32),
         pltpu.VMEM((DEVICES, LANES), f32)],
        40, 8 * 10**9,
        me, far_index.reshape(-1), counts.reshape(-1), far_rows, below, above, by_row[0], own_sum,
        far_in.transpose(1, 0, 2), far_out, by_row[2], stay_atoms, new_atoms, stay_basis, new_basis, pair,
    )
    return local, pot.reshape(SLOTS)


def solution(mesh):
    in_specs = (
        P(None, AXES),
        P(AXES),
        P(AXES),
        P(AXES, None, None),
        P(None, AXES),
        P(None, AXES),
        P(),
        P(),
        P(),
        P(),
        P(),
        P(),
        P(),
    )
    out_specs = (P(None, AXES), P(AXES))
    return jax.shard_map(on_device, mesh=mesh, in_specs=in_specs, out_specs=out_specs, check_vma=False)
```

time: 318 us -> 149 us (0.47)
  local copies, waits for them, and re-layouts: 102 us -> 21.5 us
  Pallas kernels: 0 us -> 80 us
  blocking collectives: 67.6 us -> 0 us
  matrix products: 46.8 us -> 0 us
  other arithmetic: 42.6 us -> 3.69 us
  waiting for transfers between devices: 15.4 us -> 2.14 us
  loops' own time: 9.65 us -> 0 us
  starting transfers between devices: 31.6 us -> 39.2 us
    gather x2 -> x0, local copies, waits for them, and re-layouts: 87.9 us -> none  [the longest x1 57 us: near_apply(): jnp.take(table_rows, entry_dev.reshape(-1), axis=0)]
    pallas_call x0 -> x6, Pallas kernels: none -> 80 us  [call(): pl.pallas_call(kernel, name=name, in_specs=ins, out_specs=[VM] * len(outs...]
    unnamed x1 -> x0, blocking collectives: 67.6 us -> none
    dot_general x15 -> x0, matrix products: 46.8 us -> none  [the longest x1 15.2 us: near_apply(): jnp.einsum('lck,olc->ock', gathered, class_hot, precision=highest)]
    reduce_sum x7 -> x0, other arithmetic: 20.7 us -> none  [the longest x5 20.6 us: one_block(): return jnp.sum(weights, axis=1)]
    unnamed x31 -> x60, local copies, waits for them, and re-layouts: 6.66 us -> 19.9 us
    all_to_all x2, waiting for transfers between devices: 15.4 us -> 2.12 us  [the longest x1 2.12 us: on_device(): lax.all_to_all(need_cells[0, :, 0].reshape(DEVICES, 1, 1), AXES, split_ax...]
    another operation x1 -> x0, loops' own time: 9.65 us -> none  [near_potential(): return lax.map(one_block, starts).reshape(-1)]
  transfers between devices with their start and end apart: 6 -> 8, of which waited for: 1 -> 1; matrix products, arithmetic and copies ran while one was open for 19% -> 3% of each run, Pallas kernels for 0% -> 33%
where the time goes in v1:
time: 149 us; the launch traced here: 147 us
  Pallas kernels  80 us (54%)
  starting transfers between devices  39.2 us (26%)
  local copies, waits for them, and re-layouts  21.5 us (14%)
  other arithmetic  3.69 us (2%)
  waiting for transfers between devices  2.14 us (1%)
    pallas_call x6, Pallas kernels, call(): pl.pallas_call(kernel, name=name, in_specs=ins, out_specs=[VM] * len(outs...  80 us
    unnamed x60, local copies, waits for them, and re-layouts  19.9 us
    ppermute x6, starting transfers between devices, shift(): return lax.ppermute(value, AXES, pairs)  16.9 us
    all_to_all x1, starting transfers between devices, on_device(): lax.all_to_all(need_cells[0, :, 0].reshape(DEVICES, 1, 1), AXES, split_ax...  14 us
    all_to_all x1, starting transfers between devices, on_device(): lax.all_to_all(send.reshape(DEVICES, 1, BLOCK * LANES), AXES, split_axis=...  8.33 us
  transfers between devices with their start and end apart: 8, of which 1 were waited for; matrix products, arithmetic and copies ran while one was open for 3% of the time, Pallas kernels for 33%

profile of v1, /device:TPU:1, one launch (start us, length us, event | category | flops | bytes accessed | tf_op | source)
XLA Modules:
  0.0 147.4 jit_solution(5394445878205295253)
XLA Ops:
  0.6 0.0 copy-start
  0.6 0.7 copy-done
  1.4 0.7 copy-done.2
  2.1 0.7 copy-done.4
  2.8 0.2 pack.1
  3.0 1.3 collective-permute-start
  4.3 3.3 %collective-permute-start.1 = (f32[8,128]{1,0:T(8,128)S(1)}, f32[8,128]{1,0:T(8,128)S(1)}, u32[]{:S(2)}, u32[]{:S(2)}) collective-permute-start(f32[8,128]{1,0:T(8,128)S(1)} %get-tuple-element.25), channel_id=1, source_target_pairs={{1,0},{2,1},{3,2},{4,3},{5,4},{6,5},{7,6},{8,7},{9,8},{10,9},{11,1... | collective-permute-start | bytes 12296 | tf_op jit(solution)/shard_map/ppermute | solution.py:40
  7.6 4.2 %collective-permute-start.2 = (f32[8,128]{1,0:T(8,128)S(1)}, f32[8,128]{1,0:T(8,128)S(1)}, u32[]{:S(2)}, u32[]{:S(2)}) collective-permute-start(f32[8,128]{1,0:T(8,128)S(1)} %get-tuple-element.26), channel_id=1, source_target_pairs={{0,1},{1,2},{2,3},{3,4},{4,5},{5,6},{6,7},{7,8},{8,9},{9,10},{10,1... | collective-permute-start | bytes 12296 | tf_op jit(solution)/shard_map/ppermute | solution.py:40
  11.8 3.2 %collective-permute-start.3 = (f32[8,128]{1,0:T(8,128)S(1)}, f32[8,128]{1,0:T(8,128)S(1)}, u32[]{:S(2)}, u32[]{:S(2)}) collective-permute-start(f32[8,128]{1,0:T(8,128)S(1)} %get-tuple-element.27), channel_id=1, source_target_pairs={{0,2},{1,3},{2,4},{3,5},{4,6},{5,7},{6,8},{7,9},{8,10},{9,11},{10,... | collective-permute-start | bytes 12296 | tf_op jit(solution)/shard_map/ppermute | solution.py:40
  15.0 0.7 slice_bitcast_fusion
  15.7 0.7 copy.23
  16.4 14.0 %all-to-all-start = ((s32[128,1,1]{2,1,0:T(1,128)}), s32[128,1,1]{2,1,0:T(1,128)S(1)}, u32[]{:S(2)}, u32[]{:S(2)}) async-start(s32[128,1,1]{2,1,0:T(1,128)} %copy.23), calls=%async_computation | async-start | bytes 131072 | tf_op jit(solution)/shard_map/all_to_all | solution.py:348
  30.5 0.7 pad_maximum_fusion
  31.2 0.1 copy.24
  31.3 0.0 copy-start.1
  31.4 0.7 copy-done.1
  32.1 0.7 copy-done.3
  32.8 0.7 copy-done.5
  33.5 1.9 %stay.1 = (f32[8,2048]{1,0:T(8,128)S(1)}, f32[128,2048]{1,0:T(8,128)S(1)}, f32[1024,128]{1,0:T(8,128)S(1)}) custom-call(s32[1]{0:T(128)} %bitcast.me_ref, s32[1,2048]{1,0:T(1,128)S(1)} %bitcast.30, f32[4,2048]{1,0:T(4,128)S(1)} %copy-done.1, s32[1,2048]{1,0:T(1,128)S(1)} %bitcast.32, f32[128,8]{1,0:T(8,128)S(1)} %pad.4.waves_ref), custom_call_target="tpu_custom_call" | custom-call | flops 4000000000 | bytes 4194304 | tf_op jit(solution)/shard_map/stay/pallas_call | solution.py:320
  35.5 1.0 copy-done.18
  36.5 0.6 copy-done.22
  37.1 0.1 order.1
  37.2 0.6 copy-done.12
  37.8 2.1 %all-to-all-done = s32[128,1,1]{2,1,0:T(1,128)S(1)} async-done(((s32[128,1,1]{2,1,0:T(1,128)}), s32[128,1,1]{2,1,0:T(1,128)S(1)}, u32[]{:S(2)}, u32[]{:S(2)}) %all-to-all-start) | async-done | bytes 544 | tf_op jit(solution)/shard_map/all_to_all | solution.py:348
  39.9 2.3 %reduce.first_ref = s32[128]{0:T(128)S(1)} reduce(s32[128,1,1]{2,1,0:T(1,128)S(1)} %all-to-all-done, s32[]{:T(128)} %constant.19), dimensions={1,2}, to_apply=%all_to_all.6.reduce_sub_computation | reduce | bytes 1028 | tf_op jit(solution)/shard_map/all_to_all | solution.py:348
  42.3 3.0 %merge.1 = (f32[2432,128]{1,0:T(8,128)}, f32[56,128]{1,0:T(8,128)}, f32[56,128]{1,0:T(8,128)}, f32[1024,128]{1,0:T(8,128)S(1)}, f32[128,512]{1,0:T(8,128)S(1)}, /*index=5*/f32[8,512]{1,0:T(8,128)S(1)}) custom-call(s32[1]{0:T(128)} %bitcast.me_ref, s32[128]{0:T(128)S(1)} %reduce.first_ref, f32[8,128]{1,0:T(8,128)S(1)} %collective-permute-done.m2_ref, ...), custom_call_target="tpu_custom_call" | custom-call | flops 2000000000 | bytes 4194304 | tf_op jit(solution)/shard_map/merge/pallas_call | solution.py:320
  45.3 0.8 copy-done.14
  46.1 0.7 copy-done.16
  46.8 2.9 %collective-permute-start.4 = (f32[56,128]{1,0:T(8,128)}, f32[56,128]{1,0:T(8,128)S(1)}, u32[]{:S(2)}, u32[]{:S(2)}) collective-permute-start(f32[56,128]{1,0:T(8,128)} %get-tuple-element.30), channel_id=1, source_target_pairs={{0,1},{1,2},{2,3},{3,4},{4,5},{5,6},{6,7},{7,8},{8,9},{9,10},{10,1... | collective-permute-start | bytes 86024 | tf_op jit(solution)/shard_map/ppermute | solution.py:40
  49.8 1.9 %collective-permute-start.5 = (f32[56,128]{1,0:T(8,128)}, f32[56,128]{1,0:T(8,128)}, u32[]{:S(2)}, u32[]{:S(2)}) collective-permute-start(f32[56,128]{1,0:T(8,128)} %get-tuple-element.31), channel_id=1, source_target_pairs={{1,0},{2,1},{3,2},{4,3},{5,4},{6,5},{7,6},{8,7},{9,8},{10,9},{11,1... | collective-permute-start | bytes 86024 | tf_op jit(solution)/shard_map/ppermute | solution.py:40
  51.7 8.3 %all-to-all-start.1 = ((f32[128,1,2432]{2,1,0:T(1,128)}), f32[128,1,2432]{2,1,0:T(1,128)S(1)}, u32[]{:S(2)}, u32[]{:S(2)}) async-start(f32[128,1,2432]{2,1,0:T(1,128)} %bitcast.10), calls=%async_computation.1 | async-start | bytes 2490368 | tf_op jit(solution)/shard_map/all_to_all | solution.py:380
  60.0 0.0 copy-start.8
  60.1 1.0 copy-done.8
  61.1 0.8 copy-done.13
  61.9 1.0 copy-done.15
  63.0 0.8 copy-done.23
  63.8 46.4 %mid.1 = (f32[1024,128]{1,0:T(8,128)S(1)}, f32[1,2560]{1,0:T(1,128)S(1)}) custom-call(s32[16384]{0:T(1024)S(1)} %bitcast.39, f32[8,2048]{1,0:T(8,128)S(1)} %copy-done.23, f32[8,512]{1,0:T(8,128)S(1)} %get-tuple-element.34.new_ref, f32[1024,128]{1,0:T(8,128)S(1)} %copy-done.15, f32[968,121]{1,0:T(8,128)S(1)} %bitcast.35), custom_call_target="tpu_custom_call" | custom-call | flops 20000000000 | bytes 4194304 | tf_op jit(solution)/shard_map/mid/pallas_call | solution.py:320
  110.3 0.8 copy-done.20
  111.1 0.6 copy-done.25
  111.6 1.0 copy-done.9
  112.7 1.0 copy-done.10
  113.7 0.9 copy-done.17
  114.7 1.2 copy-done.19
  115.9 1.0 copy-done.21
  116.9 0.8 copy-done.24
  117.8 0.7 copy-done.26
  118.5 28.3 %last.1 = (f32[121,1024]{1,0:T(8,128)}, f32[1,2560]{1,0:T(1,128)S(1)}) custom-call(s32[1]{0:T(128)} %bitcast.me_ref, s32[16384]{0:T(1024)S(1)} %bitcast.38, s32[128]{0:T(128)S(1)} %bitcast.40, f32[2432,128]{1,0:T(8,128)S(1)} %bitcast.26, f32[56,128]{1,0:T(8,128)S(1)} %collective-permute-done.4.below_ref, f32[56,128]{1,0:T(8,128)} %collective-permute-done.5.above_ref, ...), custom_call_target="tpu_custom_call" | custom-call | flops 8000000000 | bytes 4194304 | tf_op jit(solution)/shard_map/last/pallas_call | solution.py:320
  146.8 0.6 reduce.1
  (42 shorter events, 0.1 us)
Async XLA Ops:
  0.6 0.8 copy-start
  1.4 0.7 copy-start.2
  2.1 0.7 copy-start.4
  3.0 39.3 %collective-permute-start = (f32[8,128]{1,0:T(8,128)S(1)}, f32[8,128]{1,0:T(8,128)S(1)}, u32[]{:S(2)}, u32[]{:S(2)}) collective-permute-start(f32[8,128]{1,0:T(8,128)S(1)} %get-tuple-element.24), channel_id=1, source_target_pairs={{2,0},{3,1},{4,2},{5,3},{6,4},{7,5},{8,6},{9,7},{10,8},{11,9},{12,... | collective-permute-start | bytes 12296 | tf_op jit(solution)/shard_map/ppermute | solution.py:40
  4.3 38.0 %collective-permute-start.1 = (f32[8,128]{1,0:T(8,128)S(1)}, f32[8,128]{1,0:T(8,128)S(1)}, u32[]{:S(2)}, u32[]{:S(2)}) collective-permute-start(f32[8,128]{1,0:T(8,128)S(1)} %get-tuple-element.25), channel_id=1, source_target_pairs={{1,0},{2,1},{3,2},{4,3},{5,4},{6,5},{7,6},{8,7},{9,8},{10,9},{11,1... | collective-permute-start | bytes 12296 | tf_op jit(solution)/shard_map/ppermute | solution.py:40
  7.6 34.7 %collective-permute-start.2 = (f32[8,128]{1,0:T(8,128)S(1)}, f32[8,128]{1,0:T(8,128)S(1)}, u32[]{:S(2)}, u32[]{:S(2)}) collective-permute-start(f32[8,128]{1,0:T(8,128)S(1)} %get-tuple-element.26), channel_id=1, source_target_pairs={{0,1},{1,2},{2,3},{3,4},{4,5},{5,6},{6,7},{7,8},{8,9},{9,10},{10,1... | collective-permute-start | bytes 12296 | tf_op jit(solution)/shard_map/ppermute | solution.py:40
  11.8 30.5 %collective-permute-start.3 = (f32[8,128]{1,0:T(8,128)S(1)}, f32[8,128]{1,0:T(8,128)S(1)}, u32[]{:S(2)}, u32[]{:S(2)}) collective-permute-start(f32[8,128]{1,0:T(8,128)S(1)} %get-tuple-element.27), channel_id=1, source_target_pairs={{0,2},{1,3},{2,4},{3,5},{4,6},{5,7},{6,8},{7,9},{8,10},{9,11},{10,... | collective-permute-start | bytes 12296 | tf_op jit(solution)/shard_map/ppermute | solution.py:40
  16.4 23.5 %all-to-all-start = ((s32[128,1,1]{2,1,0:T(1,128)}), s32[128,1,1]{2,1,0:T(1,128)S(1)}, u32[]{:S(2)}, u32[]{:S(2)}) async-start(s32[128,1,1]{2,1,0:T(1,128)} %copy.23), calls=%async_computation | async-start | bytes 131072 | tf_op jit(solution)/shard_map/all_to_all | solution.py:348
  31.3 0.8 copy-start.1
  32.1 0.7 copy-start.3
  32.8 0.7 copy-start.5
  33.5 2.9 %copy-start.27 = (s32[16,1024]{1,0:T(8,128)S(1)}, s32[16,1024]{1,0:T(8,128)}, u32[]{:S(2)}) copy-start(s32[16,1024]{1,0:T(8,128)} %param.17) | copy-start | bytes 196612
  33.5 3.0 %copy-start.28 = (s32[16,1024]{1,0:T(8,128)S(1)}, s32[16,1024]{1,0:T(8,128)}, u32[]{:S(2)}) copy-start(s32[16,1024]{1,0:T(8,128)} %param.18) | copy-start | bytes 196612
  33.5 8.8 %copy-start.7 = (f32[8,121,121]{2,0,1:T(8,128)S(1)}, f32[8,121,121]{2,0,1:T(8,128)}, u32[]{:S(2)}) copy-start(f32[8,121,121]{2,0,1:T(8,128)} %param.22) | copy-start | bytes 1405540
  35.4 1.0 copy-start.18
  36.4 0.6 copy-start.22
  37.2 0.6 copy-start.12
  45.3 0.8 copy-start.14
  46.1 0.7 copy-start.16
  46.8 64.2 %collective-permute-start.4 = (f32[56,128]{1,0:T(8,128)}, f32[56,128]{1,0:T(8,128)S(1)}, u32[]{:S(2)}, u32[]{:S(2)}) collective-permute-start(f32[56,128]{1,0:T(8,128)} %get-tuple-element.30), channel_id=1, source_target_pairs={{0,1},{1,2},{2,3},{3,4},{4,5},{5,6},{6,7},{7,8},{8,9},{9,10},{10,1... | collective-permute-start | bytes 86024 | tf_op jit(solution)/shard_map/ppermute | solution.py:40
  49.8 61.3 %collective-permute-start.5 = (f32[56,128]{1,0:T(8,128)}, f32[56,128]{1,0:T(8,128)}, u32[]{:S(2)}, u32[]{:S(2)}) collective-permute-start(f32[56,128]{1,0:T(8,128)} %get-tuple-element.31), channel_id=1, source_target_pairs={{1,0},{2,1},{3,2},{4,3},{5,4},{6,5},{7,6},{8,7},{9,8},{10,9},{11,1... | collective-permute-start | bytes 86024 | tf_op jit(solution)/shard_map/ppermute | solution.py:40
  51.7 59.3 %all-to-all-start.1 = ((f32[128,1,2432]{2,1,0:T(1,128)}), f32[128,1,2432]{2,1,0:T(1,128)S(1)}, u32[]{:S(2)}, u32[]{:S(2)}) async-start(f32[128,1,2432]{2,1,0:T(1,128)} %bitcast.10), calls=%async_computation.1 | async-start | bytes 2490368 | tf_op jit(solution)/shard_map/all_to_all | solution.py:380
  60.0 1.0 copy-start.8
  61.1 0.8 copy-start.13
  61.9 1.0 copy-start.15
  63.0 0.8 copy-start.23
  63.8 47.8 %copy-start.6 = (f32[31,121,121]{2,0,1:T(8,128)S(1)}, f32[31,121,121]{2,0,1:T(8,128)}, u32[]{:S(2)}) copy-start(f32[31,121,121]{2,0,1:T(8,128)} %param.23) | copy-start | bytes 5446456
  63.8 47.8 %copy-start.11 = (f32[3,121,121]{2,1,0:T(8,128)S(1)}, f32[3,121,121]{2,1,0:T(8,128)}, u32[]{:S(2)}) copy-start(f32[3,121,121]{2,1,0:T(8,128)} %outer_ref.1) | copy-start | bytes 527080
  110.2 0.8 copy-start.20
  111.0 0.6 copy-start.25
  111.6 1.0 copy-start.9
  112.7 1.0 copy-start.10
  113.7 0.9 copy-start.17
  114.7 1.2 copy-start.19
  115.9 1.0 copy-start.21
  116.9 0.8 copy-start.24
  117.8 0.7 copy-start.26

commit v2 on v1

v2 whole, which is shorter than its diff:
```python
import math

import jax
import jax.numpy as jnp
from jax import lax
from jax.experimental import pallas as pl
from jax.experimental.pallas import tpu as pltpu
from jax.sharding import PartitionSpec as P

COEF = 121
LANES = 128
CELLS = 1024
STAY = 2048
CAP = 128
ARRIVE = 4 * CAP
SLOTS = STAY + ARRIVE
LIST = 16
OPS = 8
SLOT = 72
SHORT = 18
BLOCK = SHORT + 1
DEVICES = 128
MEMBERS = 32
GROUPS = 4
PIECE = 6
EXTRA = 56
FAR_ROWS = DEVICES * BLOCK
REMOTE = FAR_ROWS + 2 * EXTRA
WRAP = CELLS + 80
AXES = ("group", "dev")
MIB = 2**20
f32, bf16, i32 = jnp.float32, jnp.bfloat16, jnp.int32
SIN = [(-1) ** n * (2 * math.pi) ** (2 * n + 1) / math.factorial(2 * n + 1) for n in range(6)]

NT = (((1,), (1,)), ((), ()))
NN = (((1,), (0,)), ((), ()))


def shift(value, by):
    pairs = [(i, i + by) for i in range(DEVICES) if 0 <= i + by < DEVICES]
    return lax.ppermute(value, AXES, pairs)


def split(value):
    high = value.astype(bf16)
    return high, (value - high.astype(f32)).astype(bf16)


def basis_of(waves, atoms):
    turns = waves[:, 3:4] + waves[:, 0:1] * atoms[0:1, :]
    turns = turns + waves[:, 1:2] * atoms[1:2, :]
    turns = turns + waves[:, 2:3] * atoms[2:3, :]
    turns = turns - jnp.floor(turns + 0.5)
    base = 0.25 - jnp.abs(turns)
    square = base * base
    total = jnp.full_like(square, SIN[5])
    for factor in SIN[4::-1]:
        total = total * square + factor
    return base * total


def cell_hot(cell_row):
    ids = lax.broadcasted_iota(i32, (CELLS, cell_row.shape[1]), 0) + 1
    return jnp.where(ids == cell_row, 1.0, 0.0).astype(bf16)


def poles(basis, charge, hot):
    high, low = split(basis * charge)
    both = lax.dot_general(hot, jnp.concatenate([high, low], axis=0), NT, preferred_element_type=f32)
    return both[:, :LANES] + both[:, LANES:]


def load(sems, *pairs):
    copies = [pltpu.make_async_copy(src, dst, sems.at[i]) for i, (src, dst) in enumerate(pairs)]
    for copy in copies:
        copy.start()
    return copies


def waves_of(freq_ref, phase_ref, flat):
    flat[...] = jnp.zeros_like(flat)
    flat[0:3, 0:COEF] = freq_ref[...] * (0.5 / math.pi)
    flat[3:4, 0:COEF] = phase_ref[...] * (0.5 / math.pi)
    return flat[...].T


def pack_kernel(me_ref, need_hbm, owner_hbm, rows_hbm, cell_hbm, out_ref, need, owner, rows, cell, buf, sems):
    copies = load(
        sems, (owner_hbm, owner), (rows_hbm, rows), (cell_hbm, cell), (need_hbm.at[0, pl.ds(0, 8), :], need)
    )
    out_ref[...] = jnp.zeros_like(out_ref)
    buf[...] = jnp.zeros_like(buf)
    for copy in copies:
        copy.wait()
    me = me_ref[0]
    gap = owner[...] - me

    def count(by):
        return jnp.sum(jnp.where(gap == by, 1.0, 0.0)).astype(i32)

    for at, lo in ((0, 0), (256, STAY - 256)):
        buf[0:4, at : at + 256] = rows[:, lo : lo + 256]
        buf[4:5, at : at + 256] = (cell[:, lo : lo + 256] + 1).astype(f32)
    lane = lax.broadcasted_iota(i32, (8, CAP), 1)
    low2, low1, up1, up2 = count(-2), count(-1), count(1), count(2)
    first = jnp.broadcast_to(need[0:1, :].astype(f32), (LANES, LANES)).T
    out_ref[pl.ds(5, DEVICES, stride=PIECE), :] = first
    ahead = pltpu.roll(buf[:, :256], lax.rem(256 - low2, 256), 1)
    behind = pltpu.roll(buf[:, 256:], lax.rem(up1 + up2, 256), 1)
    last = pltpu.roll(buf[:, 256:], lax.rem(up2, 256), 1)
    for by, count_by, piece in (
        (-2, low2, buf[:, :CAP]), (-1, low1, ahead[:, :CAP]), (1, up1, behind[:, :CAP]), (2, up2, last[:, :CAP])
    ):
        to = me + by

        @pl.when((to >= 0) & (to < DEVICES))
        def _(to=to, count_by=count_by, piece=piece):
            out_ref[pl.ds(to * PIECE, 5), :] = jnp.where(lane < count_by, piece, 0.0)[0:5, :]


def order(me, entry, kind, own_ref, far_ref, count_ref):
    own_ref[...] = jnp.where(entry < CELLS, kind * CELLS + entry, OPS * CELLS)
    asked = jnp.maximum(entry - CELLS, 0)
    source = jnp.floor((asked.astype(f32) + 0.5) * (1.0 / SLOT)).astype(i32)
    slot = asked - source * SLOT
    side = jnp.where(source < me, FAR_ROWS, FAR_ROWS + EXTRA)
    row = jnp.where(slot < SHORT, source * BLOCK + slot, side + slot - SHORT)
    key = jnp.where(entry < CELLS, -1, kind * REMOTE + row)
    keys = [key[l] for l in range(LIST)]
    used = keys[0] * 0
    for one in keys:
        used = used + jnp.where(one >= 0, 1, 0)
    step = 1
    while step < LIST:
        gap = step
        while gap >= 1:
            for base in range(gap % step, LIST - gap, 2 * gap):
                for i in range(min(gap, LIST - base - gap)):
                    a, b = base + i, base + i + gap
                    if a // (2 * step) == b // (2 * step):
                        keys[a], keys[b] = jnp.maximum(keys[a], keys[b]), jnp.minimum(keys[a], keys[b])
            gap //= 2
        step *= 2
    for l in range(LIST):
        far_ref[l] = jnp.where(keys[l] < 0, OPS * REMOTE, keys[l])
    count_ref[...] = jnp.max(used, axis=0, keepdims=True)


def early_kernel(
    me_ref, owner_hbm, rows_hbm, cell_hbm, freq_hbm, phase_hbm, entry_hbm, class_hbm,
    atoms_hbm, basis_hbm, pole_hbm, own_hbm, far_hbm, count_hbm,
    owner, rows, cell, freq, phase, entry, kind, entry3, kind3, flat, atoms_ref, basis_ref, pole_ref,
    own_ref, far_ref, count_ref, sems, out_sems,
):
    copies = load(
        sems, (owner_hbm, owner), (rows_hbm, rows), (cell_hbm, cell), (freq_hbm, freq), (phase_hbm, phase),
        (entry_hbm, entry), (class_hbm, kind),
    )
    atoms_ref[...] = jnp.zeros_like(atoms_ref)
    for copy in copies[:5]:
        copy.wait()
    stays = owner[...] == me_ref[0]
    atoms_ref[0:4, :] = jnp.where(stays, rows[...], 0.0)
    atoms_ref[4:5, :] = jnp.where(stays, (cell[...] + 1).astype(f32), 0.0)
    waves = waves_of(freq, phase, flat)
    width = 512
    for lo in range(0, STAY, width):
        atoms = atoms_ref[:, lo : lo + width]
        basis = basis_of(waves, atoms)
        basis_ref[:, lo : lo + width] = basis
        part = poles(basis, atoms[3:4, :], cell_hot(atoms[4:5, :].astype(i32)))
        pole_ref[...] = part if lo == 0 else pole_ref[...] + part
    outs = load(out_sems, (atoms_ref, atoms_hbm), (basis_ref, basis_hbm), (pole_ref, pole_hbm))
    for copy in copies[5:]:
        copy.wait()
    for l in range(LIST):
        for r in range(CELLS // LANES):
            entry3[l, r : r + 1, :] = entry[l : l + 1, r * LANES : (r + 1) * LANES]
            kind3[l, r : r + 1, :] = kind[l : l + 1, r * LANES : (r + 1) * LANES]
    order(me_ref[0], entry3[...], kind3[...], own_ref, far_ref, count_ref)
    more = [
        pltpu.make_async_copy(src, dst, out_sems.at[3 + i])
        for i, (src, dst) in enumerate(((own_ref, own_hbm), (far_ref, far_hbm), (count_ref, count_hbm)))
    ]
    for copy in more:
        copy.start()
    for copy in outs + more:
        copy.wait()


def merge_kernel(
    me_ref, got_ref, freq_hbm, phase_hbm, stay_hbm, up_hbm,
    send_ref, low_ref, high_ref, pole_hbm, basis_hbm, atoms_hbm,
    freq, phase, stay, up, flat, atoms_ref, basis_ref, pole_ref, ring, turned, ids, first_ref, sems, out_sems,
):
    copies = load(sems, (freq_hbm, freq), (phase_hbm, phase), (stay_hbm, stay), (up_hbm, up))
    me = me_ref[0]
    row = lax.broadcasted_iota(i32, (DEVICES, LANES), 0)
    lane = lax.broadcasted_iota(i32, (DEVICES, LANES), 1)
    asked = jnp.where(row == lane, got_ref[pl.ds(5, DEVICES, stride=PIECE), :], 0.0)
    ids[...] = jnp.maximum(jnp.sum(asked, axis=0, keepdims=True).astype(i32), 0)
    to_scalars = pltpu.make_async_copy(ids, first_ref, sems.at[4])
    to_scalars.start()
    atoms_ref[...] = jnp.zeros_like(atoms_ref)
    for at, by in enumerate((-2, -1, 1, 2)):
        source = me - by

        @pl.when((source >= 0) & (source < DEVICES))
        def _(at=at, source=source):
            atoms_ref[0:5, at * CAP : (at + 1) * CAP] = got_ref[pl.ds(source * PIECE, 5), :]

    copies[0].wait()
    copies[1].wait()
    atoms = atoms_ref[...]
    basis = basis_of(waves_of(freq, phase, flat), atoms)
    basis_ref[...] = basis
    both = poles(basis, atoms[3:4, :], cell_hot(atoms[4:5, :].astype(i32)))
    copies[2].wait()
    pole = stay[...] + both
    pole_ref[...] = pole
    outs = load(out_sems, (atoms_ref, atoms_hbm), (basis_ref, basis_hbm), (pole_ref, pole_hbm))
    ring[0:CELLS, :] = pole
    ring[CELLS:WRAP, :] = pole[0 : WRAP - CELLS, :]
    grouped = jnp.sum(pole.reshape(CELLS // 8, 8, LANES), axis=0)
    copies[3].wait()
    raised = up[...].reshape(COEF, OPS, COEF) * grouped[None, :, :COEF]
    turned[...] = jnp.zeros_like(turned)
    turned[0:COEF, 0:COEF] = jnp.sum(raised, axis=1)
    coarse = jnp.sum(turned[...].T, axis=0, keepdims=True)
    to_scalars.wait()

    def one(t, _):
        send_ref[pl.ds(t * BLOCK, SHORT), :] = ring[pl.ds(first_ref[0, t], SHORT), :]
        send_ref[pl.ds(t * BLOCK + SHORT, 1), :] = coarse
        return 0

    lax.fori_loop(0, DEVICES, one, 0, unroll=8)
    low_ref[...] = ring[pl.ds(first_ref[0, jnp.maximum(me - 1, 0)] + SHORT, EXTRA), :]
    high_ref[...] = ring[pl.ds(first_ref[0, jnp.minimum(me + 1, DEVICES - 1)] + SHORT, EXTRA), :]
    for copy in outs:
        copy.wait()


def load_ops(ops_ref, both):
    both[...] = jnp.zeros_like(both)
    for o in range(OPS):
        high, low = split(ops_ref[pl.ds(o, COEF, stride=OPS), :])
        for at, part in enumerate((high, high, low)):
            both[o * LANES : o * LANES + COEF, at * LANES : at * LANES + COEF] = part


def premultiply(rows, both, table, at, pitch):
    high, low = split(rows)
    out = lax.dot_general(jnp.concatenate([high, low, high], axis=1), both[...], NT, preferred_element_type=f32)
    for o in range(OPS):
        table[pl.ds(o * pitch + at, rows.shape[0]), :] = out[:, o * LANES : (o + 1) * LANES]


def index_of(index_ref, l, r, g):
    return index_ref.at[pl.ds(l * CELLS + r * LANES, LANES)][g]


def features(atoms_ref, left, right):
    def parts(value, count):
        out = []
        for _ in range(count):
            out.append(value.astype(bf16).astype(f32))
            value = value - out[-1]
        return out

    left[...] = jnp.zeros_like(left)
    right[...] = jnp.zeros_like(right)
    square = None
    for d in range(3):
        value = atoms_ref[d : d + 1, :]
        square = value * value if square is None else square + value * value
        for i, (a, b) in enumerate((a, b) for a in parts(value, 2) for b in parts(value, 2)):
            left[4 * d + i : 4 * d + i + 1, :] = a
            right[4 * d + i : 4 * d + i + 1, :] = -2.0 * b
    ones = jnp.ones_like(square)
    for i, part in enumerate(parts(square, 3)):
        left[12 + i : 13 + i, :] = part
        right[12 + i : 13 + i, :] = ones
    for i, part in enumerate(parts(square + 0.25, 3)):
        left[15 + i : 16 + i, :] = ones
        right[15 + i : 16 + i, :] = part


def pair_sums(atoms_ref, pair_ref, left, right, left_cols, cols, cells, far):
    features(atoms_ref, left, right)
    for lo in range(0, SLOTS, LANES):
        cols[lo : lo + LANES, :] = atoms_ref[:, lo : lo + LANES].T
        left_cols[lo : lo + LANES, :] = left[:, lo : lo + LANES].T
    cells[...] = jnp.broadcast_to(atoms_ref[4:5, :], (8, SLOTS))
    chunk = far.shape[0]

    def block(c, total):
        at = pl.multiple_of(c * chunk, chunk)
        far[...] = lax.dot_general(
            left_cols[pl.ds(at, chunk), :].astype(bf16), right[...].astype(bf16), NN, preferred_element_type=f32
        )

        def tile(i, total):
            down = cols[pl.ds(pl.multiple_of(at + i * 8, 8), 8), :]
            charge = jnp.where(down[:, 4:5] == cells[...], down[:, 3:4], 0.0)
            return total + charge * lax.rsqrt(far[pl.ds(pl.multiple_of(i * 8, 8), 8), :])

        return lax.fori_loop(0, chunk // 8, tile, total)

    total = lax.fori_loop(0, SLOTS // chunk, block, jnp.zeros((8, SLOTS), f32))
    itself = atoms_ref[3:4, :] * lax.rsqrt(jnp.full((1, SLOTS), 0.25, f32))
    pair_ref[...] = jnp.sum(total, axis=0, keepdims=True) - itself


def mid_kernel(
    own_ref, stay_hbm, new_hbm, pole_hbm, ops_hbm, sum_hbm, pair_hbm,
    table, both, ops, pole, atoms_ref, sum_ref, pair_ref, left, right, left_cols, cols, cells, far, sems, out_sems,
):
    copies = load(
        sems, (ops_hbm, ops), (pole_hbm, pole), (stay_hbm, atoms_ref.at[:, pl.ds(0, STAY)]),
        (new_hbm, atoms_ref.at[:, pl.ds(STAY, ARRIVE)]),
    )
    copies[0].wait()
    load_ops(ops, both)
    table[OPS * CELLS :, :] = jnp.zeros((8, LANES), f32)
    copies[1].wait()
    width = CELLS // 2
    for lo in range(0, CELLS, width):
        premultiply(pole[lo : lo + width, :], both, table, lo, CELLS)

    def gather(g, _):
        for r in range(8):
            total = None
            for l in range(LIST):
                row = table[pl.ds(index_of(own_ref, l, r, g), 1), :]
                total = row if total is None else total + row
            sum_ref[pl.ds(r * LANES + g, 1), :] = total
        return 0

    lax.fori_loop(0, LANES, gather, 0)
    sums_out = pltpu.make_async_copy(sum_ref, sum_hbm, out_sems.at[0])
    sums_out.start()
    copies[2].wait()
    copies[3].wait()
    pair_sums(atoms_ref, pair_ref, left, right, left_cols, cols, cells, far)
    pairs_out = pltpu.make_async_copy(pair_ref, pair_hbm, out_sems.at[1])
    pairs_out.start()
    sums_out.wait()
    pairs_out.wait()


def last_kernel(
    me_ref, index_ref, count_ref, far_ref, below_ref, above_ref, ops_hbm, sum_hbm, inner_hbm, outer_hbm, down_hbm,
    stay_hbm, new_hbm, stay_basis_hbm, new_basis_hbm, pair_hbm, local_ref, pot_ref,
    table, both, rows, coarse, ops, inner, outer, down, atoms_ref, basis_ref, pair, sems,
):
    copies = load(
        sems, (ops_hbm, ops), (sum_hbm, rows), (inner_hbm, inner), (outer_hbm, outer), (down_hbm, down),
        (stay_hbm, atoms_ref.at[:, pl.ds(0, STAY)]), (new_hbm, atoms_ref.at[:, pl.ds(STAY, ARRIVE)]),
        (stay_basis_hbm, basis_ref.at[:, pl.ds(0, STAY)]), (new_basis_hbm, basis_ref.at[:, pl.ds(STAY, ARRIVE)]),
        (pair_hbm, pair),
    )
    copies[0].wait()
    load_ops(ops, both)
    width = FAR_ROWS // 4
    for lo in range(0, FAR_ROWS, width):
        premultiply(far_ref[lo : lo + width, :], both, table, lo, REMOTE)
    premultiply(below_ref[...], both, table, FAR_ROWS, REMOTE)
    premultiply(above_ref[...], both, table, FAR_ROWS + EXTRA, REMOTE)
    table[OPS * REMOTE :, :] = jnp.zeros((8, LANES), f32)

    coarse[...] = far_ref[pl.ds(SHORT, DEVICES, stride=BLOCK), :]
    me = me_ref[0]
    group, member = me // MEMBERS, lax.rem(me, MEMBERS)
    who = lax.broadcasted_iota(i32, (40, DEVICES), 1)
    which = lax.broadcasted_iota(i32, (40, DEVICES), 0)
    its_group, its_member = who // MEMBERS, lax.rem(who, MEMBERS)
    near = (its_group == group) & (jnp.abs(its_member - member) - 1 == which) & (which < MEMBERS)
    away = (jnp.abs(its_group - group) - 1 == which - MEMBERS) & (which >= MEMBERS)
    chosen = jnp.where(near | away, 1.0, 0.0)
    sums = lax.dot_general(chosen, coarse[...], NN, precision=lax.Precision.HIGHEST, preferred_element_type=f32)
    for copy in copies[1:5]:
        copy.wait()
    field = jnp.sum(inner[...] * sums[None, 0 : MEMBERS - 1, 0:COEF], axis=1)
    for o in range(GROUPS - 1):
        field = field + outer[o] * sums[MEMBERS + o : MEMBERS + o + 1, 0:COEF]
    field = jnp.broadcast_to(jnp.sum(field, axis=1, keepdims=True), (COEF, LANES))
    child = lax.rem(lax.broadcasted_iota(i32, (COEF, LANES), 1), OPS)
    pattern = jnp.zeros((COEF, LANES), f32)
    for o in range(OPS):
        one = lax.dot_general(
            down[pl.ds(o, COEF, stride=OPS), :], field, NN,
            precision=lax.Precision.HIGHEST, preferred_element_type=f32,
        )
        pattern = jnp.where(child == o, one, pattern)

    def gather(g, _):
        def steps(count):
            totals = []
            for r in range(8):
                total = rows[pl.ds(r * LANES + g, 1), :]
                for l in range(count):
                    total = total + table[pl.ds(index_of(index_ref, l, r, g), 1), :]
                totals.append(total)
            return tuple(totals)

        used = count_ref[g]

        def tree(low, high):
            if low == high:
                return steps(2 * low)
            middle = (low + high) // 2
            return lax.cond(used <= 2 * middle, lambda: tree(low, middle), lambda: tree(middle + 1, high))

        totals = tree(1, LIST // 2)
        for r in range(8):
            rows[pl.ds(r * LANES + g, 1), :] = totals[r]
        return 0

    lax.fori_loop(0, LANES, gather, 0)

    for lo in range(0, CELLS, LANES):
        local_ref[:, lo : lo + LANES] = rows[lo : lo + LANES, :].T[0:COEF, :] + pattern
    local = local_ref[...]
    high, rest = split(local)
    high = jnp.concatenate([high, jnp.zeros((LANES - COEF, CELLS), bf16)], axis=0)
    rest = jnp.concatenate([rest, jnp.zeros((LANES - COEF, CELLS), bf16)], axis=0)
    stacked = jnp.concatenate([high, rest], axis=0)
    for copy in copies[5:]:
        copy.wait()
    wide = 512
    for lo in range(0, SLOTS, wide):
        cells, basis = atoms_ref[4:5, lo : lo + wide], basis_ref[:, lo : lo + wide]
        at = lax.dot_general(stacked, cell_hot(cells.astype(i32)), NN, preferred_element_type=f32)
        read = jnp.sum((at[:LANES] + at[LANES:]) * basis, axis=0, keepdims=True)
        pot_ref[:, lo : lo + wide] = read * COEF**-0.5 + pair[:, lo : lo + wide]


VM = pl.BlockSpec(memory_space=pltpu.VMEM)
SM = pl.BlockSpec(memory_space=pltpu.SMEM)
HB = pl.BlockSpec(memory_space=pltpu.HBM)


def call(kernel, name, ins, outs, scratch, copies, flops, *operands):
    cost = pl.CostEstimate(flops=flops, bytes_accessed=4 * MIB, transcendentals=0)
    return pl.pallas_call(
        kernel,
        name=name,
        in_specs=ins,
        out_specs=[spec for spec, _, _ in outs],
        out_shape=[jax.ShapeDtypeStruct(shape, kind) for _, shape, kind in outs],
        scratch_shapes=[pltpu.VMEM(shape, kind) if isinstance(shape, tuple) else shape for shape, kind in scratch]
        + [pltpu.SemaphoreType.DMA((count,)) for count in copies],
        cost_estimate=cost,
        compiler_params=pltpu.CompilerParams(vmem_limit_bytes=48 * MIB),
    )(*operands)


def on_device(
    atom_rows,
    atom_owner,
    atom_cell,
    need_cells,
    list_entry,
    list_class,
    basis_freq,
    basis_phase,
    near_ops,
    up_ops,
    far_in,
    far_out,
    down_ops,
):
    me = (lax.axis_index("group") * MEMBERS + lax.axis_index("dev")).reshape(1).astype(i32)
    freq, phase = basis_freq.T, basis_phase.reshape(1, COEF)
    waves = [((3, COEF), f32), ((1, COEF), f32)]
    owner_row, cell_row = atom_owner.reshape(1, STAY), atom_cell.reshape(1, STAY)
    by_row = [ops.transpose(1, 0, 2).reshape(COEF * OPS, COEF) for ops in (near_ops, up_ops, down_ops)]
    ops_shape = ((COEF * OPS, COEF), f32)
    mine = [((1, STAY), i32), ((4, STAY), f32), ((1, STAY), i32)]

    (outbound,) = call(
        pack_kernel, "pack", [SM, HB, HB, HB, HB], [(VM, (DEVICES * PIECE, LANES), f32)],
        [((8, LANES), i32), ((STAY // LANES, LANES), i32), *mine[1:], ((8, 512), f32)], [4], 10**6,
        me, need_cells.transpose(0, 2, 1), atom_owner.reshape(STAY // LANES, LANES), atom_rows, cell_row,
    )
    got = lax.all_to_all(outbound.reshape(DEVICES, 1, PIECE * LANES), AXES, split_axis=0, concat_axis=0, tiled=True)
    got = got.reshape(DEVICES * PIECE, LANES)

    shape3 = (LIST, CELLS // LANES, LANES)
    stay_outs = [((8, STAY), f32), ((LANES, STAY), f32), ((CELLS, LANES), f32), (shape3, i32), (shape3, i32), ((1, LANES), i32)]
    stay_atoms, stay_basis, stay_pole, own_index, far_index, counts = call(
        early_kernel, "early", [SM] + [HB] * 7, [(HB, *out) for out in stay_outs],
        [*mine, *waves, *[((LIST, CELLS), i32)] * 2, *[(shape3, i32)] * 2, ((8, LANES), f32), *stay_outs], [7, 6], 4 * 10**9,
        me, owner_row, atom_rows, cell_row, freq, phase, list_entry, list_class,
    )
    merge_outs = [((CELLS, LANES), f32), ((LANES, ARRIVE), f32), ((8, ARRIVE), f32)]
    send, low, high, pole, new_basis, new_atoms = call(
        merge_kernel, "merge", [SM, VM, HB, HB, HB, HB],
        [(VM, (FAR_ROWS, LANES), f32), (VM, (EXTRA, LANES), f32), (VM, (EXTRA, LANES), f32), *[(HB, *out) for out in merge_outs]],
        [*waves, ((CELLS, LANES), f32), ops_shape, ((8, LANES), f32), *merge_outs[::-1],
         ((WRAP, LANES), f32), ((LANES, LANES), f32), ((1, LANES), i32), (pltpu.SMEM((1, LANES), i32), None)],
        [5, 3], 2 * 10**9,
        me, got, freq, phase, stay_pole, by_row[1],
    )
    below, above = shift(high, 1), shift(low, -1)
    far_rows = lax.all_to_all(send.reshape(DEVICES, 1, BLOCK * LANES), AXES, split_axis=0, concat_axis=0, tiled=True)
    far_rows = far_rows.reshape(FAR_ROWS, LANES)
    mid_outs = [((CELLS, LANES), f32), ((1, SLOTS), f32)]
    own_sum, pair = call(
        mid_kernel, "mid", [SM, HB, HB, HB, HB], [(HB, *out) for out in mid_outs],
        [((OPS * CELLS + 8, LANES), f32), ((OPS * LANES, 3 * LANES), bf16), ops_shape, ((CELLS, LANES), f32), ((8, SLOTS), f32),
         *mid_outs, ((32, SLOTS), f32), ((32, SLOTS), f32), ((SLOTS, 32), f32), ((SLOTS, 8), f32), ((8, SLOTS), f32),
         ((256, SLOTS), f32)],
        [4, 2], 20 * 10**9,
        own_index.reshape(-1), stay_atoms, new_atoms, pole, by_row[0],
    )
    local, pot = call(
        last_kernel, "last", [SM, SM, SM, VM, VM, VM] + [HB] * 10, [(VM, (COEF, CELLS), f32), (VM, (1, SLOTS), f32)],
        [((OPS * REMOTE + 8, LANES), f32), ((OPS * LANES, 3 * LANES), bf16), ((CELLS, LANES), f32), ((DEVICES, LANES), f32), ops_shape,
         ((COEF, MEMBERS - 1, COEF), f32), ((GROUPS - 1, COEF, COEF), f32), ops_shape, ((8, SLOTS), f32), ((LANES, SLOTS), f32),
         ((1, SLOTS), f32)],
        [10], 8 * 10**9,
        me, far_index.reshape(-1), counts.reshape(-1), far_rows, below, above, by_row[0], own_sum,
        far_in.transpose(1, 0, 2), far_out, by_row[2], stay_atoms, new_atoms, stay_basis, new_basis, pair,
    )
    return local, pot.reshape(SLOTS)


def solution(mesh):
    in_specs = (
        P(None, AXES),
        P(AXES),
        P(AXES),
        P(AXES, None, None),
        P(None, AXES),
        P(None, AXES),
        P(),
        P(),
        P(),
        P(),
        P(),
        P(),
        P(),
    )
    out_specs = (P(None, AXES), P(AXES))
    return jax.shard_map(on_device, mesh=mesh, in_specs=in_specs, out_specs=out_specs, check_vma=False)
```

time: 149 us -> 115 us (0.77)
  starting transfers between devices: 39.2 us -> 23.9 us
  local copies, waits for them, and re-layouts: 21.5 us -> 9.28 us
  Pallas kernels: 80 us -> 71.8 us
  waiting for transfers between devices: 2.14 us -> 7.72 us
  other arithmetic: 3.69 us -> 0.63 us
    ppermute x6 -> x2, starting transfers between devices: 16.9 us -> 4.88 us  [shift(): return lax.ppermute(value, AXES, pairs)]
    unnamed x60 -> x44, local copies, waits for them, and re-layouts: 19.9 us -> 9.28 us
    pallas_call x6 -> x5, Pallas kernels: 80 us -> 71.8 us  [call(): pl.pallas_call(kernel, name=name, in_specs=ins, out_specs=[spec for spec,...]
    all_to_all x1, waiting for transfers between devices: 2.12 us -> 7.71 us  [on_device(): lax.all_to_all(outbound.reshape(DEVICES, 1, PIECE * LANES), AXES, split_a...]
    all_to_all x1, starting transfers between devices: 14 us -> 11.5 us  [on_device(): lax.all_to_all(outbound.reshape(DEVICES, 1, PIECE * LANES), AXES, split_a...]
    all_to_all x1 -> x0, other arithmetic: 2.35 us -> none  [on_device(): lax.all_to_all(need_cells[0, :, 0].reshape(DEVICES, 1, 1), AXES, split_ax...]
  transfers between devices with their start and end apart: 8 -> 4, of which waited for: 1 -> 1; matrix products, arithmetic and copies ran while one was open for 3% -> 0% of each run, Pallas kernels for 33% -> 44%
where the time goes in v2:
time: 115 us; the launch traced here: 114 us
  Pallas kernels  71.8 us (62%)
  starting transfers between devices  23.9 us (21%)
  local copies, waits for them, and re-layouts  9.28 us (8%)
  waiting for transfers between devices  7.72 us (7%)
    pallas_call x5, Pallas kernels, call(): pl.pallas_call(kernel, name=name, in_specs=ins, out_specs=[spec for spec,...  71.8 us
    all_to_all x1, starting transfers between devices, on_device(): lax.all_to_all(outbound.reshape(DEVICES, 1, PIECE * LANES), AXES, split_a...  11.5 us
    unnamed x44, local copies, waits for them, and re-layouts  9.28 us
    all_to_all x1, waiting for transfers between devices, on_device(): lax.all_to_all(outbound.reshape(DEVICES, 1, PIECE * LANES), AXES, split_a...  7.71 us
    all_to_all x1, starting transfers between devices, on_device(): lax.all_to_all(send.reshape(DEVICES, 1, BLOCK * LANES), AXES, split_axis=...  7.5 us
    ppermute x2, starting transfers between devices, shift(): return lax.ppermute(value, AXES, pairs)  4.88 us
  transfers between devices with their start and end apart: 4, of which 1 were waited for; matrix products, arithmetic and copies ran while one was open for 0% of the time, Pallas kernels for 44%

profile of v2, /device:TPU:1, one launch (start us, length us, event | category | flops | bytes accessed | tf_op | source)
XLA Modules:
  0.0 114.3 jit_solution(7847985977801155835)
XLA Ops:
  0.6 0.0 copy-start.6
  0.6 0.0 copy-start.4
  0.7 0.0 copy-start.13
  0.7 0.0 copy-start.14
  0.7 0.0 copy-start
  0.7 0.8 copy-done
  1.5 0.0 copy-start.1
  1.5 0.8 copy-done.1
  2.2 0.7 copy-done.3
  2.9 0.7 copy-done.5
  3.6 1.1 pack.1
  4.7 11.5 %all-to-all-start = ((f32[128,1,768]{2,1,0:T(1,128)}), f32[128,1,768]{2,1,0:T(1,128)S(1)}, u32[]{:S(2)}, u32[]{:S(2)}) async-start(f32[128,1,768]{2,1,0:T(1,128)} %bitcast.9), calls=%async_computation | async-start | bytes 786432 | tf_op jit(solution)/shard_map/all_to_all | solution.py:487
  16.2 0.0 copy-done.6
  16.2 0.0 copy-done.4
  16.3 0.0 copy-done.13
  16.3 0.0 copy-done.14
  16.3 0.0 copy-done.2
  16.3 0.0 copy-done.11
  16.3 0.0 copy-done.12
  16.3 0.0 copy-start.7
  16.3 2.9 %early.1 = (f32[8,2048]{1,0:T(8,128)S(1)}, f32[128,2048]{1,0:T(8,128)S(1)}, f32[1024,128]{1,0:T(8,128)S(1)}, s32[16,8,128]{2,1,0:T(8,128)S(1)}, s32[16,8,128]{2,1,0:T(8,128)S(1)}, /*index=5*/s32[1,128]{1,0:T(1,128)S(1)}) custom-call(s32[1]{0:T(128)} %bitcast.me_ref, s32[1,2048]{1,0:T(1,128)S(1)} %bitcast.28, f32[4,2048]{1,0:T(4,128)S(1)} %copy-done.2, ...), custom_call_target="tpu_custom_call" | custom-call | flops 4000000000 | bytes 4194304 | tf_op jit(solution)/shard_map/early/pallas_call | solution.py:446
  19.3 0.0 copy-start.15
  19.3 1.0 copy-done.15
  20.2 0.6 copy-done.19
  20.8 7.7 %all-to-all-done = f32[128,1,768]{2,1,0:T(1,128)S(1)} async-done(((f32[128,1,768]{2,1,0:T(1,128)}), f32[128,1,768]{2,1,0:T(1,128)S(1)}, u32[]{:S(2)}, u32[]{:S(2)}) %all-to-all-start) | async-done | bytes 393248 | tf_op jit(solution)/shard_map/all_to_all | solution.py:487
  28.6 0.0 copy-done.7
  28.6 3.2 %merge.1 = (f32[2432,128]{1,0:T(8,128)}, f32[56,128]{1,0:T(8,128)S(1)}, f32[56,128]{1,0:T(8,128)S(1)}, f32[1024,128]{1,0:T(8,128)S(1)}, f32[128,512]{1,0:T(8,128)S(1)}, /*index=5*/f32[8,512]{1,0:T(8,128)S(1)}) custom-call(s32[1]{0:T(128)} %bitcast.me_ref, f32[768,128]{1,0:T(8,128)S(1)} %bitcast.25, f32[3,121]{1,0:T(4,128)S(1)} %bitcast.36, ...), custom_call_target="tpu_custom_call" | custom-call | flops 2000000000 | bytes 4194304 | tf_op jit(solution)/shard_map/merge/pallas_call | solution.py:446
  31.7 3.0 %collective-permute-start = (f32[56,128]{1,0:T(8,128)S(1)}, f32[56,128]{1,0:T(8,128)S(1)}, u32[]{:S(2)}, u32[]{:S(2)}) collective-permute-start(f32[56,128]{1,0:T(8,128)S(1)} %get-tuple-element.22), channel_id=1, source_target_pairs={{0,1},{1,2},{2,3},{3,4},{4,5},{5,6},{6,7},{7,8},{8,9},{9,10},{10,1... | collective-permute-start | bytes 86024 | tf_op jit(solution)/shard_map/ppermute | solution.py:41
  34.7 1.9 %collective-permute-start.1 = (f32[56,128]{1,0:T(8,128)S(1)}, f32[56,128]{1,0:T(8,128)S(1)}, u32[]{:S(2)}, u32[]{:S(2)}) collective-permute-start(f32[56,128]{1,0:T(8,128)S(1)} %get-tuple-element.23), channel_id=1, source_target_pairs={{1,0},{2,1},{3,2},{4,3},{5,4},{6,5},{7,6},{8,7},{9,8},{10,9},{11,1... | collective-permute-start | bytes 86024 | tf_op jit(solution)/shard_map/ppermute | solution.py:41
  36.6 0.0 copy-start.8
  36.6 7.5 %all-to-all-start.1 = ((f32[128,1,2432]{2,1,0:T(1,128)}), f32[128,1,2432]{2,1,0:T(1,128)S(1)}, u32[]{:S(2)}, u32[]{:S(2)}) async-start(f32[128,1,2432]{2,1,0:T(1,128)} %bitcast.13), calls=%async_computation.1 | async-start | bytes 2490368 | tf_op jit(solution)/shard_map/all_to_all | solution.py:507
  44.2 0.0 copy-done.8
  44.2 0.0 copy-start.20
  44.2 0.8 copy-done.20
  45.0 47.1 %mid.1 = (f32[1024,128]{1,0:T(8,128)S(1)}, f32[1,2560]{1,0:T(1,128)S(1)}) custom-call(s32[16384]{0:T(1024)S(1)} %bitcast.40, f32[8,2048]{1,0:T(8,128)S(1)} %copy-done.20, f32[8,512]{1,0:T(8,128)S(1)} %get-tuple-element.26.new_hbm, f32[1024,128]{1,0:T(8,128)S(1)} %get-tuple-element.27.pole_hbm, f32[968,121]{1,0:T(8,128)S(1)} %bitcast.32), custom_call_target="tpu_custom_call" | custom-call | flops 20000000000 | bytes 4194304 | tf_op jit(solution)/shard_map/mid/pallas_call | solution.py:446
  92.1 0.0 copy-start.17
  92.1 0.8 copy-done.17
  92.9 0.0 collective-permute-done.below_ref
  92.9 0.0 collective-permute-done.1.above_ref
  92.9 0.0 all-to-all-done.1
  92.9 0.0 copy-done.9
  92.9 0.0 copy-done.10
  92.9 0.0 copy-start.16
  93.0 1.2 %copy-done.16 = f32[128,2048]{1,0:T(8,128)S(1)} copy-done((f32[128,2048]{1,0:T(8,128)S(1)}, f32[128,2048]{1,0:T(8,128)}, u32[]{:S(2)}) %copy-start.16) | copy-done | bytes 1048600
  94.2 1.0 copy-done.18
  95.2 0.8 copy-done.21
  96.1 17.6 %last.1 = (f32[121,1024]{1,0:T(8,128)}, f32[1,2560]{1,0:T(1,128)S(1)}) custom-call(s32[1]{0:T(128)} %bitcast.me_ref, s32[16384]{0:T(1024)S(1)} %bitcast.39, s32[128]{0:T(128)S(1)} %bitcast.41, f32[2432,128]{1,0:T(8,128)S(1)} %bitcast.24, f32[56,128]{1,0:T(8,128)S(1)} %collective-permute-done.below_ref, f32[56,128]{1,0:T(8,128)S(1)} %collective-permute-done.1.above_ref, ...), custom_call_target="tpu_custom_call" | custom-call | flops 8000000000 | bytes 4194304 | tf_op jit(solution)/shard_map/last/pallas_call | solution.py:446
  113.6 0.6 reduce
  (10 shorter events, 0.0 us)
Async XLA Ops:
  0.6 15.6 %copy-start.6 = (s32[2048]{0:T(1024)S(1)}, s32[2048]{0:T(1024)}, u32[]{:S(2)}) copy-start(s32[2048]{0:T(1024)} %param.15) | copy-start | bytes 24580
  0.6 15.6 %copy-start.4 = (s32[2048]{0:T(1024)S(1)}, s32[2048]{0:T(1024)}, u32[]{:S(2)}) copy-start(s32[2048]{0:T(1024)} %param.14) | copy-start | bytes 24580
  0.7 15.6 %copy-start.13 = (f32[121,3]{0,1:T(4,128)S(1)}, f32[121,3]{0,1:T(4,128)}, u32[]{:S(2)}) copy-start(f32[121,3]{0,1:T(4,128)} %param.19) | copy-start | bytes 4360
  0.7 15.6 %copy-start.14 = (f32[121]{0:T(128)S(1)}, f32[121]{0:T(128)}, u32[]{:S(2)}) copy-start(f32[121]{0:T(128)} %param.20) | copy-start | bytes 1456
  0.7 0.8 copy-start
  1.5 0.8 copy-start.1
  2.2 0.7 copy-start.3
  2.9 0.7 copy-start.5
  3.6 12.7 %copy-start.2 = (f32[4,2048]{1,0:T(4,128)S(1)}, f32[4,2048]{1,0:T(4,128)}, u32[]{:S(2)}) copy-start(f32[4,2048]{1,0:T(4,128)} %rows_hbm.3) | copy-start | bytes 98308
  3.6 12.7 %copy-start.11 = (s32[16,1024]{1,0:T(8,128)S(1)}, s32[16,1024]{1,0:T(8,128)}, u32[]{:S(2)}) copy-start(s32[16,1024]{1,0:T(8,128)} %entry_hbm.1) | copy-start | bytes 196612
  3.6 12.7 %copy-start.12 = (s32[16,1024]{1,0:T(8,128)S(1)}, s32[16,1024]{1,0:T(8,128)}, u32[]{:S(2)}) copy-start(s32[16,1024]{1,0:T(8,128)} %class_hbm.1) | copy-start | bytes 196612
  4.7 23.8 %all-to-all-start = ((f32[128,1,768]{2,1,0:T(1,128)}), f32[128,1,768]{2,1,0:T(1,128)S(1)}, u32[]{:S(2)}, u32[]{:S(2)}) async-start(f32[128,1,768]{2,1,0:T(1,128)} %bitcast.9), calls=%async_computation | async-start | bytes 786432 | tf_op jit(solution)/shard_map/all_to_all | solution.py:487
  16.3 12.3 %copy-start.7 = (f32[8,121,121]{2,0,1:T(8,128)S(1)}, f32[8,121,121]{2,0,1:T(8,128)}, u32[]{:S(2)}) copy-start(f32[8,121,121]{2,0,1:T(8,128)} %param.22) | copy-start | bytes 1405540
  19.3 1.0 copy-start.15
  20.2 0.6 copy-start.19
  31.7 61.2 %collective-permute-start = (f32[56,128]{1,0:T(8,128)S(1)}, f32[56,128]{1,0:T(8,128)S(1)}, u32[]{:S(2)}, u32[]{:S(2)}) collective-permute-start(f32[56,128]{1,0:T(8,128)S(1)} %get-tuple-element.22), channel_id=1, source_target_pairs={{0,1},{1,2},{2,3},{3,4},{4,5},{5,6},{6,7},{7,8},{8,9},{9,10},{10,1... | collective-permute-start | bytes 86024 | tf_op jit(solution)/shard_map/ppermute | solution.py:41
  34.7 58.2 %collective-permute-start.1 = (f32[56,128]{1,0:T(8,128)S(1)}, f32[56,128]{1,0:T(8,128)S(1)}, u32[]{:S(2)}, u32[]{:S(2)}) collective-permute-start(f32[56,128]{1,0:T(8,128)S(1)} %get-tuple-element.23), channel_id=1, source_target_pairs={{1,0},{2,1},{3,2},{4,3},{5,4},{6,5},{7,6},{8,7},{9,8},{10,9},{11,1... | collective-permute-start | bytes 86024 | tf_op jit(solution)/shard_map/ppermute | solution.py:41
  36.6 7.5 %copy-start.8 = (f32[8,121,121]{2,0,1:T(8,128)S(1)}, f32[8,121,121]{2,0,1:T(8,128)}, u32[]{:S(2)}) copy-start(f32[8,121,121]{2,0,1:T(8,128)} %param.21) | copy-start | bytes 1405540
  36.6 56.3 %all-to-all-start.1 = ((f32[128,1,2432]{2,1,0:T(1,128)}), f32[128,1,2432]{2,1,0:T(1,128)S(1)}, u32[]{:S(2)}, u32[]{:S(2)}) async-start(f32[128,1,2432]{2,1,0:T(1,128)} %bitcast.13), calls=%async_computation.1 | async-start | bytes 2490368 | tf_op jit(solution)/shard_map/all_to_all | solution.py:507
  44.2 0.8 copy-start.20
  45.0 47.9 %copy-start.9 = (f32[8,121,121]{2,0,1:T(8,128)S(1)}, f32[8,121,121]{2,0,1:T(8,128)}, u32[]{:S(2)}) copy-start(f32[8,121,121]{2,0,1:T(8,128)} %param.25) | copy-start | bytes 1405540
  45.0 47.9 %copy-start.10 = (f32[3,121,121]{2,1,0:T(8,128)S(1)}, f32[3,121,121]{2,1,0:T(8,128)}, u32[]{:S(2)}) copy-start(f32[3,121,121]{2,1,0:T(8,128)} %outer_hbm.1) | copy-start | bytes 527080
  92.1 0.8 copy-start.17
  92.9 1.2 %copy-start.16 = (f32[128,2048]{1,0:T(8,128)S(1)}, f32[128,2048]{1,0:T(8,128)}, u32[]{:S(2)}) copy-start(f32[128,2048]{1,0:T(8,128)} %copy-done.15) | copy-start | bytes 3145732
  94.2 1.0 copy-start.18
  95.2 0.8 copy-start.21

commit v3 on v2

--- a/solution.py
+++ b/solution.py
@@ -27,6 +27,7 @@
 FAR_ROWS = DEVICES * BLOCK
 REMOTE = FAR_ROWS + 2 * EXTRA
 WRAP = CELLS + 80
+TALL, WIDE = 128, 512
 AXES = ("group", "dev")
 MIB = 2**20
 f32, bf16, i32 = jnp.float32, jnp.bfloat16, jnp.int32
@@ -286,35 +287,56 @@
         right[15 + i : 16 + i, :] = part
 
 
-def pair_sums(atoms_ref, pair_ref, left, right, left_cols, cols, cells, far):
+def pair_sums(atoms_ref, pair_ref, left, right, left_cols, right_low, charges, cells, back):
     features(atoms_ref, left, right)
+    right_low[...] = right[...].astype(bf16)
     for lo in range(0, SLOTS, LANES):
-        cols[lo : lo + LANES, :] = atoms_ref[:, lo : lo + LANES].T
-        left_cols[lo : lo + LANES, :] = left[:, lo : lo + LANES].T
-    cells[...] = jnp.broadcast_to(atoms_ref[4:5, :], (8, SLOTS))
-    chunk = far.shape[0]
-
-    def block(c, total):
-        at = pl.multiple_of(c * chunk, chunk)
-        far[...] = lax.dot_general(
-            left_cols[pl.ds(at, chunk), :].astype(bf16), right[...].astype(bf16), NN, preferred_element_type=f32
+        cut = slice(lo, lo + LANES)
+        left_cols[cut, :] = left[:, cut].T.astype(bf16)
+        charges[cut, :] = jnp.broadcast_to(atoms_ref[3:4, cut], (LANES, LANES)).T
+        cells[cut, :] = jnp.broadcast_to(atoms_ref[4:5, cut], (LANES, LANES)).T
+    back[...] = jnp.zeros_like(back)
+    itself = atoms_ref[3:4, :] * lax.rsqrt(jnp.full((1, SLOTS), 0.25, f32))
+    pair_ref[...] = -itself
+
+    def near_ones(c, j):
+        at, lo = pl.multiple_of(c * TALL, TALL), pl.multiple_of(j * WIDE, WIDE)
+        far = lax.dot_general(
+            left_cols[pl.ds(at, TALL), :], right_low[:, pl.ds(lo, WIDE)], NN, preferred_element_type=f32
         )
-
-        def tile(i, total):
-            down = cols[pl.ds(pl.multiple_of(at + i * 8, 8), 8), :]
-            charge = jnp.where(down[:, 4:5] == cells[...], down[:, 3:4], 0.0)
-            return total + charge * lax.rsqrt(far[pl.ds(pl.multiple_of(i * 8, 8), 8), :])
-
-        return lax.fori_loop(0, chunk // 8, tile, total)
-
-    total = lax.fori_loop(0, SLOTS // chunk, block, jnp.zeros((8, SLOTS), f32))
-    itself = atoms_ref[3:4, :] * lax.rsqrt(jnp.full((1, SLOTS), 0.25, f32))
-    pair_ref[...] = jnp.sum(total, axis=0, keepdims=True) - itself
+        its_cell = jnp.concatenate([cells[pl.ds(at, TALL), :]] * (WIDE // LANES), axis=1)
+        its_charge = jnp.concatenate([charges[pl.ds(at, TALL), :]] * (WIDE // LANES), axis=1)
+        near = jnp.where(its_cell == atoms_ref[4:5, pl.ds(lo, WIDE)], lax.rsqrt(far), 0.0)
+        total = jnp.sum((near * its_charge).reshape(TALL // 8, 8, WIDE), axis=0)
+        pair_ref[:, pl.ds(lo, WIDE)] += jnp.sum(total, axis=0, keepdims=True)
+        return at, lo, near
+
+    def row(c, _):
+        diagonal = c // (WIDE // TALL)
+        near_ones(c, diagonal)
+
+        def block(j, _):
+            at, lo, near = near_ones(c, j)
+            near = near * atoms_ref[3:4, pl.ds(lo, WIDE)]
+            total = near[:, 0:LANES]
+            for k in range(1, WIDE // LANES):
+                total = total + near[:, k * LANES : (k + 1) * LANES]
+            back[pl.ds(at, TALL), :] += total
+            return 0
+
+        lax.fori_loop(diagonal + 1, SLOTS // WIDE, block, 0)
+        return 0
+
+    lax.fori_loop(0, SLOTS // TALL, row, 0)
+    for lo in range(0, SLOTS, LANES):
+        cut = slice(lo, lo + LANES)
+        pair_ref[:, cut] += jnp.sum(back[cut, :].T, axis=0, keepdims=True)
 
 
 def mid_kernel(
     own_ref, stay_hbm, new_hbm, pole_hbm, ops_hbm, sum_hbm, pair_hbm,
-    table, both, ops, pole, atoms_ref, sum_ref, pair_ref, left, right, left_cols, cols, cells, far, sems, out_sems,
+    table, both, ops, pole, atoms_ref, sum_ref, pair_ref, left, right, left_cols, right_low, charges, cells, back,
+    sems, out_sems,
 ):
     copies = load(
         sems, (ops_hbm, ops), (pole_hbm, pole), (stay_hbm, atoms_ref.at[:, pl.ds(0, STAY)]),
@@ -342,7 +364,7 @@
     sums_out.start()
     copies[2].wait()
     copies[3].wait()
-    pair_sums(atoms_ref, pair_ref, left, right, left_cols, cols, cells, far)
+    pair_sums(atoms_ref, pair_ref, left, right, left_cols, right_low, charges, cells, back)
     pairs_out = pltpu.make_async_copy(pair_ref, pair_hbm, out_sems.at[1])
     pairs_out.start()
     sums_out.wait()
@@ -433,7 +455,10 @@
         cells, basis = atoms_ref[4:5, lo : lo + wide], basis_ref[:, lo : lo + wide]
         at = lax.dot_general(stacked, cell_hot(cells.astype(i32)), NN, preferred_element_type=f32)
         read = jnp.sum((at[:LANES] + at[LANES:]) * basis, axis=0, keepdims=True)
-        pot_ref[:, lo : lo + wide] = read * COEF**-0.5 + pair[:, lo : lo + wide]
+        read = read * COEF**-0.5 + pair[:, lo : lo + wide]
+        for at in range(0, wide, LANES):
+            i = (lo + at) // LANES
+            pot_ref[i : i + 1, :] = read[:, at : at + LANES]
 
 
 VM = pl.BlockSpec(memory_space=pltpu.VMEM)
@@ -452,7 +477,7 @@
         scratch_shapes=[pltpu.VMEM(shape, kind) if isinstance(shape, tuple) else shape for shape, kind in scratch]
         + [pltpu.SemaphoreType.DMA((count,)) for count in copies],
         cost_estimate=cost,
-        compiler_params=pltpu.CompilerParams(vmem_limit_bytes=48 * MIB),
+        compiler_params=pltpu.CompilerParams(vmem_limit_bytes=60 * MIB),
     )(*operands)
 
 
@@ -510,13 +535,13 @@
     own_sum, pair = call(
         mid_kernel, "mid", [SM, HB, HB, HB, HB], [(HB, *out) for out in mid_outs],
         [((OPS * CELLS + 8, LANES), f32), ((OPS * LANES, 3 * LANES), bf16), ops_shape, ((CELLS, LANES), f32), ((8, SLOTS), f32),
-         *mid_outs, ((32, SLOTS), f32), ((32, SLOTS), f32), ((SLOTS, 32), f32), ((SLOTS, 8), f32), ((8, SLOTS), f32),
-         ((256, SLOTS), f32)],
+         *mid_outs, ((32, SLOTS), f32), ((32, SLOTS), f32), ((SLOTS, 32), bf16), ((32, SLOTS), bf16),
+         *[((SLOTS, LANES), f32)] * 3],
         [4, 2], 20 * 10**9,
         own_index.reshape(-1), stay_atoms, new_atoms, pole, by_row[0],
     )
     local, pot = call(
-        last_kernel, "last", [SM, SM, SM, VM, VM, VM] + [HB] * 10, [(VM, (COEF, CELLS), f32), (VM, (1, SLOTS), f32)],
+        last_kernel, "last", [SM, SM, SM, VM, VM, VM] + [HB] * 10, [(VM, (COEF, CELLS), f32), (VM, (SLOTS // LANES, LANES), f32)],
         [((OPS * REMOTE + 8, LANES), f32), ((OPS * LANES, 3 * LANES), bf16), ((CELLS, LANES), f32), ((DEVICES, LANES), f32), ops_shape,
          ((COEF, MEMBERS - 1, COEF), f32), ((GROUPS - 1, COEF, COEF), f32), ops_shape, ((8, SLOTS), f32), ((LANES, SLOTS), f32),
          ((1, SLOTS), f32)],

time: 115 us -> 93.1 us (0.81)
  Pallas kernels: 71.8 us -> 57.3 us
  local copies, waits for them, and re-layouts: 9.28 us -> 1.81 us
    pallas_call x5, Pallas kernels: 71.8 us -> 57.3 us  [call(): pl.pallas_call(kernel, name=name, in_specs=ins, out_specs=[spec for spec,...]
    unnamed x44 -> x8, local copies, waits for them, and re-layouts: 9.28 us -> 1.81 us
  transfers between devices with their start and end apart: 4 -> 4, of which waited for: 1 -> 1; matrix products, arithmetic and copies ran while one was open for 0% -> 0% of each run, Pallas kernels for 44% -> 35%
where the time goes in v3:
time: 93.1 us; the launch traced here: 92.5 us
  Pallas kernels  57.3 us (62%)
  starting transfers between devices  23.9 us (26%)
  waiting for transfers between devices  8.59 us (9%)
  local copies, waits for them, and re-layouts  1.81 us (2%)
    pallas_call x5, Pallas kernels, call(): pl.pallas_call(kernel, name=name, in_specs=ins, out_specs=[spec for spec,...  57.3 us
    all_to_all x1, starting transfers between devices, on_device(): lax.all_to_all(outbound.reshape(DEVICES, 1, PIECE * LANES), AXES, split_a...  11.5 us
    all_to_all x1, waiting for transfers between devices, on_device(): lax.all_to_all(outbound.reshape(DEVICES, 1, PIECE * LANES), AXES, split_a...  8.59 us
    all_to_all x1, starting transfers between devices, on_device(): lax.all_to_all(send.reshape(DEVICES, 1, BLOCK * LANES), AXES, split_axis=...  7.5 us
    ppermute x2, starting transfers between devices, shift(): return lax.ppermute(value, AXES, pairs)  4.89 us
  transfers between devices with their start and end apart: 4, of which 1 were waited for; matrix products, arithmetic and copies ran while one was open for 0% of the time, Pallas kernels for 35%

profile of v3, /device:TPU:1, one launch (start us, length us, event | category | flops | bytes accessed | tf_op | source)
XLA Modules:
  0.0 92.5 jit_solution(6477848941769875537)
XLA Ops:
  0.6 1.8 %pack.1 = f32[768,128]{1,0:T(8,128)} custom-call(s32[1]{0:T(128)} %bitcast.me_ref, s32[1,72,128]{2,1,0:T(8,128)} %bitcast.29, s32[16,128]{1,0:T(8,128)} %bitcast.30, f32[4,2048]{1,0:T(4,128)} %rows_hbm.3, s32[1,2048]{1,0:T(1,128)} %bitcast.32), custom_call_target="tpu_custom_call" | custom-call | flops 1000000 | bytes 4194304 | tf_op jit(solution)/shard_map/pack/pallas_call | solution.py:471
  2.4 11.5 %all-to-all-start = ((f32[128,1,768]{2,1,0:T(1,128)}), f32[128,1,768]{2,1,0:T(1,128)S(1)}, u32[]{:S(2)}, u32[]{:S(2)}) async-start(f32[128,1,768]{2,1,0:T(1,128)} %bitcast.25), calls=%async_computation | async-start | bytes 786432 | tf_op jit(solution)/shard_map/all_to_all | solution.py:512
  13.9 3.7 %early.1 = (f32[8,2048]{1,0:T(8,128)}, f32[128,2048]{1,0:T(8,128)}, f32[1024,128]{1,0:T(8,128)}, s32[16,8,128]{2,1,0:T(8,128)}, s32[16,8,128]{2,1,0:T(8,128)}, /*index=5*/s32[1,128]{1,0:T(1,128)}) custom-call(s32[1]{0:T(128)} %bitcast.me_ref, s32[1,2048]{1,0:T(1,128)} %bitcast.31, f32[4,2048]{1,0:T(4,128)} %rows_hbm.3, s32[1,2048]{1,0:T(1,128)} %bitcast.33, ...), custom_call_target="tpu_custom_call" | custom-call | flops 4000000000 | bytes 4194304 | tf_op jit(solution)/shard_map/early/pallas_call | solution.py:471
  17.7 8.6 %all-to-all-done = f32[128,1,768]{2,1,0:T(1,128)S(1)} async-done(((f32[128,1,768]{2,1,0:T(1,128)}), f32[128,1,768]{2,1,0:T(1,128)S(1)}, u32[]{:S(2)}, u32[]{:S(2)}) %all-to-all-start) | async-done | bytes 393248 | tf_op jit(solution)/shard_map/all_to_all | solution.py:512
  26.2 0.0 copy-start.1
  26.2 0.8 copy-done.1
  27.0 4.5 %merge.1 = (f32[2432,128]{1,0:T(8,128)}, f32[56,128]{1,0:T(8,128)}, f32[56,128]{1,0:T(8,128)}, f32[1024,128]{1,0:T(8,128)}, f32[128,512]{1,0:T(8,128)}, /*index=5*/f32[8,512]{1,0:T(8,128)}) custom-call(s32[1]{0:T(128)} %bitcast.me_ref, f32[768,128]{1,0:T(8,128)} %bitcast.28, f32[3,121]{1,0:T(4,128)} %bitcast.40, f32[1,121]{1,0:T(1,128)} %bitcast.42, ...), custom_call_target="tpu_custom_call" | custom-call | flops 2000000000 | bytes 4194304 | tf_op jit(solution)/shard_map/merge/pallas_call | solution.py:471
  31.5 3.0 %collective-permute-start = (f32[56,128]{1,0:T(8,128)}, f32[56,128]{1,0:T(8,128)S(1)}, u32[]{:S(2)}, u32[]{:S(2)}) collective-permute-start(f32[56,128]{1,0:T(8,128)} %get-tuple-element.22), channel_id=1, source_target_pairs={{0,1},{1,2},{2,3},{3,4},{4,5},{5,6},{6,7},{7,8},{8,9},{9,10},{10,1... | collective-permute-start | bytes 86024 | tf_op jit(solution)/shard_map/ppermute | solution.py:42
  34.5 1.9 %collective-permute-start.1 = (f32[56,128]{1,0:T(8,128)}, f32[56,128]{1,0:T(8,128)S(1)}, u32[]{:S(2)}, u32[]{:S(2)}) collective-permute-start(f32[56,128]{1,0:T(8,128)} %get-tuple-element.23), channel_id=1, source_target_pairs={{1,0},{2,1},{3,2},{4,3},{5,4},{6,5},{7,6},{8,7},{9,8},{10,9},{11,1... | collective-permute-start | bytes 86024 | tf_op jit(solution)/shard_map/ppermute | solution.py:42
  36.4 7.5 %all-to-all-start.1 = ((f32[128,1,2432]{2,1,0:T(1,128)}), f32[128,1,2432]{2,1,0:T(1,128)S(1)}, u32[]{:S(2)}, u32[]{:S(2)}) async-start(f32[128,1,2432]{2,1,0:T(1,128)} %bitcast.27), calls=%async_computation.1 | async-start | bytes 2490368 | tf_op jit(solution)/shard_map/all_to_all | solution.py:532
  43.9 28.7 %mid.1 = (f32[1024,128]{1,0:T(8,128)}, f32[1,2560]{1,0:T(1,128)}) custom-call(s32[16384]{0:T(1024)} %bitcast.44, f32[8,2048]{1,0:T(8,128)} %get-tuple-element.25.stay_hbm, f32[8,512]{1,0:T(8,128)} %get-tuple-element.26.new_hbm, f32[1024,128]{1,0:T(8,128)} %get-tuple-element.27.pole_hbm, f32[968,121]{1,0:T(8,128)} %bitcast.36), custom_call_target="tpu_custom_call" | custom-call | flops 20000000000 | bytes 4194304 | tf_op jit(solution)/shard_map/mid/pallas_call | solution.py:471
  72.6 0.0 collective-permute-done.below_ref
  72.7 0.0 copy-start.2
  72.7 0.0 collective-permute-done.1.above_ref
  72.7 0.0 copy-start.3
  72.7 0.0 all-to-all-done.1
  72.7 0.0 copy-start
  72.7 0.6 copy-done.2
  73.3 0.0 copy-done.3
  73.3 0.5 copy-done
  73.8 18.6 %last.1 = (f32[121,1024]{1,0:T(8,128)}, f32[20,128]{1,0:T(8,128)}) custom-call(s32[1]{0:T(128)} %bitcast.me_ref, s32[16384]{0:T(1024)} %bitcast.43, s32[128]{0:T(128)} %bitcast.46, f32[2432,128]{1,0:T(8,128)} %bitcast.26, f32[56,128]{1,0:T(8,128)} %copy-done.2, f32[56,128]{1,0:T(8,128)} %copy-done.3, f32[968,121]{1,0:T(8,128)} %bitcast.37, ...), custom_call_target="tpu_custom_call" | custom-call | flops 8000000000 | bytes 4194304 | tf_op jit(solution)/shard_map/last/pallas_call | solution.py:471
Async XLA Ops:
  2.4 23.8 %all-to-all-start = ((f32[128,1,768]{2,1,0:T(1,128)}), f32[128,1,768]{2,1,0:T(1,128)S(1)}, u32[]{:S(2)}, u32[]{:S(2)}) async-start(f32[128,1,768]{2,1,0:T(1,128)} %bitcast.25), calls=%async_computation | async-start | bytes 786432 | tf_op jit(solution)/shard_map/all_to_all | solution.py:512
  26.2 0.8 copy-start.1
  31.5 41.1 %collective-permute-start = (f32[56,128]{1,0:T(8,128)}, f32[56,128]{1,0:T(8,128)S(1)}, u32[]{:S(2)}, u32[]{:S(2)}) collective-permute-start(f32[56,128]{1,0:T(8,128)} %get-tuple-element.22), channel_id=1, source_target_pairs={{0,1},{1,2},{2,3},{3,4},{4,5},{5,6},{6,7},{7,8},{8,9},{9,10},{10,1... | collective-permute-start | bytes 86024 | tf_op jit(solution)/shard_map/ppermute | solution.py:42
  34.5 38.2 %collective-permute-start.1 = (f32[56,128]{1,0:T(8,128)}, f32[56,128]{1,0:T(8,128)S(1)}, u32[]{:S(2)}, u32[]{:S(2)}) collective-permute-start(f32[56,128]{1,0:T(8,128)} %get-tuple-element.23), channel_id=1, source_target_pairs={{1,0},{2,1},{3,2},{4,3},{5,4},{6,5},{7,6},{8,7},{9,8},{10,9},{11,1... | collective-permute-start | bytes 86024 | tf_op jit(solution)/shard_map/ppermute | solution.py:42
  36.4 36.3 %all-to-all-start.1 = ((f32[128,1,2432]{2,1,0:T(1,128)}), f32[128,1,2432]{2,1,0:T(1,128)S(1)}, u32[]{:S(2)}, u32[]{:S(2)}) async-start(f32[128,1,2432]{2,1,0:T(1,128)} %bitcast.27), calls=%async_computation.1 | async-start | bytes 2490368 | tf_op jit(solution)/shard_map/all_to_all | solution.py:532
  72.7 0.6 copy-start.2
  72.7 0.6 copy-start.3
  72.7 1.1 %copy-start = (f32[128,1,2432]{2,1,0:T(1,128)}, f32[128,1,2432]{2,1,0:T(1,128)S(1)}, u32[]{:S(2)}) copy-start(f32[128,1,2432]{2,1,0:T(1,128)S(1)} %all-to-all-done.1) | copy-start | bytes 3735556

commit v4 on v2

--- a/solution.py
+++ b/solution.py
@@ -27,6 +27,7 @@
 FAR_ROWS = DEVICES * BLOCK
 REMOTE = FAR_ROWS + 2 * EXTRA
 WRAP = CELLS + 80
+TALL, WIDE = 256, 512
 AXES = ("group", "dev")
 MIB = 2**20
 f32, bf16, i32 = jnp.float32, jnp.bfloat16, jnp.int32
@@ -118,18 +119,77 @@
             out_ref[pl.ds(to * PIECE, 5), :] = jnp.where(lane < count_by, piece, 0.0)[0:5, :]
 
 
-def order(me, entry, kind, own_ref, far_ref, count_ref):
-    own_ref[...] = jnp.where(entry < CELLS, kind * CELLS + entry, OPS * CELLS)
-    asked = jnp.maximum(entry - CELLS, 0)
-    source = jnp.floor((asked.astype(f32) + 0.5) * (1.0 / SLOT)).astype(i32)
-    slot = asked - source * SLOT
-    side = jnp.where(source < me, FAR_ROWS, FAR_ROWS + EXTRA)
-    row = jnp.where(slot < SHORT, source * BLOCK + slot, side + slot - SHORT)
-    key = jnp.where(entry < CELLS, -1, kind * REMOTE + row)
-    keys = [key[l] for l in range(LIST)]
-    used = keys[0] * 0
-    for one in keys:
-        used = used + jnp.where(one >= 0, 1, 0)
+def features(atoms_ref, left, right):
+    def parts(value, count):
+        out = []
+        for _ in range(count):
+            out.append(value.astype(bf16).astype(f32))
+            value = value - out[-1]
+        return out
+
+    left[...] = jnp.zeros_like(left)
+    right[...] = jnp.zeros_like(right)
+    square = None
+    for d in range(3):
+        value = atoms_ref[d : d + 1, :]
+        square = value * value if square is None else square + value * value
+        for i, (a, b) in enumerate((a, b) for a in parts(value, 2) for b in parts(value, 2)):
+            left[4 * d + i : 4 * d + i + 1, :] = a
+            right[4 * d + i : 4 * d + i + 1, :] = -2.0 * b
+    ones = jnp.ones_like(square)
+    for i, part in enumerate(parts(square, 3)):
+        left[12 + i : 13 + i, :] = part
+        right[12 + i : 13 + i, :] = ones
+    for i, part in enumerate(parts(square + 0.25, 3)):
+        left[15 + i : 16 + i, :] = ones
+        right[15 + i : 16 + i, :] = part
+
+
+class Pairs:
+    def __init__(self, atoms_ref, pair_ref, left, right, left_cols, right_low, charges, cells, back, start):
+        self.atoms, self.pair, self.left_cols, self.right_low = atoms_ref, pair_ref, left_cols, right_low
+        self.charges, self.cells, self.back, self.start = charges, cells, back, start
+        features(atoms_ref, left, right)
+        right_low[...] = right[...].astype(bf16)
+        for at in range(0, left_cols.shape[0], LANES):
+            cut, rows = slice(start + at, start + at + LANES), slice(at, at + LANES)
+            left_cols[rows, :] = left[:, cut].T.astype(bf16)
+            charges[rows, :] = jnp.broadcast_to(atoms_ref[3:4, cut], (LANES, LANES)).T
+            cells[rows, :] = jnp.broadcast_to(atoms_ref[4:5, cut], (LANES, LANES)).T
+        back[...] = jnp.zeros_like(back)
+
+    def block(self, at, lo, both):
+        far = lax.dot_general(
+            self.left_cols[pl.ds(at, TALL), :], self.right_low[:, pl.ds(lo, WIDE)], NN, preferred_element_type=f32
+        )
+        its_cell = jnp.concatenate([self.cells[pl.ds(at, TALL), :]] * (WIDE // LANES), axis=1)
+        its_charge = jnp.concatenate([self.charges[pl.ds(at, TALL), :]] * (WIDE // LANES), axis=1)
+        near = jnp.where(its_cell == self.atoms[4:5, pl.ds(lo, WIDE)], lax.rsqrt(far), 0.0)
+        total = jnp.sum((near * its_charge).reshape(TALL // 8, 8, WIDE), axis=0)
+        self.pair[:, pl.ds(lo, WIDE)] += jnp.sum(total, axis=0, keepdims=True)
+        if both:
+            near = near * self.atoms[3:4, pl.ds(lo, WIDE)]
+            total = near[:, 0:LANES]
+            for k in range(1, WIDE // LANES):
+                total = total + near[:, k * LANES : (k + 1) * LANES]
+            self.back[pl.ds(at, TALL), :] += total
+
+    def close(self):
+        for at in range(0, self.back.shape[0], LANES):
+            cut = slice(self.start + at, self.start + at + LANES)
+            itself = self.atoms[3:4, cut] * lax.rsqrt(jnp.full((1, LANES), 0.25, f32))
+            self.pair[:, cut] += jnp.sum(self.back[at : at + LANES, :].T, axis=0, keepdims=True) - itself
+
+
+def pair_scratch(slots, rows):
+    return [
+        ((32, slots), f32), ((32, slots), f32), ((rows, 32), bf16), ((32, slots), bf16),
+        *[((rows, LANES), f32)] * 3,
+    ]
+
+
+def sort_rows(keys):
+    keys = list(keys)
     step = 1
     while step < LIST:
         gap = step
@@ -141,17 +201,67 @@
                         keys[a], keys[b] = jnp.maximum(keys[a], keys[b]), jnp.minimum(keys[a], keys[b])
             gap //= 2
         step *= 2
+    return keys
+
+
+def order(me, entry, kind, own_ref, far_ref, cell_ref, count_ref, lists):
+    asked = jnp.maximum(entry - CELLS, 0)
+    source = jnp.floor((asked.astype(f32) + 0.5) * (1.0 / SLOT)).astype(i32)
+    slot = asked - source * SLOT
+    side = jnp.where(source < me, FAR_ROWS, FAR_ROWS + EXTRA)
+    row = jnp.where(slot < SHORT, source * BLOCK + slot, side + slot - SHORT)
+    key = jnp.where(entry < CELLS, -1, kind * REMOTE + row)
+    used = jnp.sum(jnp.where(key >= 0, 1, 0), axis=0)
+    far = sort_rows(key[l] for l in range(LIST))
+    key = jnp.where(entry < CELLS, kind * CELLS + entry, -1)
+    own = sort_rows(key[l] for l in range(LIST))
+    own = [jnp.where(one < 0, OPS * CELLS, one) for one in own]
+    far = [jnp.where(one < 0, OPS * REMOTE, one) for one in far]
+
+    def flat(value):
+        return jnp.concatenate([value[r : r + 1, :] for r in range(CELLS // LANES)], axis=1)
+
+    used_row = flat(used).astype(f32)
+    rank_key = used_row * CELLS + lax.broadcasted_iota(i32, (1, CELLS), 1).astype(f32)
+    rank = jnp.zeros((8, CELLS), f32)
+    for lo in range(0, CELLS, LANES):
+        column = jnp.broadcast_to(rank_key[:, lo : lo + LANES], (LANES, LANES)).T
+        ahead = jnp.where(jnp.concatenate([column] * (CELLS // LANES), axis=1) > rank_key, 1.0, 0.0)
+        rank = rank + jnp.sum(ahead.reshape(LANES // 8, 8, CELLS), axis=0)
+    rank = jnp.sum(rank, axis=0, keepdims=True).astype(i32)
+    place = (rank & 7) * LANES + (rank >> 3)
+    moved = jnp.where(lax.broadcasted_iota(i32, (CELLS, CELLS), 0) == place, 1.0, 0.0).astype(bf16)
+    lists[...] = jnp.zeros_like(lists)
     for l in range(LIST):
-        far_ref[l] = jnp.where(keys[l] < 0, OPS * REMOTE, keys[l])
-    count_ref[...] = jnp.max(used, axis=0, keepdims=True)
+        for at, value in ((l, far[l] >> 8), (16 + l, far[l] & 255), (32 + l, own[l] >> 8), (48 + l, own[l] & 255)):
+            for r in range(CELLS // LANES):
+                lists[at : at + 1, r * LANES : (r + 1) * LANES] = value[r : r + 1, :].astype(f32)
+    ids = lax.broadcasted_iota(i32, (1, CELLS), 1)
+    lists[64:65, :] = (ids >> 8).astype(f32)
+    lists[65:66, :] = (ids & 255).astype(f32)
+    lists[66:67, :] = used_row
+    sorted_lists = lax.dot_general(lists[...].astype(bf16), moved, NT, preferred_element_type=f32).astype(i32)
+    far_rows = sorted_lists[0:16] * 256 + sorted_lists[16:32]
+    own_rows = sorted_lists[32:48] * 256 + sorted_lists[48:64]
+    cells = sorted_lists[64:65] * 256 + sorted_lists[65:66]
+    for r in range(CELLS // LANES):
+        cut = slice(r * LANES, (r + 1) * LANES)
+        for l in range(LIST):
+            far_ref[l, r : r + 1, :] = far_rows[l : l + 1, cut]
+            own_ref[l, r : r + 1, :] = own_rows[l : l + 1, cut]
+        cell_ref[r : r + 1, :] = cells[:, cut]
+    count_ref[...] = jnp.zeros_like(count_ref)
+    count_ref[0:1, :] = sorted_lists[66:67, 0:LANES]
+    count_ref[1:2, :] = LIST - sorted_lists[66:67, CELLS - LANES : CELLS]
 
 
 def early_kernel(
     me_ref, owner_hbm, rows_hbm, cell_hbm, freq_hbm, phase_hbm, entry_hbm, class_hbm,
-    atoms_hbm, basis_hbm, pole_hbm, own_hbm, far_hbm, count_hbm,
-    owner, rows, cell, freq, phase, entry, kind, entry3, kind3, flat, atoms_ref, basis_ref, pole_ref,
-    own_ref, far_ref, count_ref, sems, out_sems,
+    atoms_hbm, basis_hbm, pole_hbm, pair_hbm, own_hbm, far_hbm, place_hbm, count_hbm,
+    owner, rows, cell, freq, phase, entry, kind, entry3, kind3, lists, flat,
+    atoms_ref, basis_ref, pole_ref, pair_ref, own_ref, far_ref, place_ref, count_ref, *rest,
 ):
+    *pair_buffers, sems, out_sems = rest
     copies = load(
         sems, (owner_hbm, owner), (rows_hbm, rows), (cell_hbm, cell), (freq_hbm, freq), (phase_hbm, phase),
         (entry_hbm, entry), (class_hbm, kind),
@@ -177,29 +287,52 @@
         for r in range(CELLS // LANES):
             entry3[l, r : r + 1, :] = entry[l : l + 1, r * LANES : (r + 1) * LANES]
             kind3[l, r : r + 1, :] = kind[l : l + 1, r * LANES : (r + 1) * LANES]
-    order(me_ref[0], entry3[...], kind3[...], own_ref, far_ref, count_ref)
-    more = [
-        pltpu.make_async_copy(src, dst, out_sems.at[3 + i])
-        for i, (src, dst) in enumerate(((own_ref, own_hbm), (far_ref, far_hbm), (count_ref, count_hbm)))
-    ]
-    for copy in more:
-        copy.start()
-    for copy in outs + more:
-        copy.wait()
+    order(me_ref[0], entry3[...], kind3[...], own_ref, far_ref, place_ref, count_ref, lists)
+    more = [(own_ref, own_hbm), (far_ref, far_hbm), (place_ref, place_hbm), (count_ref, count_hbm)]
+    outs += load(out_sems.at[pl.ds(3, 4)], *more)
+
+    pair_ref[...] = jnp.zeros_like(pair_ref)
+    pairs = Pairs(atoms_ref, pair_ref, *pair_buffers, 0)
+    blocks, strips = STAY // WIDE, WIDE // TALL
+
+    def strip(c, reach):
+        at, mine = pl.multiple_of(c * TALL, TALL), c // strips
+        pairs.block(at, pl.multiple_of(mine * WIDE, WIDE), False)
+        for by in range(1, reach + 1):
+            pairs.block(at, pl.multiple_of(lax.rem(mine + by, blocks) * WIDE, WIDE), True)
+
+    def wide_strip(c, _):
+        strip(c, 2)
+        return 0
+
+    def short_strip(c, _):
+        strip(c, 1)
+        return 0
+
+    half = blocks * strips // 2
+    lax.fori_loop(0, half, wide_strip, 0)
+    lax.fori_loop(half, 2 * half, short_strip, 0)
+    pairs.close()
+    last = pltpu.make_async_copy(pair_ref, pair_hbm, out_sems.at[7])
+    last.start()
+    for copy in outs:
+        copy.wait()
+    last.wait()
 
 
 def merge_kernel(
-    me_ref, got_ref, freq_hbm, phase_hbm, stay_hbm, up_hbm,
+    me_ref, got_hbm, freq_hbm, phase_hbm, stay_hbm, up_hbm,
     send_ref, low_ref, high_ref, pole_hbm, basis_hbm, atoms_hbm,
-    freq, phase, stay, up, flat, atoms_ref, basis_ref, pole_ref, ring, turned, ids, first_ref, sems, out_sems,
+    got_ref, freq, phase, stay, up, flat, atoms_ref, basis_ref, pole_ref, ring, turned, ids, first_ref, sems, out_sems,
 ):
-    copies = load(sems, (freq_hbm, freq), (phase_hbm, phase), (stay_hbm, stay), (up_hbm, up))
+    copies = load(sems, (freq_hbm, freq), (phase_hbm, phase), (stay_hbm, stay), (up_hbm, up), (got_hbm, got_ref))
+    copies[4].wait()
     me = me_ref[0]
     row = lax.broadcasted_iota(i32, (DEVICES, LANES), 0)
     lane = lax.broadcasted_iota(i32, (DEVICES, LANES), 1)
     asked = jnp.where(row == lane, got_ref[pl.ds(5, DEVICES, stride=PIECE), :], 0.0)
     ids[...] = jnp.maximum(jnp.sum(asked, axis=0, keepdims=True).astype(i32), 0)
-    to_scalars = pltpu.make_async_copy(ids, first_ref, sems.at[4])
+    to_scalars = pltpu.make_async_copy(ids, first_ref, sems.at[5])
     to_scalars.start()
     atoms_ref[...] = jnp.zeros_like(atoms_ref)
     for at, by in enumerate((-2, -1, 1, 2)):
@@ -251,75 +384,48 @@
 
 def premultiply(rows, both, table, at, pitch):
     high, low = split(rows)
-    out = lax.dot_general(jnp.concatenate([high, low, high], axis=1), both[...], NT, preferred_element_type=f32)
-    for o in range(OPS):
-        table[pl.ds(o * pitch + at, rows.shape[0]), :] = out[:, o * LANES : (o + 1) * LANES]
+    parts = jnp.concatenate([high, low, high], axis=1)
+    for o in range(0, OPS, 2):
+        pair = both[o * LANES : (o + 2) * LANES, :]
+        out = lax.dot_general(parts, pair, NT, preferred_element_type=f32)
+        for k in range(2):
+            table[pl.ds((o + k) * pitch + at, rows.shape[0]), :] = out[:, k * LANES : (k + 1) * LANES]
 
 
 def index_of(index_ref, l, r, g):
     return index_ref.at[pl.ds(l * CELLS + r * LANES, LANES)][g]
 
 
-def features(atoms_ref, left, right):
-    def parts(value, count):
-        out = []
-        for _ in range(count):
-            out.append(value.astype(bf16).astype(f32))
-            value = value - out[-1]
-        return out
-
-    left[...] = jnp.zeros_like(left)
-    right[...] = jnp.zeros_like(right)
-    square = None
-    for d in range(3):
-        value = atoms_ref[d : d + 1, :]
-        square = value * value if square is None else square + value * value
-        for i, (a, b) in enumerate((a, b) for a in parts(value, 2) for b in parts(value, 2)):
-            left[4 * d + i : 4 * d + i + 1, :] = a
-            right[4 * d + i : 4 * d + i + 1, :] = -2.0 * b
-    ones = jnp.ones_like(square)
-    for i, part in enumerate(parts(square, 3)):
-        left[12 + i : 13 + i, :] = part
-        right[12 + i : 13 + i, :] = ones
-    for i, part in enumerate(parts(square + 0.25, 3)):
-        left[15 + i : 16 + i, :] = ones
-        right[15 + i : 16 + i, :] = part
-
-
-def pair_sums(atoms_ref, pair_ref, left, right, left_cols, cols, cells, far):
-    features(atoms_ref, left, right)
-    for lo in range(0, SLOTS, LANES):
-        cols[lo : lo + LANES, :] = atoms_ref[:, lo : lo + LANES].T
-        left_cols[lo : lo + LANES, :] = left[:, lo : lo + LANES].T
-    cells[...] = jnp.broadcast_to(atoms_ref[4:5, :], (8, SLOTS))
-    chunk = far.shape[0]
-
-    def block(c, total):
-        at = pl.multiple_of(c * chunk, chunk)
-        far[...] = lax.dot_general(
-            left_cols[pl.ds(at, chunk), :].astype(bf16), right[...].astype(bf16), NN, preferred_element_type=f32
-        )
-
-        def tile(i, total):
-            down = cols[pl.ds(pl.multiple_of(at + i * 8, 8), 8), :]
-            charge = jnp.where(down[:, 4:5] == cells[...], down[:, 3:4], 0.0)
-            return total + charge * lax.rsqrt(far[pl.ds(pl.multiple_of(i * 8, 8), 8), :])
-
-        return lax.fori_loop(0, chunk // 8, tile, total)
-
-    total = lax.fori_loop(0, SLOTS // chunk, block, jnp.zeros((8, SLOTS), f32))
-    itself = atoms_ref[3:4, :] * lax.rsqrt(jnp.full((1, SLOTS), 0.25, f32))
-    pair_ref[...] = jnp.sum(total, axis=0, keepdims=True) - itself
+def row_sums(index_ref, used, g, table, start):
+    def steps(count):
+        totals = []
+        for r in range(8):
+            total = None if start is None else start(r)
+            for l in range(count):
+                row = table[pl.ds(index_of(index_ref, l, r, g), 1), :]
+                total = row if total is None else total + row
+            totals.append(total)
+        return tuple(totals)
+
+    def tree(low, high):
+        if low == high:
+            return steps(2 * low)
+        middle = (low + high) // 2
+        return lax.cond(used <= 2 * middle, lambda: tree(low, middle), lambda: tree(middle + 1, high))
+
+    return tree(1, LIST // 2)
 
 
 def mid_kernel(
-    own_ref, stay_hbm, new_hbm, pole_hbm, ops_hbm, sum_hbm, pair_hbm,
-    table, both, ops, pole, atoms_ref, sum_ref, pair_ref, left, right, left_cols, cols, cells, far, sems, out_sems,
+    own_ref, count_ref, stay_hbm, new_hbm, pole_hbm, ops_hbm, stay_pair_hbm, sum_hbm, pair_hbm,
+    table, both, ops, pole, atoms_ref, sum_ref, pair_ref, *rest,
 ):
+    *pair_buffers, sems, out_sems = rest
     copies = load(
         sems, (ops_hbm, ops), (pole_hbm, pole), (stay_hbm, atoms_ref.at[:, pl.ds(0, STAY)]),
-        (new_hbm, atoms_ref.at[:, pl.ds(STAY, ARRIVE)]),
-    )
+        (new_hbm, atoms_ref.at[:, pl.ds(STAY, ARRIVE)]), (stay_pair_hbm, pair_ref.at[:, pl.ds(0, STAY)]),
+    )
+    pair_ref[:, STAY:] = jnp.zeros((1, ARRIVE), f32)
     copies[0].wait()
     load_ops(ops, both)
     table[OPS * CELLS :, :] = jnp.zeros((8, LANES), f32)
@@ -329,20 +435,27 @@
         premultiply(pole[lo : lo + width, :], both, table, lo, CELLS)
 
     def gather(g, _):
+        totals = row_sums(own_ref, count_ref.at[pl.ds(LANES, LANES)][g], g, table, None)
         for r in range(8):
-            total = None
-            for l in range(LIST):
-                row = table[pl.ds(index_of(own_ref, l, r, g), 1), :]
-                total = row if total is None else total + row
-            sum_ref[pl.ds(r * LANES + g, 1), :] = total
+            sum_ref[pl.ds(r * LANES + g, 1), :] = totals[r]
         return 0
 
     lax.fori_loop(0, LANES, gather, 0)
     sums_out = pltpu.make_async_copy(sum_ref, sum_hbm, out_sems.at[0])
     sums_out.start()
-    copies[2].wait()
-    copies[3].wait()
-    pair_sums(atoms_ref, pair_ref, left, right, left_cols, cols, cells, far)
+    for copy in copies[2:]:
+        copy.wait()
+    pairs = Pairs(atoms_ref, pair_ref, *pair_buffers, STAY)
+
+    def strip(c, _):
+        at = pl.multiple_of(c * TALL, TALL)
+        pairs.block(at, STAY, False)
+        for lo in range(0, STAY, WIDE):
+            pairs.block(at, lo, True)
+        return 0
+
+    lax.fori_loop(0, ARRIVE // TALL, strip, 0)
+    pairs.close()
     pairs_out = pltpu.make_async_copy(pair_ref, pair_hbm, out_sems.at[1])
     pairs_out.start()
     sums_out.wait()
@@ -350,18 +463,21 @@
 
 
 def last_kernel(
-    me_ref, index_ref, count_ref, far_ref, below_ref, above_ref, ops_hbm, sum_hbm, inner_hbm, outer_hbm, down_hbm,
-    stay_hbm, new_hbm, stay_basis_hbm, new_basis_hbm, pair_hbm, local_ref, pot_ref,
-    table, both, rows, coarse, ops, inner, outer, down, atoms_ref, basis_ref, pair, sems,
+    me_ref, index_ref, count_ref, place_ref, far_hbm, below_hbm, above_hbm, ops_hbm, sum_hbm, inner_hbm, outer_hbm,
+    down_hbm, stay_hbm, new_hbm, stay_basis_hbm, new_basis_hbm, pair_hbm, local_ref, pot_ref,
+    table, both, sums_ref, rows, coarse, ops, inner, outer, down, atoms_ref, basis_ref, pair, far_ref, below_ref, above_ref,
+    sems,
 ):
     copies = load(
-        sems, (ops_hbm, ops), (sum_hbm, rows), (inner_hbm, inner), (outer_hbm, outer), (down_hbm, down),
+        sems, (ops_hbm, ops), (sum_hbm, sums_ref), (inner_hbm, inner), (outer_hbm, outer), (down_hbm, down),
         (stay_hbm, atoms_ref.at[:, pl.ds(0, STAY)]), (new_hbm, atoms_ref.at[:, pl.ds(STAY, ARRIVE)]),
         (stay_basis_hbm, basis_ref.at[:, pl.ds(0, STAY)]), (new_basis_hbm, basis_ref.at[:, pl.ds(STAY, ARRIVE)]),
-        (pair_hbm, pair),
+        (pair_hbm, pair), (far_hbm, far_ref), (below_hbm, below_ref), (above_hbm, above_ref),
     )
     copies[0].wait()
     load_ops(ops, both)
+    for copy in copies[10:]:
+        copy.wait()
     width = FAR_ROWS // 4
     for lo in range(0, FAR_ROWS, width):
         premultiply(far_ref[lo : lo + width, :], both, table, lo, REMOTE)
@@ -395,26 +511,11 @@
         pattern = jnp.where(child == o, one, pattern)
 
     def gather(g, _):
-        def steps(count):
-            totals = []
-            for r in range(8):
-                total = rows[pl.ds(r * LANES + g, 1), :]
-                for l in range(count):
-                    total = total + table[pl.ds(index_of(index_ref, l, r, g), 1), :]
-                totals.append(total)
-            return tuple(totals)
-
-        used = count_ref[g]
-
-        def tree(low, high):
-            if low == high:
-                return steps(2 * low)
-            middle = (low + high) // 2
-            return lax.cond(used <= 2 * middle, lambda: tree(low, middle), lambda: tree(middle + 1, high))
-
-        totals = tree(1, LIST // 2)
+        totals = row_sums(
+            index_ref, count_ref.at[pl.ds(0, LANES)][g], g, table, lambda r: sums_ref[pl.ds(r * LANES + g, 1), :]
+        )
         for r in range(8):
-            rows[pl.ds(r * LANES + g, 1), :] = totals[r]
+            rows[pl.ds(place_ref.at[pl.ds(r * LANES, LANES)][g], 1), :] = totals[r]
         return 0
 
     lax.fori_loop(0, LANES, gather, 0)
@@ -426,14 +527,17 @@
     high = jnp.concatenate([high, jnp.zeros((LANES - COEF, CELLS), bf16)], axis=0)
     rest = jnp.concatenate([rest, jnp.zeros((LANES - COEF, CELLS), bf16)], axis=0)
     stacked = jnp.concatenate([high, rest], axis=0)
-    for copy in copies[5:]:
+    for copy in copies[5:10]:
         copy.wait()
     wide = 512
     for lo in range(0, SLOTS, wide):
         cells, basis = atoms_ref[4:5, lo : lo + wide], basis_ref[:, lo : lo + wide]
         at = lax.dot_general(stacked, cell_hot(cells.astype(i32)), NN, preferred_element_type=f32)
         read = jnp.sum((at[:LANES] + at[LANES:]) * basis, axis=0, keepdims=True)
-        pot_ref[:, lo : lo + wide] = read * COEF**-0.5 + pair[:, lo : lo + wide]
+        read = read * COEF**-0.5 + pair[:, lo : lo + wide]
+        for at in range(0, wide, LANES):
+            i = (lo + at) // LANES
+            pot_ref[i : i + 1, :] = read[:, at : at + LANES]
 
 
 VM = pl.BlockSpec(memory_space=pltpu.VMEM)
@@ -452,7 +556,7 @@
         scratch_shapes=[pltpu.VMEM(shape, kind) if isinstance(shape, tuple) else shape for shape, kind in scratch]
         + [pltpu.SemaphoreType.DMA((count,)) for count in copies],
         cost_estimate=cost,
-        compiler_params=pltpu.CompilerParams(vmem_limit_bytes=48 * MIB),
+        compiler_params=pltpu.CompilerParams(vmem_limit_bytes=60 * MIB),
     )(*operands)
 
 
@@ -487,20 +591,25 @@
     got = lax.all_to_all(outbound.reshape(DEVICES, 1, PIECE * LANES), AXES, split_axis=0, concat_axis=0, tiled=True)
     got = got.reshape(DEVICES * PIECE, LANES)
 
-    shape3 = (LIST, CELLS // LANES, LANES)
-    stay_outs = [((8, STAY), f32), ((LANES, STAY), f32), ((CELLS, LANES), f32), (shape3, i32), (shape3, i32), ((1, LANES), i32)]
-    stay_atoms, stay_basis, stay_pole, own_index, far_index, counts = call(
-        early_kernel, "early", [SM] + [HB] * 7, [(HB, *out) for out in stay_outs],
-        [*mine, *waves, *[((LIST, CELLS), i32)] * 2, *[(shape3, i32)] * 2, ((8, LANES), f32), *stay_outs], [7, 6], 4 * 10**9,
+    shape3, tile = (LIST, CELLS // LANES, LANES), (CELLS // LANES, LANES)
+    early_outs = [
+        ((8, STAY), f32), ((LANES, STAY), f32), ((CELLS, LANES), f32), ((1, STAY), f32),
+        (shape3, i32), (shape3, i32), (tile, i32), (tile, i32),
+    ]
+    stay_atoms, stay_basis, stay_pole, stay_pair, own_index, far_index, place, counts = call(
+        early_kernel, "early", [SM] + [HB] * 7, [(HB, *out) for out in early_outs],
+        [*mine, *waves, *[((LIST, CELLS), i32)] * 2, *[(shape3, i32)] * 2, ((80, CELLS), f32), ((8, LANES), f32), *early_outs,
+         *pair_scratch(STAY, STAY)], [7, 8], 12 * 10**9,
         me, owner_row, atom_rows, cell_row, freq, phase, list_entry, list_class,
     )
+    own_index, far_index, place, counts = (one.reshape(-1) for one in (own_index, far_index, place, counts))
     merge_outs = [((CELLS, LANES), f32), ((LANES, ARRIVE), f32), ((8, ARRIVE), f32)]
     send, low, high, pole, new_basis, new_atoms = call(
-        merge_kernel, "merge", [SM, VM, HB, HB, HB, HB],
+        merge_kernel, "merge", [SM] + [HB] * 5,
         [(VM, (FAR_ROWS, LANES), f32), (VM, (EXTRA, LANES), f32), (VM, (EXTRA, LANES), f32), *[(HB, *out) for out in merge_outs]],
-        [*waves, ((CELLS, LANES), f32), ops_shape, ((8, LANES), f32), *merge_outs[::-1],
+        [((DEVICES * PIECE, LANES), f32), *waves, ((CELLS, LANES), f32), ops_shape, ((8, LANES), f32), *merge_outs[::-1],
          ((WRAP, LANES), f32), ((LANES, LANES), f32), ((1, LANES), i32), (pltpu.SMEM((1, LANES), i32), None)],
-        [5, 3], 2 * 10**9,
+        [6, 3], 2 * 10**9,
         me, got, freq, phase, stay_pole, by_row[1],
     )
     below, above = shift(high, 1), shift(low, -1)
@@ -508,20 +617,19 @@
     far_rows = far_rows.reshape(FAR_ROWS, LANES)
     mid_outs = [((CELLS, LANES), f32), ((1, SLOTS), f32)]
     own_sum, pair = call(
-        mid_kernel, "mid", [SM, HB, HB, HB, HB], [(HB, *out) for out in mid_outs],
+        mid_kernel, "mid", [SM, SM] + [HB] * 5, [(HB, *out) for out in mid_outs],
         [((OPS * CELLS + 8, LANES), f32), ((OPS * LANES, 3 * LANES), bf16), ops_shape, ((CELLS, LANES), f32), ((8, SLOTS), f32),
-         *mid_outs, ((32, SLOTS), f32), ((32, SLOTS), f32), ((SLOTS, 32), f32), ((SLOTS, 8), f32), ((8, SLOTS), f32),
-         ((256, SLOTS), f32)],
-        [4, 2], 20 * 10**9,
-        own_index.reshape(-1), stay_atoms, new_atoms, pole, by_row[0],
+         *mid_outs, *pair_scratch(SLOTS, ARRIVE)],
+        [5, 2], 20 * 10**9,
+        own_index, counts, stay_atoms, new_atoms, pole, by_row[0], stay_pair,
     )
     local, pot = call(
-        last_kernel, "last", [SM, SM, SM, VM, VM, VM] + [HB] * 10, [(VM, (COEF, CELLS), f32), (VM, (1, SLOTS), f32)],
-        [((OPS * REMOTE + 8, LANES), f32), ((OPS * LANES, 3 * LANES), bf16), ((CELLS, LANES), f32), ((DEVICES, LANES), f32), ops_shape,
-         ((COEF, MEMBERS - 1, COEF), f32), ((GROUPS - 1, COEF, COEF), f32), ops_shape, ((8, SLOTS), f32), ((LANES, SLOTS), f32),
-         ((1, SLOTS), f32)],
-        [10], 8 * 10**9,
-        me, far_index.reshape(-1), counts.reshape(-1), far_rows, below, above, by_row[0], own_sum,
+        last_kernel, "last", [SM] * 4 + [HB] * 13, [(VM, (COEF, CELLS), f32), (VM, (SLOTS // LANES, LANES), f32)],
+        [((OPS * REMOTE + 8, LANES), f32), ((OPS * LANES, 3 * LANES), bf16), *[((CELLS, LANES), f32)] * 2, ((DEVICES, LANES), f32),
+         ops_shape, ((COEF, MEMBERS - 1, COEF), f32), ((GROUPS - 1, COEF, COEF), f32), ops_shape, ((8, SLOTS), f32),
+         ((LANES, SLOTS), f32), ((1, SLOTS), f32), ((FAR_ROWS, LANES), f32), *[((EXTRA, LANES), f32)] * 2],
+        [13], 8 * 10**9,
+        me, far_index, counts, place, far_rows, below, above, by_row[0], own_sum,
         far_in.transpose(1, 0, 2), far_out, by_row[2], stay_atoms, new_atoms, stay_basis, new_basis, pair,
     )
     return local, pot.reshape(SLOTS)

time: 115 us -> 86.8 us (0.75)
  Pallas kernels: 71.8 us -> 52.7 us
  local copies, waits for them, and re-layouts: 9.28 us -> 1.82 us
    pallas_call x5, Pallas kernels: 71.8 us -> 52.7 us  [call(): pl.pallas_call(kernel, name=name, in_specs=ins, out_specs=[spec for spec,...]
    unnamed x44 -> x8, local copies, waits for them, and re-layouts: 9.28 us -> 1.82 us
    all_to_all x1, waiting for transfers between devices: 7.71 us -> 2.98 us  [on_device(): lax.all_to_all(outbound.reshape(DEVICES, 1, PIECE * LANES), AXES, split_a...]
    all_to_all x1, waiting for transfers between devices: 0.01 us -> 3.86 us  [on_device(): lax.all_to_all(send.reshape(DEVICES, 1, BLOCK * LANES), AXES, split_axis=...]
  transfers between devices with their start and end apart: 4 -> 4, of which waited for: 1 -> 2; matrix products, arithmetic and copies ran while one was open for 0% -> 0% of each run, Pallas kernels for 44% -> 31%
where the time goes in v4:
time: 86.8 us; the launch traced here: 86.2 us
  Pallas kernels  52.7 us (61%)
  starting transfers between devices  23.9 us (28%)
  waiting for transfers between devices  6.84 us (8%)
  local copies, waits for them, and re-layouts  1.82 us (2%)
  between operations  0.9 us (1%)
    pallas_call x5, Pallas kernels, call(): pl.pallas_call(kernel, name=name, in_specs=ins, out_specs=[spec for spec,...  52.7 us
    all_to_all x1, starting transfers between devices, on_device(): lax.all_to_all(outbound.reshape(DEVICES, 1, PIECE * LANES), AXES, split_a...  11.5 us
    all_to_all x1, starting transfers between devices, on_device(): lax.all_to_all(send.reshape(DEVICES, 1, BLOCK * LANES), AXES, split_axis=...  7.5 us
    ppermute x2, starting transfers between devices, shift(): return lax.ppermute(value, AXES, pairs)  4.88 us
    all_to_all x1, waiting for transfers between devices, on_device(): lax.all_to_all(send.reshape(DEVICES, 1, BLOCK * LANES), AXES, split_axis=...  3.86 us
    all_to_all x1, waiting for transfers between devices, on_device(): lax.all_to_all(outbound.reshape(DEVICES, 1, PIECE * LANES), AXES, split_a...  2.98 us
    unnamed x8, local copies, waits for them, and re-layouts  1.82 us
  transfers between devices with their start and end apart: 4, of which 2 were waited for; matrix products, arithmetic and copies ran while one was open for 0% of the time, Pallas kernels for 31%

profile of v4, /device:TPU:1, one launch (start us, length us, event | category | flops | bytes accessed | tf_op | source)
XLA Modules:
  0.0 86.2 jit_solution(468733915938360282)
XLA Ops:
  0.6 1.8 %pack.1 = f32[768,128]{1,0:T(8,128)} custom-call(s32[1]{0:T(128)} %bitcast.me_ref, s32[1,72,128]{2,1,0:T(8,128)} %bitcast.30, s32[16,128]{1,0:T(8,128)} %bitcast.31, f32[4,2048]{1,0:T(4,128)} %rows_hbm.3, s32[1,2048]{1,0:T(1,128)} %bitcast.33), custom_call_target="tpu_custom_call" | custom-call | flops 1000000 | bytes 4194304 | tf_op jit(solution)/shard_map/pack/pallas_call | solution.py:550
  2.4 11.5 %all-to-all-start = ((f32[128,1,768]{2,1,0:T(1,128)}), f32[128,1,768]{2,1,0:T(1,128)S(1)}, u32[]{:S(2)}, u32[]{:S(2)}) async-start(f32[128,1,768]{2,1,0:T(1,128)} %bitcast.26), calls=%async_computation | async-start | bytes 786432 | tf_op jit(solution)/shard_map/all_to_all | solution.py:591
  13.9 9.3 %early.1 = (f32[8,2048]{1,0:T(8,128)}, f32[128,2048]{1,0:T(8,128)}, f32[1024,128]{1,0:T(8,128)}, f32[1,2048]{1,0:T(1,128)}, s32[16,8,128]{2,1,0:T(8,128)}, /*ind...) custom-call(s32[1]{0:T(128)} %bitcast.me_ref, s32[1,2048]{1,0:T(1,128)} %bitcast.32, f32[4,2048]{1,0:T(4,128)} %rows_hbm.3, ...), custom_call_target="tpu_custom_call" | custom-call | flops 12000000000 | bytes 4194304 | tf_op jit(solution)/shard_map/early/pallas_call | solution.py:550
  23.3 3.0 %all-to-all-done = f32[128,1,768]{2,1,0:T(1,128)S(1)} async-done(((f32[128,1,768]{2,1,0:T(1,128)}), f32[128,1,768]{2,1,0:T(1,128)S(1)}, u32[]{:S(2)}, u32[]{:S(2)}) %all-to-all-start) | async-done | bytes 393248 | tf_op jit(solution)/shard_map/all_to_all | solution.py:591
  26.2 0.0 copy-start.1
  26.2 0.8 copy-done.1
  27.0 4.2 %merge.1 = (f32[2432,128]{1,0:T(8,128)}, f32[56,128]{1,0:T(8,128)}, f32[56,128]{1,0:T(8,128)}, f32[1024,128]{1,0:T(8,128)}, f32[128,512]{1,0:T(8,128)}, /*index=5*/f32[8,512]{1,0:T(8,128)}) custom-call(s32[1]{0:T(128)} %bitcast.me_ref, f32[768,128]{1,0:T(8,128)} %bitcast.29, f32[3,121]{1,0:T(4,128)} %bitcast.41, f32[1,121]{1,0:T(1,128)} %bitcast.43, ...), custom_call_target="tpu_custom_call" | custom-call | flops 2000000000 | bytes 4194304 | tf_op jit(solution)/shard_map/merge/pallas_call | solution.py:550
  31.2 3.0 %collective-permute-start = (f32[56,128]{1,0:T(8,128)}, f32[56,128]{1,0:T(8,128)S(1)}, u32[]{:S(2)}, u32[]{:S(2)}) collective-permute-start(f32[56,128]{1,0:T(8,128)} %get-tuple-element.25), channel_id=1, source_target_pairs={{0,1},{1,2},{2,3},{3,4},{4,5},{5,6},{6,7},{7,8},{8,9},{9,10},{10,1... | collective-permute-start | bytes 86024 | tf_op jit(solution)/shard_map/ppermute | solution.py:42
  34.2 1.9 %collective-permute-start.1 = (f32[56,128]{1,0:T(8,128)}, f32[56,128]{1,0:T(8,128)S(1)}, u32[]{:S(2)}, u32[]{:S(2)}) collective-permute-start(f32[56,128]{1,0:T(8,128)} %get-tuple-element.26), channel_id=1, source_target_pairs={{1,0},{2,1},{3,2},{4,3},{5,4},{6,5},{7,6},{8,7},{9,8},{10,9},{11,1... | collective-permute-start | bytes 86024 | tf_op jit(solution)/shard_map/ppermute | solution.py:42
  36.1 7.5 %all-to-all-start.1 = ((f32[128,1,2432]{2,1,0:T(1,128)}), f32[128,1,2432]{2,1,0:T(1,128)S(1)}, u32[]{:S(2)}, u32[]{:S(2)}) async-start(f32[128,1,2432]{2,1,0:T(1,128)} %bitcast.28), calls=%async_computation.1 | async-start | bytes 2490368 | tf_op jit(solution)/shard_map/all_to_all | solution.py:616
  43.6 17.5 %mid.1 = (f32[1024,128]{1,0:T(8,128)}, f32[1,2560]{1,0:T(1,128)}) custom-call(s32[16384]{0:T(1024)} %bitcast.45, s32[1024]{0:T(1024)} %bitcast.48, f32[8,2048]{1,0:T(8,128)} %get-tuple-element.28.stay_hbm, f32[8,512]{1,0:T(8,128)} %get-tuple-element.29.new_hbm, f32[1024,128]{1,0:T(8,128)} %get-tuple-element.30.pole_hbm, f32[968,121]{1,0:T(8,128)} %bitcast.37, ...), custom_call_target="tpu_custom_call" | custom-call | flops 20000000000 | bytes 4194304 | tf_op jit(solution)/shard_map/mid/pallas_call | solution.py:550
  61.2 0.0 collective-permute-done.below_hbm
  61.2 0.0 copy-start.2
  61.2 0.0 collective-permute-done.1.above_hbm
  61.2 0.0 copy-start.3
  61.2 3.9 %all-to-all-done.1 = f32[128,1,2432]{2,1,0:T(1,128)S(1)} async-done(((f32[128,1,2432]{2,1,0:T(1,128)}), f32[128,1,2432]{2,1,0:T(1,128)S(1)}, u32[]{:S(2)}, u32[]{:S(2)}) %all-to-all-start.1) | async-done | bytes 1245216 | tf_op jit(solution)/shard_map/all_to_all | solution.py:616
  65.1 0.0 copy-start
  65.1 0.0 copy-done.2
  65.1 0.0 copy-done.3
  65.1 1.1 %copy-done = f32[128,1,2432]{2,1,0:T(1,128)} copy-done((f32[128,1,2432]{2,1,0:T(1,128)}, f32[128,1,2432]{2,1,0:T(1,128)S(1)}, u32[]{:S(2)}) %copy-start) | copy-done | bytes 1245208
  66.2 19.9 %last.1 = (f32[121,1024]{1,0:T(8,128)}, f32[20,128]{1,0:T(8,128)}) custom-call(s32[1]{0:T(128)} %bitcast.me_ref, s32[16384]{0:T(1024)} %bitcast.44, s32[1024]{0:T(1024)} %bitcast.49, s32[1024]{0:T(1024)} %bitcast.47, f32[2432,128]{1,0:T(8,128)} %bitcast.27, f32[56,128]{1,0:T(8,128)} %copy-done.2, f32[56,128]{1,0:T(8,128)} %copy-done.3, f32[968,121]{1,0:T(8,128)} %bitcast.38, ...), custom_call_target="tpu_custom_call" | custom-call | flops 8000000000 | bytes 4194304 | tf_op jit(solution)/shard_map/last/pallas_call | solution.py:550
Async XLA Ops:
  2.4 23.8 %all-to-all-start = ((f32[128,1,768]{2,1,0:T(1,128)}), f32[128,1,768]{2,1,0:T(1,128)S(1)}, u32[]{:S(2)}, u32[]{:S(2)}) async-start(f32[128,1,768]{2,1,0:T(1,128)} %bitcast.26), calls=%async_computation | async-start | bytes 786432 | tf_op jit(solution)/shard_map/all_to_all | solution.py:591
  26.2 0.8 copy-start.1
  31.2 30.0 %collective-permute-start = (f32[56,128]{1,0:T(8,128)}, f32[56,128]{1,0:T(8,128)S(1)}, u32[]{:S(2)}, u32[]{:S(2)}) collective-permute-start(f32[56,128]{1,0:T(8,128)} %get-tuple-element.25), channel_id=1, source_target_pairs={{0,1},{1,2},{2,3},{3,4},{4,5},{5,6},{6,7},{7,8},{8,9},{9,10},{10,1... | collective-permute-start | bytes 86024 | tf_op jit(solution)/shard_map/ppermute | solution.py:42
  34.2 27.0 %collective-permute-start.1 = (f32[56,128]{1,0:T(8,128)}, f32[56,128]{1,0:T(8,128)S(1)}, u32[]{:S(2)}, u32[]{:S(2)}) collective-permute-start(f32[56,128]{1,0:T(8,128)} %get-tuple-element.26), channel_id=1, source_target_pairs={{1,0},{2,1},{3,2},{4,3},{5,4},{6,5},{7,6},{8,7},{9,8},{10,9},{11,1... | collective-permute-start | bytes 86024 | tf_op jit(solution)/shard_map/ppermute | solution.py:42
  36.1 29.0 %all-to-all-start.1 = ((f32[128,1,2432]{2,1,0:T(1,128)}), f32[128,1,2432]{2,1,0:T(1,128)S(1)}, u32[]{:S(2)}, u32[]{:S(2)}) async-start(f32[128,1,2432]{2,1,0:T(1,128)} %bitcast.28), calls=%async_computation.1 | async-start | bytes 2490368 | tf_op jit(solution)/shard_map/all_to_all | solution.py:616
  61.2 3.9 %copy-start.2 = (f32[56,128]{1,0:T(8,128)}, f32[56,128]{1,0:T(8,128)S(1)}, u32[]{:S(2)}) copy-start(f32[56,128]{1,0:T(8,128)S(1)} %collective-permute-done.below_hbm) | copy-start | bytes 86020
  61.2 3.9 %copy-start.3 = (f32[56,128]{1,0:T(8,128)}, f32[56,128]{1,0:T(8,128)S(1)}, u32[]{:S(2)}) copy-start(f32[56,128]{1,0:T(8,128)S(1)} %collective-permute-done.1.above_hbm) | copy-start | bytes 86020
  65.1 1.1 %copy-start = (f32[128,1,2432]{2,1,0:T(1,128)}, f32[128,1,2432]{2,1,0:T(1,128)S(1)}, u32[]{:S(2)}) copy-start(f32[128,1,2432]{2,1,0:T(1,128)S(1)} %all-to-all-done.1) | copy-start | bytes 3735556

commit v5 on v4

--- a/solution.py
+++ b/solution.py
@@ -250,9 +250,15 @@
             far_ref[l, r : r + 1, :] = far_rows[l : l + 1, cut]
             own_ref[l, r : r + 1, :] = own_rows[l : l + 1, cut]
         cell_ref[r : r + 1, :] = cells[:, cut]
+    group = lax.broadcasted_iota(i32, (LANES, LANES), 0)
+    number = lax.broadcasted_iota(i32, (LANES, LANES), 1)
+    most = jnp.broadcast_to(sorted_lists[66:67, 0:LANES].astype(f32), (LANES, LANES)).T.astype(i32)
+    least = jnp.broadcast_to(sorted_lists[66:67, CELLS - LANES : CELLS].astype(f32), (LANES, LANES)).T.astype(i32)
     count_ref[...] = jnp.zeros_like(count_ref)
-    count_ref[0:1, :] = sorted_lists[66:67, 0:LANES]
-    count_ref[1:2, :] = LIST - sorted_lists[66:67, CELLS - LANES : CELLS]
+    remote = jnp.where((most >= number) & ((group & 1) == 0), 1.0, 0.0)
+    local = jnp.where((LIST - least <= number) & ((group & 1) == 1), 1.0, 0.0)
+    count_ref[0:1, :] = jnp.sum(remote, axis=0, keepdims=True).astype(i32)
+    count_ref[1:2, :] = jnp.sum(local, axis=0, keepdims=True).astype(i32)
 
 
 def early_kernel(
@@ -321,18 +327,17 @@
 
 
 def merge_kernel(
-    me_ref, got_hbm, freq_hbm, phase_hbm, stay_hbm, up_hbm,
+    me_ref, got_ref, freq_hbm, phase_hbm, stay_hbm, up_hbm,
     send_ref, low_ref, high_ref, pole_hbm, basis_hbm, atoms_hbm,
-    got_ref, freq, phase, stay, up, flat, atoms_ref, basis_ref, pole_ref, ring, turned, ids, first_ref, sems, out_sems,
+    freq, phase, stay, up, flat, atoms_ref, basis_ref, pole_ref, ring, turned, ids, first_ref, sems, out_sems,
 ):
-    copies = load(sems, (freq_hbm, freq), (phase_hbm, phase), (stay_hbm, stay), (up_hbm, up), (got_hbm, got_ref))
-    copies[4].wait()
+    copies = load(sems, (freq_hbm, freq), (phase_hbm, phase), (stay_hbm, stay), (up_hbm, up))
     me = me_ref[0]
     row = lax.broadcasted_iota(i32, (DEVICES, LANES), 0)
     lane = lax.broadcasted_iota(i32, (DEVICES, LANES), 1)
     asked = jnp.where(row == lane, got_ref[pl.ds(5, DEVICES, stride=PIECE), :], 0.0)
     ids[...] = jnp.maximum(jnp.sum(asked, axis=0, keepdims=True).astype(i32), 0)
-    to_scalars = pltpu.make_async_copy(ids, first_ref, sems.at[5])
+    to_scalars = pltpu.make_async_copy(ids, first_ref, sems.at[4])
     to_scalars.start()
     atoms_ref[...] = jnp.zeros_like(atoms_ref)
     for at, by in enumerate((-2, -1, 1, 2)):
@@ -396,55 +401,32 @@
     return index_ref.at[pl.ds(l * CELLS + r * LANES, LANES)][g]
 
 
-def row_sums(index_ref, used, g, table, start):
-    def steps(count):
-        totals = []
-        for r in range(8):
-            total = None if start is None else start(r)
-            for l in range(count):
-                row = table[pl.ds(index_of(index_ref, l, r, g), 1), :]
-                total = row if total is None else total + row
-            totals.append(total)
-        return tuple(totals)
-
-    def tree(low, high):
-        if low == high:
-            return steps(2 * low)
-        middle = (low + high) // 2
-        return lax.cond(used <= 2 * middle, lambda: tree(low, middle), lambda: tree(middle + 1, high))
-
-    return tree(1, LIST // 2)
-
-
-def mid_kernel(
-    own_ref, count_ref, stay_hbm, new_hbm, pole_hbm, ops_hbm, stay_pair_hbm, sum_hbm, pair_hbm,
-    table, both, ops, pole, atoms_ref, sum_ref, pair_ref, *rest,
+def row_sums(index_ref, table, count, first, last, start, store):
+    def pair(p, _):
+        for g in (2 * p, 2 * p + 1):
+            for r in range(8):
+                total = None if start is None else start(r, g)
+                for l in range(count):
+                    row = table[pl.ds(index_of(index_ref, l, r, g), 1), :]
+                    total = row if total is None else total + row
+                store(r, g, jnp.zeros((1, LANES), f32) if total is None else total)
+        return 0
+
+    lax.fori_loop(first, last, pair, 0)
+
+
+def cross_kernel(
+    low_hbm, high_hbm, stay_hbm, new_hbm, stay_pair_hbm, low_out, high_out, pair_hbm, low, high, atoms_ref, pair_ref, *rest
 ):
     *pair_buffers, sems, out_sems = rest
     copies = load(
-        sems, (ops_hbm, ops), (pole_hbm, pole), (stay_hbm, atoms_ref.at[:, pl.ds(0, STAY)]),
-        (new_hbm, atoms_ref.at[:, pl.ds(STAY, ARRIVE)]), (stay_pair_hbm, pair_ref.at[:, pl.ds(0, STAY)]),
+        sems, (stay_hbm, atoms_ref.at[:, pl.ds(0, STAY)]), (new_hbm, atoms_ref.at[:, pl.ds(STAY, ARRIVE)]),
+        (low_hbm, low), (high_hbm, high), (stay_pair_hbm, pair_ref.at[:, pl.ds(0, STAY)]),
     )
     pair_ref[:, STAY:] = jnp.zeros((1, ARRIVE), f32)
-    copies[0].wait()
-    load_ops(ops, both)
-    table[OPS * CELLS :, :] = jnp.zeros((8, LANES), f32)
-    copies[1].wait()
-    width = CELLS // 2
-    for lo in range(0, CELLS, width):
-        premultiply(pole[lo : lo + width, :], both, table, lo, CELLS)
-
-    def gather(g, _):
-        totals = row_sums(own_ref, count_ref.at[pl.ds(LANES, LANES)][g], g, table, None)
-        for r in range(8):
-            sum_ref[pl.ds(r * LANES + g, 1), :] = totals[r]
-        return 0
-
-    lax.fori_loop(0, LANES, gather, 0)
-    sums_out = pltpu.make_async_copy(sum_ref, sum_hbm, out_sems.at[0])
-    sums_out.start()
-    for copy in copies[2:]:
-        copy.wait()
+    for copy in copies:
+        copy.wait()
+    outs = load(out_sems, (low, low_out), (high, high_out))
     pairs = Pairs(atoms_ref, pair_ref, *pair_buffers, STAY)
 
     def strip(c, _):
@@ -456,34 +438,52 @@
 
     lax.fori_loop(0, ARRIVE // TALL, strip, 0)
     pairs.close()
-    pairs_out = pltpu.make_async_copy(pair_ref, pair_hbm, out_sems.at[1])
-    pairs_out.start()
-    sums_out.wait()
-    pairs_out.wait()
+    last = pltpu.make_async_copy(pair_ref, pair_hbm, out_sems.at[2])
+    last.start()
+    for copy in outs + [last]:
+        copy.wait()
+
+
+def mid_kernel(own_ref, count_ref, pole_hbm, ops_hbm, sum_hbm, table, both, ops, pole, sum_ref, sems):
+    copies = load(sems, (ops_hbm, ops), (pole_hbm, pole))
+    table[OPS * CELLS :, :] = jnp.zeros((8, LANES), f32)
+    copies[0].wait()
+    load_ops(ops, both)
+    copies[1].wait()
+    width = CELLS // 2
+    for lo in range(0, CELLS, width):
+        premultiply(pole[lo : lo + width, :], both, table, lo, CELLS)
+
+    def store(r, g, total):
+        sum_ref[pl.ds(r * LANES + g, 1), :] = total
+
+    for n in range(LIST + 1):
+        first = 0 if n == 0 else count_ref[LANES + n - 1]
+        row_sums(own_ref, table, n, first, count_ref[LANES + n], None, store)
+    out = pltpu.make_async_copy(sum_ref, sum_hbm, sems.at[2])
+    out.start()
+    out.wait()
 
 
 def last_kernel(
-    me_ref, index_ref, count_ref, place_ref, far_hbm, below_hbm, above_hbm, ops_hbm, sum_hbm, inner_hbm, outer_hbm,
+    me_ref, index_ref, count_ref, place_ref, far_ref, below_ref, above_ref, ops_hbm, sum_hbm, inner_hbm, outer_hbm,
     down_hbm, stay_hbm, new_hbm, stay_basis_hbm, new_basis_hbm, pair_hbm, local_ref, pot_ref,
-    table, both, sums_ref, rows, coarse, ops, inner, outer, down, atoms_ref, basis_ref, pair, far_ref, below_ref, above_ref,
-    sems,
+    table, both, sums_ref, rows, coarse, ops, inner, outer, down, atoms_ref, basis_ref, pair, sems,
 ):
     copies = load(
         sems, (ops_hbm, ops), (sum_hbm, sums_ref), (inner_hbm, inner), (outer_hbm, outer), (down_hbm, down),
         (stay_hbm, atoms_ref.at[:, pl.ds(0, STAY)]), (new_hbm, atoms_ref.at[:, pl.ds(STAY, ARRIVE)]),
         (stay_basis_hbm, basis_ref.at[:, pl.ds(0, STAY)]), (new_basis_hbm, basis_ref.at[:, pl.ds(STAY, ARRIVE)]),
-        (pair_hbm, pair), (far_hbm, far_ref), (below_hbm, below_ref), (above_hbm, above_ref),
-    )
+        (pair_hbm, pair),
+    )
+    table[OPS * REMOTE :, :] = jnp.zeros((8, LANES), f32)
     copies[0].wait()
     load_ops(ops, both)
-    for copy in copies[10:]:
-        copy.wait()
     width = FAR_ROWS // 4
     for lo in range(0, FAR_ROWS, width):
         premultiply(far_ref[lo : lo + width, :], both, table, lo, REMOTE)
     premultiply(below_ref[...], both, table, FAR_ROWS, REMOTE)
     premultiply(above_ref[...], both, table, FAR_ROWS + EXTRA, REMOTE)
-    table[OPS * REMOTE :, :] = jnp.zeros((8, LANES), f32)
 
     coarse[...] = far_ref[pl.ds(SHORT, DEVICES, stride=BLOCK), :]
     me = me_ref[0]
@@ -510,15 +510,13 @@
         )
         pattern = jnp.where(child == o, one, pattern)
 
-    def gather(g, _):
-        totals = row_sums(
-            index_ref, count_ref.at[pl.ds(0, LANES)][g], g, table, lambda r: sums_ref[pl.ds(r * LANES + g, 1), :]
+    def store(r, g, total):
+        rows[pl.ds(place_ref.at[pl.ds(r * LANES, LANES)][g], 1), :] = total
+
+    for n in range(LIST, -1, -1):
+        row_sums(
+            index_ref, table, n, count_ref[n + 1], count_ref[n], lambda r, g: sums_ref[pl.ds(r * LANES + g, 1), :], store
         )
-        for r in range(8):
-            rows[pl.ds(place_ref.at[pl.ds(r * LANES, LANES)][g], 1), :] = totals[r]
-        return 0
-
-    lax.fori_loop(0, LANES, gather, 0)
 
     for lo in range(0, CELLS, LANES):
         local_ref[:, lo : lo + LANES] = rows[lo : lo + LANES, :].T[0:COEF, :] + pattern
@@ -546,7 +544,7 @@
 
 
 def call(kernel, name, ins, outs, scratch, copies, flops, *operands):
-    cost = pl.CostEstimate(flops=flops, bytes_accessed=4 * MIB, transcendentals=0)
+    cost = pl.CostEstimate(flops=1000, bytes_accessed=1000, transcendentals=0)
     return pl.pallas_call(
         kernel,
         name=name,
@@ -556,7 +554,7 @@
         scratch_shapes=[pltpu.VMEM(shape, kind) if isinstance(shape, tuple) else shape for shape, kind in scratch]
         + [pltpu.SemaphoreType.DMA((count,)) for count in copies],
         cost_estimate=cost,
-        compiler_params=pltpu.CompilerParams(vmem_limit_bytes=60 * MIB),
+        compiler_params=pltpu.CompilerParams(vmem_limit_bytes=56 * MIB),
     )(*operands)
 
 
@@ -605,30 +603,34 @@
     own_index, far_index, place, counts = (one.reshape(-1) for one in (own_index, far_index, place, counts))
     merge_outs = [((CELLS, LANES), f32), ((LANES, ARRIVE), f32), ((8, ARRIVE), f32)]
     send, low, high, pole, new_basis, new_atoms = call(
-        merge_kernel, "merge", [SM] + [HB] * 5,
+        merge_kernel, "merge", [SM, VM] + [HB] * 4,
         [(VM, (FAR_ROWS, LANES), f32), (VM, (EXTRA, LANES), f32), (VM, (EXTRA, LANES), f32), *[(HB, *out) for out in merge_outs]],
-        [((DEVICES * PIECE, LANES), f32), *waves, ((CELLS, LANES), f32), ops_shape, ((8, LANES), f32), *merge_outs[::-1],
+        [*waves, ((CELLS, LANES), f32), ops_shape, ((8, LANES), f32), *merge_outs[::-1],
          ((WRAP, LANES), f32), ((LANES, LANES), f32), ((1, LANES), i32), (pltpu.SMEM((1, LANES), i32), None)],
-        [6, 3], 2 * 10**9,
+        [5, 3], 2 * 10**9,
         me, got, freq, phase, stay_pole, by_row[1],
     )
-    below, above = shift(high, 1), shift(low, -1)
     far_rows = lax.all_to_all(send.reshape(DEVICES, 1, BLOCK * LANES), AXES, split_axis=0, concat_axis=0, tiled=True)
     far_rows = far_rows.reshape(FAR_ROWS, LANES)
-    mid_outs = [((CELLS, LANES), f32), ((1, SLOTS), f32)]
-    own_sum, pair = call(
-        mid_kernel, "mid", [SM, SM] + [HB] * 5, [(HB, *out) for out in mid_outs],
-        [((OPS * CELLS + 8, LANES), f32), ((OPS * LANES, 3 * LANES), bf16), ops_shape, ((CELLS, LANES), f32), ((8, SLOTS), f32),
-         *mid_outs, *pair_scratch(SLOTS, ARRIVE)],
-        [5, 2], 20 * 10**9,
-        own_index, counts, stay_atoms, new_atoms, pole, by_row[0], stay_pair,
+    extra = ((EXTRA, LANES), f32)
+    low, high, pair = call(
+        cross_kernel, "cross", [HB] * 5, [(HB, *extra), (HB, *extra), (HB, (1, SLOTS), f32)],
+        [extra, extra, ((8, SLOTS), f32), ((1, SLOTS), f32), *pair_scratch(SLOTS, ARRIVE)], [5, 3], 4 * 10**9,
+        low, high, stay_atoms, new_atoms, stay_pair,
+    )
+    below, above = shift(high, 1), shift(low, -1)
+    (own_sum,) = call(
+        mid_kernel, "mid", [SM, SM, HB, HB], [(HB, (CELLS, LANES), f32)],
+        [((OPS * CELLS + 8, LANES), f32), ((OPS * LANES, 3 * LANES), bf16), ops_shape, *[((CELLS, LANES), f32)] * 2],
+        [3], 20 * 10**9,
+        own_index, counts, pole, by_row[0],
     )
     local, pot = call(
-        last_kernel, "last", [SM] * 4 + [HB] * 13, [(VM, (COEF, CELLS), f32), (VM, (SLOTS // LANES, LANES), f32)],
+        last_kernel, "last", [SM] * 4 + [VM] * 3 + [HB] * 10, [(VM, (COEF, CELLS), f32), (VM, (SLOTS // LANES, LANES), f32)],
         [((OPS * REMOTE + 8, LANES), f32), ((OPS * LANES, 3 * LANES), bf16), *[((CELLS, LANES), f32)] * 2, ((DEVICES, LANES), f32),
          ops_shape, ((COEF, MEMBERS - 1, COEF), f32), ((GROUPS - 1, COEF, COEF), f32), ops_shape, ((8, SLOTS), f32),
-         ((LANES, SLOTS), f32), ((1, SLOTS), f32), ((FAR_ROWS, LANES), f32), *[((EXTRA, LANES), f32)] * 2],
-        [13], 8 * 10**9,
+         ((LANES, SLOTS), f32), ((1, SLOTS), f32)],
+        [10], 8 * 10**9,
         me, far_index, counts, place, far_rows, below, above, by_row[0], own_sum,
         far_in.transpose(1, 0, 2), far_out, by_row[2], stay_atoms, new_atoms, stay_basis, new_basis, pair,
     )

time: 86.8 us -> 78.5 us (0.904)
  the two profiles are of different devices: /device:TPU:1 before, /device:TPU:8 now
where the time goes in v5:
time: 78.5 us; the launch traced here: 77.9 us
  Pallas kernels  45.1 us (57%)
  starting transfers between devices  28 us (36%)
  waiting for transfers between devices  2.05 us (3%)
  local copies, waits for them, and re-layouts  1.81 us (2%)
  between operations  0.92 us (1%)
    pallas_call x6, Pallas kernels, call(): pl.pallas_call(kernel, name=name, in_specs=ins, out_specs=[spec for spec,...  45.1 us
    all_to_all x1, starting transfers between devices, on_device(): lax.all_to_all(outbound.reshape(DEVICES, 1, PIECE * LANES), AXES, split_a...  10.5 us
    ppermute x2, starting transfers between devices, shift(): return lax.ppermute(value, AXES, pairs)  9.78 us
    all_to_all x1, starting transfers between devices, on_device(): lax.all_to_all(send.reshape(DEVICES, 1, BLOCK * LANES), AXES, split_axis=...  7.74 us
    all_to_all x1, waiting for transfers between devices, on_device(): lax.all_to_all(outbound.reshape(DEVICES, 1, PIECE * LANES), AXES, split_a...  2.04 us
    unnamed x8, local copies, waits for them, and re-layouts  1.81 us
  transfers between devices with their start and end apart: 4, of which 1 were waited for; matrix products, arithmetic and copies ran while one was open for 0% of the time, Pallas kernels for 32%

profile of v5, /device:TPU:8, one launch (start us, length us, event | category | flops | bytes accessed | tf_op | source)
XLA Modules:
  0.0 77.9 jit_solution(16925089314164377753)
XLA Ops:
  0.6 1.8 %pack.1 = f32[768,128]{1,0:T(8,128)} custom-call(s32[1]{0:T(128)} %bitcast.me_ref, s32[1,72,128]{2,1,0:T(8,128)} %bitcast.37, s32[16,128]{1,0:T(8,128)} %bitcast.38, f32[4,2048]{1,0:T(4,128)} %rows_hbm.3, s32[1,2048]{1,0:T(1,128)} %bitcast.40), custom_call_target="tpu_custom_call" | custom-call | flops 1000 | bytes 1000 | tf_op jit(solution)/shard_map/pack/pallas_call | solution.py:548
  2.4 10.5 %all-to-all-start = ((f32[128,1,768]{2,1,0:T(1,128)}), f32[128,1,768]{2,1,0:T(1,128)S(1)}, u32[]{:S(2)}, u32[]{:S(2)}) async-start(f32[128,1,768]{2,1,0:T(1,128)} %bitcast.30), calls=%async_computation | async-start | bytes 786432 | tf_op jit(solution)/shard_map/all_to_all | solution.py:589
  12.9 9.4 %early.1 = (f32[8,2048]{1,0:T(8,128)}, f32[128,2048]{1,0:T(8,128)}, f32[1024,128]{1,0:T(8,128)}, f32[1,2048]{1,0:T(1,128)}, s32[16,8,128]{2,1,0:T(8,128)}, /*ind...) custom-call(s32[1]{0:T(128)} %bitcast.me_ref, s32[1,2048]{1,0:T(1,128)} %bitcast.39, f32[4,2048]{1,0:T(4,128)} %rows_hbm.3, ...), custom_call_target="tpu_custom_call" | custom-call | flops 1000 | bytes 1000 | tf_op jit(solution)/shard_map/early/pallas_call | solution.py:548
  22.3 2.0 %all-to-all-done = f32[128,1,768]{2,1,0:T(1,128)S(1)} async-done(((f32[128,1,768]{2,1,0:T(1,128)}), f32[128,1,768]{2,1,0:T(1,128)S(1)}, u32[]{:S(2)}, u32[]{:S(2)}) %all-to-all-start) | async-done | bytes 393248 | tf_op jit(solution)/shard_map/all_to_all | solution.py:589
  24.3 0.0 copy-start.1
  24.3 0.8 copy-done.1
  25.1 4.5 %merge.1 = (f32[2432,128]{1,0:T(8,128)}, f32[56,128]{1,0:T(8,128)}, f32[56,128]{1,0:T(8,128)}, f32[1024,128]{1,0:T(8,128)}, f32[128,512]{1,0:T(8,128)}, /*index=5*/f32[8,512]{1,0:T(8,128)}) custom-call(s32[1]{0:T(128)} %bitcast.me_ref, f32[768,128]{1,0:T(8,128)} %bitcast.31, f32[3,121]{1,0:T(4,128)} %bitcast.45, f32[1,121]{1,0:T(1,128)} %bitcast.48, ...), custom_call_target="tpu_custom_call" | custom-call | flops 1000 | bytes 1000 | tf_op jit(solution)/shard_map/merge/pallas_call | solution.py:548
  29.6 7.7 %all-to-all-start.1 = ((f32[128,1,2432]{2,1,0:T(1,128)}), f32[128,1,2432]{2,1,0:T(1,128)S(1)}, u32[]{:S(2)}, u32[]{:S(2)}) async-start(f32[128,1,2432]{2,1,0:T(1,128)} %bitcast.32), calls=%async_computation.1 | async-start | bytes 2490368 | tf_op jit(solution)/shard_map/all_to_all | solution.py:613
  37.4 3.7 %cross.1 = (f32[56,128]{1,0:T(8,128)}, f32[56,128]{1,0:T(8,128)}, f32[1,2560]{1,0:T(1,128)}) custom-call(f32[56,128]{1,0:T(8,128)} %get-tuple-element.26.low_hbm, f32[56,128]{1,0:T(8,128)} %get-tuple-element.27.high_hbm, f32[8,2048]{1,0:T(8,128)} %get-tuple-element.28.stay_hbm, f32[8,512]{1,0:T(8,128)} %get-tuple-element.29.new_hbm, ...), custom_call_target="tpu_custom_call" | custom-call | flops 1000 | bytes 1000 | tf_op jit(solution)/shard_map/cross/pallas_call | solution.py:548
  41.1 2.1 %collective-permute-start = (f32[56,128]{1,0:T(8,128)}, f32[56,128]{1,0:T(8,128)S(1)}, u32[]{:S(2)}, u32[]{:S(2)}) collective-permute-start(f32[56,128]{1,0:T(8,128)} %get-tuple-element.31), channel_id=1, source_target_pairs={{0,1},{1,2},{2,3},{3,4},{4,5},{5,6},{6,7},{7,8},{8,9},{9,10},{10,1... | collective-permute-start | bytes 86024 | tf_op jit(solution)/shard_map/ppermute | solution.py:42
  43.1 7.7 %collective-permute-start.1 = (f32[56,128]{1,0:T(8,128)}, f32[56,128]{1,0:T(8,128)S(1)}, u32[]{:S(2)}, u32[]{:S(2)}) collective-permute-start(f32[56,128]{1,0:T(8,128)} %get-tuple-element.32), channel_id=1, source_target_pairs={{1,0},{2,1},{3,2},{4,3},{5,4},{6,5},{7,6},{8,7},{9,8},{10,9},{11,1... | collective-permute-start | bytes 86024 | tf_op jit(solution)/shard_map/ppermute | solution.py:42
  50.9 11.9 %mid.1.sum_hbm = f32[1024,128]{1,0:T(8,128)} custom-call(s32[16384]{0:T(1024)} %bitcast.36, s32[1024]{0:T(1024)} %bitcast.42, f32[1024,128]{1,0:T(8,128)} %get-tuple-element.34.pole_hbm, f32[968,121]{1,0:T(8,128)} %bitcast.28), custom_call_target="tpu_custom_call" | custom-call | flops 1000 | bytes 1000 | tf_op jit(solution)/shard_map/mid/pallas_call | solution.py:548
  62.7 0.0 collective-permute-done.below_ref
  62.7 0.0 copy-start.2
  62.8 0.0 collective-permute-done.1.above_ref
  62.8 0.0 copy-start.3
  62.8 0.0 all-to-all-done.1
  62.8 0.0 copy-start
  62.8 0.6 copy-done.2
  63.4 0.0 copy-done.3
  63.4 0.5 copy-done
  63.9 13.9 %last.1 = (f32[121,1024]{1,0:T(8,128)}, f32[20,128]{1,0:T(8,128)}) custom-call(s32[1]{0:T(128)} %bitcast.me_ref, s32[16384]{0:T(1024)} %bitcast.35, s32[1024]{0:T(1024)} %bitcast.43, s32[1024]{0:T(1024)} %bitcast.46, f32[2432,128]{1,0:T(8,128)} %bitcast.26, f32[56,128]{1,0:T(8,128)} %copy-done.2, f32[56,128]{1,0:T(8,128)} %copy-done.3, f32[968,121]{1,0:T(8,128)} %bitcast.29, ...), custom_call_target="tpu_custom_call" | custom-call | flops 1000 | bytes 1000 | tf_op jit(solution)/shard_map/last/pallas_call | solution.py:548
Async XLA Ops:
  2.4 21.9 %all-to-all-start = ((f32[128,1,768]{2,1,0:T(1,128)}), f32[128,1,768]{2,1,0:T(1,128)S(1)}, u32[]{:S(2)}, u32[]{:S(2)}) async-start(f32[128,1,768]{2,1,0:T(1,128)} %bitcast.30), calls=%async_computation | async-start | bytes 786432 | tf_op jit(solution)/shard_map/all_to_all | solution.py:589
  24.3 0.8 copy-start.1
  29.6 33.1 %all-to-all-start.1 = ((f32[128,1,2432]{2,1,0:T(1,128)}), f32[128,1,2432]{2,1,0:T(1,128)S(1)}, u32[]{:S(2)}, u32[]{:S(2)}) async-start(f32[128,1,2432]{2,1,0:T(1,128)} %bitcast.32), calls=%async_computation.1 | async-start | bytes 2490368 | tf_op jit(solution)/shard_map/all_to_all | solution.py:613
  41.1 21.7 %collective-permute-start = (f32[56,128]{1,0:T(8,128)}, f32[56,128]{1,0:T(8,128)S(1)}, u32[]{:S(2)}, u32[]{:S(2)}) collective-permute-start(f32[56,128]{1,0:T(8,128)} %get-tuple-element.31), channel_id=1, source_target_pairs={{0,1},{1,2},{2,3},{3,4},{4,5},{5,6},{6,7},{7,8},{8,9},{9,10},{10,1... | collective-permute-start | bytes 86024 | tf_op jit(solution)/shard_map/ppermute | solution.py:42
  43.1 19.6 %collective-permute-start.1 = (f32[56,128]{1,0:T(8,128)}, f32[56,128]{1,0:T(8,128)S(1)}, u32[]{:S(2)}, u32[]{:S(2)}) collective-permute-start(f32[56,128]{1,0:T(8,128)} %get-tuple-element.32), channel_id=1, source_target_pairs={{1,0},{2,1},{3,2},{4,3},{5,4},{6,5},{7,6},{8,7},{9,8},{10,9},{11,1... | collective-permute-start | bytes 86024 | tf_op jit(solution)/shard_map/ppermute | solution.py:42
  62.7 0.6 copy-start.2
  62.8 0.6 copy-start.3
  62.8 1.1 %copy-start = (f32[128,1,2432]{2,1,0:T(1,128)}, f32[128,1,2432]{2,1,0:T(1,128)S(1)}, u32[]{:S(2)}) copy-start(f32[128,1,2432]{2,1,0:T(1,128)S(1)} %all-to-all-done.1) | copy-start | bytes 3735556

commit v6 on v5

--- a/solution.py
+++ b/solution.py
@@ -37,9 +37,9 @@
 NN = (((1,), (0,)), ((), ()))
 
 
-def shift(value, by):
-    pairs = [(i, i + by) for i in range(DEVICES) if 0 <= i + by < DEVICES]
-    return lax.ppermute(value, AXES, pairs)
+def swap(value, first):
+    pairs = [(i, i + 1) for i in range(first, DEVICES - 1, 2)]
+    return lax.ppermute(value, AXES, pairs + [(j, i) for i, j in pairs])
 
 
 def split(value):
@@ -208,7 +208,7 @@
     asked = jnp.maximum(entry - CELLS, 0)
     source = jnp.floor((asked.astype(f32) + 0.5) * (1.0 / SLOT)).astype(i32)
     slot = asked - source * SLOT
-    side = jnp.where(source < me, FAR_ROWS, FAR_ROWS + EXTRA)
+    side = jnp.where((source | 1) == (me | 1), FAR_ROWS, FAR_ROWS + EXTRA)
     row = jnp.where(slot < SHORT, source * BLOCK + slot, side + slot - SHORT)
     key = jnp.where(entry < CELLS, -1, kind * REMOTE + row)
     used = jnp.sum(jnp.where(key >= 0, 1, 0), axis=0)
@@ -328,7 +328,7 @@
 
 def merge_kernel(
     me_ref, got_ref, freq_hbm, phase_hbm, stay_hbm, up_hbm,
-    send_ref, low_ref, high_ref, pole_hbm, basis_hbm, atoms_hbm,
+    send_ref, mate_ref, other_ref, pole_hbm, basis_hbm, atoms_hbm,
     freq, phase, stay, up, flat, atoms_ref, basis_ref, pole_ref, ring, turned, ids, first_ref, sems, out_sems,
 ):
     copies = load(sems, (freq_hbm, freq), (phase_hbm, phase), (stay_hbm, stay), (up_hbm, up))
@@ -373,8 +373,11 @@
         return 0
 
     lax.fori_loop(0, DEVICES, one, 0, unroll=8)
-    low_ref[...] = ring[pl.ds(first_ref[0, jnp.maximum(me - 1, 0)] + SHORT, EXTRA), :]
-    high_ref[...] = ring[pl.ds(first_ref[0, jnp.minimum(me + 1, DEVICES - 1)] + SHORT, EXTRA), :]
+    odd = lax.rem(me, 2)
+    mate = me + 1 - 2 * odd
+    other = jnp.clip(me - 1 + 2 * odd, 0, DEVICES - 1)
+    mate_ref[...] = ring[pl.ds(first_ref[0, mate] + SHORT, EXTRA), :]
+    other_ref[...] = ring[pl.ds(first_ref[0, other] + SHORT, EXTRA), :]
     for copy in outs:
         copy.wait()
 
@@ -415,18 +418,15 @@
     lax.fori_loop(first, last, pair, 0)
 
 
-def cross_kernel(
-    low_hbm, high_hbm, stay_hbm, new_hbm, stay_pair_hbm, low_out, high_out, pair_hbm, low, high, atoms_ref, pair_ref, *rest
-):
+def cross_kernel(stay_hbm, new_hbm, stay_pair_hbm, pair_hbm, atoms_ref, pair_ref, *rest):
     *pair_buffers, sems, out_sems = rest
     copies = load(
         sems, (stay_hbm, atoms_ref.at[:, pl.ds(0, STAY)]), (new_hbm, atoms_ref.at[:, pl.ds(STAY, ARRIVE)]),
-        (low_hbm, low), (high_hbm, high), (stay_pair_hbm, pair_ref.at[:, pl.ds(0, STAY)]),
+        (stay_pair_hbm, pair_ref.at[:, pl.ds(0, STAY)]),
     )
     pair_ref[:, STAY:] = jnp.zeros((1, ARRIVE), f32)
     for copy in copies:
         copy.wait()
-    outs = load(out_sems, (low, low_out), (high, high_out))
     pairs = Pairs(atoms_ref, pair_ref, *pair_buffers, STAY)
 
     def strip(c, _):
@@ -438,14 +438,12 @@
 
     lax.fori_loop(0, ARRIVE // TALL, strip, 0)
     pairs.close()
-    last = pltpu.make_async_copy(pair_ref, pair_hbm, out_sems.at[2])
-    last.start()
-    for copy in outs + [last]:
-        copy.wait()
-
-
-def mid_kernel(own_ref, count_ref, pole_hbm, ops_hbm, sum_hbm, table, both, ops, pole, sum_ref, sems):
-    copies = load(sems, (ops_hbm, ops), (pole_hbm, pole))
+    (out,) = load(out_sems, (pair_ref, pair_hbm))
+    out.wait()
+
+
+def mid_kernel(own_hbm, count_ref, pole_hbm, ops_hbm, sum_hbm, own_ref, table, both, ops, pole, sum_ref, sems):
+    copies = load(sems, (ops_hbm, ops), (pole_hbm, pole), (own_hbm, own_ref))
     table[OPS * CELLS :, :] = jnp.zeros((8, LANES), f32)
     copies[0].wait()
     load_ops(ops, both)
@@ -453,6 +451,7 @@
     width = CELLS // 2
     for lo in range(0, CELLS, width):
         premultiply(pole[lo : lo + width, :], both, table, lo, CELLS)
+    copies[2].wait()
 
     def store(r, g, total):
         sum_ref[pl.ds(r * LANES + g, 1), :] = total
@@ -460,21 +459,21 @@
     for n in range(LIST + 1):
         first = 0 if n == 0 else count_ref[LANES + n - 1]
         row_sums(own_ref, table, n, first, count_ref[LANES + n], None, store)
-    out = pltpu.make_async_copy(sum_ref, sum_hbm, sems.at[2])
+    out = pltpu.make_async_copy(sum_ref, sum_hbm, sems.at[3])
     out.start()
     out.wait()
 
 
 def last_kernel(
-    me_ref, index_ref, count_ref, place_ref, far_ref, below_ref, above_ref, ops_hbm, sum_hbm, inner_hbm, outer_hbm,
+    me_ref, index_hbm, count_ref, place_ref, far_ref, near_ref, next_ref, ops_hbm, sum_hbm, inner_hbm, outer_hbm,
     down_hbm, stay_hbm, new_hbm, stay_basis_hbm, new_basis_hbm, pair_hbm, local_ref, pot_ref,
-    table, both, sums_ref, rows, coarse, ops, inner, outer, down, atoms_ref, basis_ref, pair, sems,
+    index_ref, table, both, sums_ref, rows, coarse, ops, inner, outer, down, atoms_ref, basis_ref, pair, sems,
 ):
     copies = load(
         sems, (ops_hbm, ops), (sum_hbm, sums_ref), (inner_hbm, inner), (outer_hbm, outer), (down_hbm, down),
         (stay_hbm, atoms_ref.at[:, pl.ds(0, STAY)]), (new_hbm, atoms_ref.at[:, pl.ds(STAY, ARRIVE)]),
         (stay_basis_hbm, basis_ref.at[:, pl.ds(0, STAY)]), (new_basis_hbm, basis_ref.at[:, pl.ds(STAY, ARRIVE)]),
-        (pair_hbm, pair),
+        (pair_hbm, pair), (index_hbm, index_ref),
     )
     table[OPS * REMOTE :, :] = jnp.zeros((8, LANES), f32)
     copies[0].wait()
@@ -482,8 +481,8 @@
     width = FAR_ROWS // 4
     for lo in range(0, FAR_ROWS, width):
         premultiply(far_ref[lo : lo + width, :], both, table, lo, REMOTE)
-    premultiply(below_ref[...], both, table, FAR_ROWS, REMOTE)
-    premultiply(above_ref[...], both, table, FAR_ROWS + EXTRA, REMOTE)
+    premultiply(near_ref[...], both, table, FAR_ROWS, REMOTE)
+    premultiply(next_ref[...], both, table, FAR_ROWS + EXTRA, REMOTE)
 
     coarse[...] = far_ref[pl.ds(SHORT, DEVICES, stride=BLOCK), :]
     me = me_ref[0]
@@ -513,6 +512,7 @@
     def store(r, g, total):
         rows[pl.ds(place_ref.at[pl.ds(r * LANES, LANES)][g], 1), :] = total
 
+    copies[10].wait()
     for n in range(LIST, -1, -1):
         row_sums(
             index_ref, table, n, count_ref[n + 1], count_ref[n], lambda r, g: sums_ref[pl.ds(r * LANES + g, 1), :], store
@@ -543,7 +543,7 @@
 HB = pl.BlockSpec(memory_space=pltpu.HBM)
 
 
-def call(kernel, name, ins, outs, scratch, copies, flops, *operands):
+def call(kernel, name, ins, outs, scratch, copies, *operands):
     cost = pl.CostEstimate(flops=1000, bytes_accessed=1000, transcendentals=0)
     return pl.pallas_call(
         kernel,
@@ -583,7 +583,7 @@
 
     (outbound,) = call(
         pack_kernel, "pack", [SM, HB, HB, HB, HB], [(VM, (DEVICES * PIECE, LANES), f32)],
-        [((8, LANES), i32), ((STAY // LANES, LANES), i32), *mine[1:], ((8, 512), f32)], [4], 10**6,
+        [((8, LANES), i32), ((STAY // LANES, LANES), i32), *mine[1:], ((8, 512), f32)], [4],
         me, need_cells.transpose(0, 2, 1), atom_owner.reshape(STAY // LANES, LANES), atom_rows, cell_row,
     )
     got = lax.all_to_all(outbound.reshape(DEVICES, 1, PIECE * LANES), AXES, split_axis=0, concat_axis=0, tiled=True)
@@ -597,41 +597,41 @@
     stay_atoms, stay_basis, stay_pole, stay_pair, own_index, far_index, place, counts = call(
         early_kernel, "early", [SM] + [HB] * 7, [(HB, *out) for out in early_outs],
         [*mine, *waves, *[((LIST, CELLS), i32)] * 2, *[(shape3, i32)] * 2, ((80, CELLS), f32), ((8, LANES), f32), *early_outs,
-         *pair_scratch(STAY, STAY)], [7, 8], 12 * 10**9,
+         *pair_scratch(STAY, STAY)], [7, 8],
         me, owner_row, atom_rows, cell_row, freq, phase, list_entry, list_class,
     )
     own_index, far_index, place, counts = (one.reshape(-1) for one in (own_index, far_index, place, counts))
     merge_outs = [((CELLS, LANES), f32), ((LANES, ARRIVE), f32), ((8, ARRIVE), f32)]
-    send, low, high, pole, new_basis, new_atoms = call(
+    send, mate_rows, other_rows, pole, new_basis, new_atoms = call(
         merge_kernel, "merge", [SM, VM] + [HB] * 4,
         [(VM, (FAR_ROWS, LANES), f32), (VM, (EXTRA, LANES), f32), (VM, (EXTRA, LANES), f32), *[(HB, *out) for out in merge_outs]],
         [*waves, ((CELLS, LANES), f32), ops_shape, ((8, LANES), f32), *merge_outs[::-1],
          ((WRAP, LANES), f32), ((LANES, LANES), f32), ((1, LANES), i32), (pltpu.SMEM((1, LANES), i32), None)],
-        [5, 3], 2 * 10**9,
+        [5, 3],
         me, got, freq, phase, stay_pole, by_row[1],
     )
     far_rows = lax.all_to_all(send.reshape(DEVICES, 1, BLOCK * LANES), AXES, split_axis=0, concat_axis=0, tiled=True)
     far_rows = far_rows.reshape(FAR_ROWS, LANES)
-    extra = ((EXTRA, LANES), f32)
-    low, high, pair = call(
-        cross_kernel, "cross", [HB] * 5, [(HB, *extra), (HB, *extra), (HB, (1, SLOTS), f32)],
-        [extra, extra, ((8, SLOTS), f32), ((1, SLOTS), f32), *pair_scratch(SLOTS, ARRIVE)], [5, 3], 4 * 10**9,
-        low, high, stay_atoms, new_atoms, stay_pair,
-    )
-    below, above = shift(high, 1), shift(low, -1)
+    near_rows, next_rows = swap(mate_rows, 0), swap(other_rows, 1)
+    (pair,) = call(
+        cross_kernel, "cross", [HB] * 3, [(HB, (1, SLOTS), f32)],
+        [((8, SLOTS), f32), ((1, SLOTS), f32), *pair_scratch(SLOTS, ARRIVE)], [3, 1],
+        stay_atoms, new_atoms, stay_pair,
+    )
+    index_scratch = (pltpu.SMEM((LIST * CELLS,), i32), None)
     (own_sum,) = call(
-        mid_kernel, "mid", [SM, SM, HB, HB], [(HB, (CELLS, LANES), f32)],
-        [((OPS * CELLS + 8, LANES), f32), ((OPS * LANES, 3 * LANES), bf16), ops_shape, *[((CELLS, LANES), f32)] * 2],
-        [3], 20 * 10**9,
+        mid_kernel, "mid", [HB, SM, HB, HB], [(HB, (CELLS, LANES), f32)],
+        [index_scratch, ((OPS * CELLS + 8, LANES), f32), ((OPS * LANES, 3 * LANES), bf16), ops_shape, *[((CELLS, LANES), f32)] * 2],
+        [4],
         own_index, counts, pole, by_row[0],
     )
     local, pot = call(
-        last_kernel, "last", [SM] * 4 + [VM] * 3 + [HB] * 10, [(VM, (COEF, CELLS), f32), (VM, (SLOTS // LANES, LANES), f32)],
-        [((OPS * REMOTE + 8, LANES), f32), ((OPS * LANES, 3 * LANES), bf16), *[((CELLS, LANES), f32)] * 2, ((DEVICES, LANES), f32),
+        last_kernel, "last", [SM, HB, SM, SM] + [VM] * 3 + [HB] * 10, [(VM, (COEF, CELLS), f32), (VM, (SLOTS // LANES, LANES), f32)],
+        [index_scratch, ((OPS * REMOTE + 8, LANES), f32), ((OPS * LANES, 3 * LANES), bf16), *[((CELLS, LANES), f32)] * 2, ((DEVICES, LANES), f32),
          ops_shape, ((COEF, MEMBERS - 1, COEF), f32), ((GROUPS - 1, COEF, COEF), f32), ops_shape, ((8, SLOTS), f32),
          ((LANES, SLOTS), f32), ((1, SLOTS), f32)],
-        [10], 8 * 10**9,
-        me, far_index, counts, place, far_rows, below, above, by_row[0], own_sum,
+        [11],
+        me, far_index, counts, place, far_rows, near_rows, next_rows, by_row[0], own_sum,
         far_in.transpose(1, 0, 2), far_out, by_row[2], stay_atoms, new_atoms, stay_basis, new_basis, pair,
     )
     return local, pot.reshape(SLOTS)

time: 78.5 us -> 74.8 us (0.953)
  the two profiles are of different devices: /device:TPU:8 before, /device:TPU:1 now
where the time goes in v6:
time: 74.8 us; the launch traced here: 74.1 us
  Pallas kernels  43.4 us (58%)
  starting transfers between devices  22.1 us (30%)
  waiting for transfers between devices  5.77 us (8%)
  local copies, waits for them, and re-layouts  1.83 us (2%)
  between operations  0.92 us (1%)
    pallas_call x6, Pallas kernels, call(): pl.pallas_call(kernel, name=name, in_specs=ins, out_specs=[spec for spec,...  43.4 us
    all_to_all x1, starting transfers between devices, on_device(): lax.all_to_all(outbound.reshape(DEVICES, 1, PIECE * LANES), AXES, split_a...  11.5 us
    all_to_all x1, starting transfers between devices, on_device(): lax.all_to_all(send.reshape(DEVICES, 1, BLOCK * LANES), AXES, split_axis=...  6.85 us
    ppermute x2, starting transfers between devices, swap(): return lax.ppermute(value, AXES, pairs + [(j, i) for i, j in pairs])  3.76 us
    all_to_all x1, waiting for transfers between devices, on_device(): lax.all_to_all(outbound.reshape(DEVICES, 1, PIECE * LANES), AXES, split_a...  2.91 us
    all_to_all x1, waiting for transfers between devices, on_device(): lax.all_to_all(send.reshape(DEVICES, 1, BLOCK * LANES), AXES, split_axis=...  2.85 us
    unnamed x12, local copies, waits for them, and re-layouts  1.83 us
  transfers between devices with their start and end apart: 4, of which 2 were waited for; matrix products, arithmetic and copies ran while one was open for 0% of the time, Pallas kernels for 32%

profile of v6, /device:TPU:1, one launch (start us, length us, event | category | flops | bytes accessed | tf_op | source)
XLA Modules:
  0.0 74.1 jit_solution(14982859532119381818)
XLA Ops:
  0.6 1.8 %pack.1 = f32[768,128]{1,0:T(8,128)} custom-call(s32[1]{0:T(128)} %bitcast.me_ref, s32[1,72,128]{2,1,0:T(8,128)} %bitcast.37, s32[16,128]{1,0:T(8,128)} %bitcast.38, f32[4,2048]{1,0:T(4,128)} %rows_hbm.3, s32[1,2048]{1,0:T(1,128)} %bitcast.40), custom_call_target="tpu_custom_call" | custom-call | flops 1000 | bytes 1000 | tf_op jit(solution)/shard_map/pack/pallas_call | solution.py:548
  2.4 11.5 %all-to-all-start = ((f32[128,1,768]{2,1,0:T(1,128)}), f32[128,1,768]{2,1,0:T(1,128)S(1)}, u32[]{:S(2)}, u32[]{:S(2)}) async-start(f32[128,1,768]{2,1,0:T(1,128)} %bitcast.30), calls=%async_computation | async-start | bytes 786432 | tf_op jit(solution)/shard_map/all_to_all | solution.py:589
  13.9 9.4 %early.1 = (f32[8,2048]{1,0:T(8,128)}, f32[128,2048]{1,0:T(8,128)}, f32[1024,128]{1,0:T(8,128)}, f32[1,2048]{1,0:T(1,128)}, s32[16,8,128]{2,1,0:T(8,128)}, /*ind...) custom-call(s32[1]{0:T(128)} %bitcast.me_ref, s32[1,2048]{1,0:T(1,128)} %bitcast.39, f32[4,2048]{1,0:T(4,128)} %rows_hbm.3, ...), custom_call_target="tpu_custom_call" | custom-call | flops 1000 | bytes 1000 | tf_op jit(solution)/shard_map/early/pallas_call | solution.py:548
  23.3 2.9 %all-to-all-done = f32[128,1,768]{2,1,0:T(1,128)S(1)} async-done(((f32[128,1,768]{2,1,0:T(1,128)}), f32[128,1,768]{2,1,0:T(1,128)S(1)}, u32[]{:S(2)}, u32[]{:S(2)}) %all-to-all-start) | async-done | bytes 393248 | tf_op jit(solution)/shard_map/all_to_all | solution.py:589
  26.2 0.0 copy-start.1
  26.2 0.7 %copy-done.1 = f32[128,1,768]{2,1,0:T(1,128)} copy-done((f32[128,1,768]{2,1,0:T(1,128)}, f32[128,1,768]{2,1,0:T(1,128)S(1)}, u32[]{:S(2)}) %copy-start.1) | copy-done | bytes 393240
  27.0 4.6 %merge.1 = (f32[2432,128]{1,0:T(8,128)}, f32[56,128]{1,0:T(8,128)}, f32[56,128]{1,0:T(8,128)}, f32[1024,128]{1,0:T(8,128)}, f32[128,512]{1,0:T(8,128)}, /*index=5*/f32[8,512]{1,0:T(8,128)}) custom-call(s32[1]{0:T(128)} %bitcast.me_ref, f32[768,128]{1,0:T(8,128)} %bitcast.31, f32[3,121]{1,0:T(4,128)} %bitcast.45, f32[1,121]{1,0:T(1,128)} %bitcast.48, ...), custom_call_target="tpu_custom_call" | custom-call | flops 1000 | bytes 1000 | tf_op jit(solution)/shard_map/merge/pallas_call | solution.py:548
  31.6 0.0 copy-start.5
  31.6 0.0 copy-start.4
  31.6 6.8 %all-to-all-start.1 = ((f32[128,1,2432]{2,1,0:T(1,128)}), f32[128,1,2432]{2,1,0:T(1,128)S(1)}, u32[]{:S(2)}, u32[]{:S(2)}) async-start(f32[128,1,2432]{2,1,0:T(1,128)} %bitcast.32), calls=%async_computation.1 | async-start | bytes 2490368 | tf_op jit(solution)/shard_map/all_to_all | solution.py:613
  38.4 0.0 copy-done.5
  38.5 1.1 %collective-permute-start = (f32[56,128]{1,0:T(8,128)S(1)}, f32[56,128]{1,0:T(8,128)S(1)}, u32[]{:S(2)}, u32[]{:S(2)}) collective-permute-start(f32[56,128]{1,0:T(8,128)S(1)} %copy-done.5), channel_id=1, source_target_pairs={{0,1},{2,3},{4,5},{6,7},{8,9},{10,11},{12,13},{14,15},{16,17},{18,... | collective-permute-start | bytes 86024 | tf_op jit(solution)/shard_map/ppermute | solution.py:42
  39.6 0.0 copy-done.4
  39.6 2.6 %collective-permute-start.1 = (f32[56,128]{1,0:T(8,128)S(1)}, f32[56,128]{1,0:T(8,128)S(1)}, u32[]{:S(2)}, u32[]{:S(2)}) collective-permute-start(f32[56,128]{1,0:T(8,128)S(1)} %copy-done.4), channel_id=1, source_target_pairs={{1,2},{3,4},{5,6},{7,8},{9,10},{11,12},{13,14},{15,16},{17,18},{19... | collective-permute-start | bytes 86024 | tf_op jit(solution)/shard_map/ppermute | solution.py:42
  42.2 3.7 %cross.1.pair_hbm = f32[1,2560]{1,0:T(1,128)} custom-call(f32[8,2048]{1,0:T(8,128)} %get-tuple-element.27.stay_hbm, f32[8,512]{1,0:T(8,128)} %get-tuple-element.28.new_hbm, f32[1,2048]{1,0:T(1,128)} %get-tuple-element.31.stay_pair_hbm), custom_call_target="tpu_custom_call" | custom-call | flops 1000 | bytes 1000 | tf_op jit(solution)/shard_map/cross/pallas_call | solution.py:548
  45.9 10.8 %mid.1.sum_hbm = f32[1024,128]{1,0:T(8,128)} custom-call(s32[16384]{0:T(1024)} %bitcast.36, s32[1024]{0:T(1024)} %bitcast.42, f32[1024,128]{1,0:T(8,128)} %get-tuple-element.26.pole_hbm, f32[968,121]{1,0:T(8,128)} %bitcast.28), custom_call_target="tpu_custom_call" | custom-call | flops 1000 | bytes 1000 | tf_op jit(solution)/shard_map/mid/pallas_call | solution.py:548
  56.7 0.0 collective-permute-done.near_ref
  56.7 0.0 copy-start.2
  56.7 0.0 collective-permute-done.1.next_ref
  56.7 0.0 copy-start.3
  56.7 2.9 %all-to-all-done.1 = f32[128,1,2432]{2,1,0:T(1,128)S(1)} async-done(((f32[128,1,2432]{2,1,0:T(1,128)}), f32[128,1,2432]{2,1,0:T(1,128)S(1)}, u32[]{:S(2)}, u32[]{:S(2)}) %all-to-all-start.1) | async-done | bytes 1245216 | tf_op jit(solution)/shard_map/all_to_all | solution.py:613
  59.6 0.0 copy-start
  59.6 0.0 copy-done.2
  59.6 0.0 copy-done.3
  59.6 1.1 %copy-done = f32[128,1,2432]{2,1,0:T(1,128)} copy-done((f32[128,1,2432]{2,1,0:T(1,128)}, f32[128,1,2432]{2,1,0:T(1,128)S(1)}, u32[]{:S(2)}) %copy-start) | copy-done | bytes 1245208
  60.7 13.2 %last.1 = (f32[121,1024]{1,0:T(8,128)}, f32[20,128]{1,0:T(8,128)}) custom-call(s32[1]{0:T(128)} %bitcast.me_ref, s32[16384]{0:T(1024)} %bitcast.35, s32[1024]{0:T(1024)} %bitcast.43, s32[1024]{0:T(1024)} %bitcast.46, f32[2432,128]{1,0:T(8,128)} %bitcast.26, f32[56,128]{1,0:T(8,128)} %copy-done.2, f32[56,128]{1,0:T(8,128)} %copy-done.3, f32[968,121]{1,0:T(8,128)} %bitcast.29, ...), custom_call_target="tpu_custom_call" | custom-call | flops 1000 | bytes 1000 | tf_op jit(solution)/shard_map/last/pallas_call | solution.py:548
Async XLA Ops:
  2.4 23.8 %all-to-all-start = ((f32[128,1,768]{2,1,0:T(1,128)}), f32[128,1,768]{2,1,0:T(1,128)S(1)}, u32[]{:S(2)}, u32[]{:S(2)}) async-start(f32[128,1,768]{2,1,0:T(1,128)} %bitcast.30), calls=%async_computation | async-start | bytes 786432 | tf_op jit(solution)/shard_map/all_to_all | solution.py:589
  26.2 0.7 %copy-start.1 = (f32[128,1,768]{2,1,0:T(1,128)}, f32[128,1,768]{2,1,0:T(1,128)S(1)}, u32[]{:S(2)}) copy-start(f32[128,1,768]{2,1,0:T(1,128)S(1)} %all-to-all-done) | copy-start | bytes 1179652
  31.6 6.9 %copy-start.5 = (f32[56,128]{1,0:T(8,128)S(1)}, f32[56,128]{1,0:T(8,128)}, u32[]{:S(2)}) copy-start(f32[56,128]{1,0:T(8,128)} %get-tuple-element.23) | copy-start | bytes 86020
  31.6 8.0 %copy-start.4 = (f32[56,128]{1,0:T(8,128)S(1)}, f32[56,128]{1,0:T(8,128)}, u32[]{:S(2)}) copy-start(f32[56,128]{1,0:T(8,128)} %get-tuple-element.24) | copy-start | bytes 86020
  31.6 28.0 %all-to-all-start.1 = ((f32[128,1,2432]{2,1,0:T(1,128)}), f32[128,1,2432]{2,1,0:T(1,128)S(1)}, u32[]{:S(2)}, u32[]{:S(2)}) async-start(f32[128,1,2432]{2,1,0:T(1,128)} %bitcast.32), calls=%async_computation.1 | async-start | bytes 2490368 | tf_op jit(solution)/shard_map/all_to_all | solution.py:613
  38.5 18.3 %collective-permute-start = (f32[56,128]{1,0:T(8,128)S(1)}, f32[56,128]{1,0:T(8,128)S(1)}, u32[]{:S(2)}, u32[]{:S(2)}) collective-permute-start(f32[56,128]{1,0:T(8,128)S(1)} %copy-done.5), channel_id=1, source_target_pairs={{0,1},{2,3},{4,5},{6,7},{8,9},{10,11},{12,13},{14,15},{16,17},{18,... | collective-permute-start | bytes 86024 | tf_op jit(solution)/shard_map/ppermute | solution.py:42
  39.6 17.1 %collective-permute-start.1 = (f32[56,128]{1,0:T(8,128)S(1)}, f32[56,128]{1,0:T(8,128)S(1)}, u32[]{:S(2)}, u32[]{:S(2)}) collective-permute-start(f32[56,128]{1,0:T(8,128)S(1)} %copy-done.4), channel_id=1, source_target_pairs={{1,2},{3,4},{5,6},{7,8},{9,10},{11,12},{13,14},{15,16},{17,18},{19... | collective-permute-start | bytes 86024 | tf_op jit(solution)/shard_map/ppermute | solution.py:42
  56.7 2.9 %copy-start.2 = (f32[56,128]{1,0:T(8,128)}, f32[56,128]{1,0:T(8,128)S(1)}, u32[]{:S(2)}) copy-start(f32[56,128]{1,0:T(8,128)S(1)} %collective-permute-done.near_ref) | copy-start | bytes 86020
  56.7 2.9 %copy-start.3 = (f32[56,128]{1,0:T(8,128)}, f32[56,128]{1,0:T(8,128)S(1)}, u32[]{:S(2)}) copy-start(f32[56,128]{1,0:T(8,128)S(1)} %collective-permute-done.1.next_ref) | copy-start | bytes 86020
  59.6 1.1 %copy-start = (f32[128,1,2432]{2,1,0:T(1,128)}, f32[128,1,2432]{2,1,0:T(1,128)S(1)}, u32[]{:S(2)}) copy-start(f32[128,1,2432]{2,1,0:T(1,128)S(1)} %all-to-all-done.1) | copy-start | bytes 3735556

commit v7 on v6

--- a/solution.py
+++ b/solution.py
@@ -29,6 +29,7 @@
 WRAP = CELLS + 80
 TALL, WIDE = 256, 512
 AXES = ("group", "dev")
+LIMITS = {"pack": 56, "early": 56}
 MIB = 2**20
 f32, bf16, i32 = jnp.float32, jnp.bfloat16, jnp.int32
 SIN = [(-1) ** n * (2 * math.pi) ** (2 * n + 1) / math.factorial(2 * n + 1) for n in range(6)]
@@ -554,7 +555,7 @@
         scratch_shapes=[pltpu.VMEM(shape, kind) if isinstance(shape, tuple) else shape for shape, kind in scratch]
         + [pltpu.SemaphoreType.DMA((count,)) for count in copies],
         cost_estimate=cost,
-        compiler_params=pltpu.CompilerParams(vmem_limit_bytes=56 * MIB),
+        compiler_params=pltpu.CompilerParams(vmem_limit_bytes=LIMITS.get(name, 52) * MIB),
     )(*operands)
 
 

time: 74.8 us -> 71.4 us (0.955)
  Pallas kernels: 43.4 us -> 39.1 us
  waiting for transfers between devices: 5.77 us -> 7.36 us
  local copies, waits for them, and re-layouts: 1.83 us -> 0.84 us
    pallas_call x6, Pallas kernels: 43.4 us -> 39.1 us  [call(): pl.pallas_call(kernel, name=name, in_specs=ins, out_specs=[spec for spec,...]
    all_to_all x1, waiting for transfers between devices: 2.85 us -> 4.42 us  [on_device(): lax.all_to_all(send.reshape(DEVICES, 1, BLOCK * LANES), AXES, split_axis=...]
    unnamed x12 -> x26, local copies, waits for them, and re-layouts: 1.83 us -> 0.84 us
  transfers between devices with their start and end apart: 4 -> 4, of which waited for: 2 -> 2; matrix products, arithmetic and copies ran while one was open for 0% -> 0% of each run, Pallas kernels for 32% -> 30%
where the time goes in v7:
time: 71.4 us; the launch traced here: 70.9 us
  Pallas kernels  39.1 us (55%)
  starting transfers between devices  22.5 us (32%)
  waiting for transfers between devices  7.36 us (10%)
  between operations  1.02 us (1%)
  local copies, waits for them, and re-layouts  0.84 us (1%)
    pallas_call x6, Pallas kernels, call(): pl.pallas_call(kernel, name=name, in_specs=ins, out_specs=[spec for spec,...  39.1 us
    all_to_all x1, starting transfers between devices, on_device(): lax.all_to_all(outbound.reshape(DEVICES, 1, PIECE * LANES), AXES, split_a...  11.5 us
    all_to_all x1, starting transfers between devices, on_device(): lax.all_to_all(send.reshape(DEVICES, 1, BLOCK * LANES), AXES, split_axis=...  7.27 us
    all_to_all x1, waiting for transfers between devices, on_device(): lax.all_to_all(send.reshape(DEVICES, 1, BLOCK * LANES), AXES, split_axis=...  4.42 us
    ppermute x2, starting transfers between devices, swap(): return lax.ppermute(value, AXES, pairs + [(j, i) for i, j in pairs])  3.76 us
    all_to_all x1, waiting for transfers between devices, on_device(): lax.all_to_all(outbound.reshape(DEVICES, 1, PIECE * LANES), AXES, split_a...  2.93 us
  transfers between devices with their start and end apart: 4, of which 2 were waited for; matrix products, arithmetic and copies ran while one was open for 0% of the time, Pallas kernels for 30%

profile of v7, /device:TPU:1, one launch (start us, length us, event | category | flops | bytes accessed | tf_op | source)
XLA Modules:
  0.0 70.9 jit_solution(10396720656756797954)
XLA Ops:
  0.6 0.0 copy-start.9
  0.6 0.0 copy-start.12
  0.7 0.0 copy-start.2
  0.7 1.8 %pack.1 = f32[768,128]{1,0:T(8,128)} custom-call(s32[1]{0:T(128)} %bitcast.me_ref, s32[1,72,128]{2,1,0:T(8,128)} %bitcast.43, s32[16,128]{1,0:T(8,128)} %bitcast.44, f32[4,2048]{1,0:T(4,128)} %rows_hbm.3, s32[1,2048]{1,0:T(1,128)} %bitcast.46), custom_call_target="tpu_custom_call" | custom-call | flops 1000 | bytes 1000 | tf_op jit(solution)/shard_map/pack/pallas_call | solution.py:549
  2.5 11.5 %all-to-all-start = ((f32[128,1,768]{2,1,0:T(1,128)}), f32[128,1,768]{2,1,0:T(1,128)S(1)}, u32[]{:S(2)}, u32[]{:S(2)}) async-start(f32[128,1,768]{2,1,0:T(1,128)} %bitcast.41), calls=%async_computation | async-start | bytes 786432 | tf_op jit(solution)/shard_map/all_to_all | solution.py:590
  14.0 9.4 %early.1 = (f32[8,2048]{1,0:T(8,128)}, f32[128,2048]{1,0:T(8,128)}, f32[1024,128]{1,0:T(8,128)}, f32[1,2048]{1,0:T(1,128)}, s32[16,8,128]{2,1,0:T(8,128)}, /*ind...) custom-call(s32[1]{0:T(128)} %bitcast.me_ref, s32[1,2048]{1,0:T(1,128)} %bitcast.45, f32[4,2048]{1,0:T(4,128)} %rows_hbm.3, ...), custom_call_target="tpu_custom_call" | custom-call | flops 1000 | bytes 1000 | tf_op jit(solution)/shard_map/early/pallas_call | solution.py:549
  23.4 2.9 %all-to-all-done = f32[128,1,768]{2,1,0:T(1,128)S(1)} async-done(((f32[128,1,768]{2,1,0:T(1,128)}), f32[128,1,768]{2,1,0:T(1,128)S(1)}, u32[]{:S(2)}, u32[]{:S(2)}) %all-to-all-start) | async-done | bytes 393248 | tf_op jit(solution)/shard_map/all_to_all | solution.py:590
  26.3 0.0 copy-done.9
  26.3 0.0 copy-done.12
  26.4 0.0 copy-done.2
  26.4 3.1 %merge.1 = (f32[2432,128]{1,0:T(8,128)}, f32[56,128]{1,0:T(8,128)S(1)}, f32[56,128]{1,0:T(8,128)S(1)}, f32[1024,128]{1,0:T(8,128)S(1)}, f32[128,512]{1,0:T(8,128)S(1)}, /*index=5*/f32[8,512]{1,0:T(8,128)S(1)}) custom-call(s32[1]{0:T(128)} %bitcast.me_ref, f32[768,128]{1,0:T(8,128)S(1)} %bitcast.28, f32[3,121]{1,0:T(4,128)S(1)} %bitcast.36, ...), custom_call_target="tpu_custom_call" | custom-call | flops 1000 | bytes 1000 | tf_op jit(solution)/shard_map/merge/pallas_call | solution.py:549
  29.5 0.0 copy-start.4
  29.5 0.0 copy-start.10
  29.5 0.0 copy-start.1
  29.5 0.0 copy-start.7
  29.5 0.0 copy-start.8
  29.6 7.3 %all-to-all-start.1 = ((f32[128,1,2432]{2,1,0:T(1,128)}), f32[128,1,2432]{2,1,0:T(1,128)}, u32[]{:S(2)}, u32[]{:S(2)}) async-start(f32[128,1,2432]{2,1,0:T(1,128)} %bitcast.42), calls=%async_computation.1 | async-start | bytes 2490368 | tf_op jit(solution)/shard_map/all_to_all | solution.py:614
  36.8 0.0 copy-start.3
  36.8 0.0 copy-start.5
  36.9 0.0 copy-start.6
  36.9 0.0 copy-start.11
  36.9 1.2 %collective-permute-start = (f32[56,128]{1,0:T(8,128)S(1)}, f32[56,128]{1,0:T(8,128)S(1)}, u32[]{:S(2)}, u32[]{:S(2)}) collective-permute-start(f32[56,128]{1,0:T(8,128)S(1)} %get-tuple-element.23), channel_id=1, source_target_pairs={{0,1},{2,3},{4,5},{6,7},{8,9},{10,11},{12,13},{14,15},{16,17},{18,... | collective-permute-start | bytes 86024 | tf_op jit(solution)/shard_map/ppermute | solution.py:43
  38.1 2.5 %collective-permute-start.1 = (f32[56,128]{1,0:T(8,128)S(1)}, f32[56,128]{1,0:T(8,128)S(1)}, u32[]{:S(2)}, u32[]{:S(2)}) collective-permute-start(f32[56,128]{1,0:T(8,128)S(1)} %get-tuple-element.24), channel_id=1, source_target_pairs={{1,2},{3,4},{5,6},{7,8},{9,10},{11,12},{13,14},{15,16},{17,18},{19... | collective-permute-start | bytes 86024 | tf_op jit(solution)/shard_map/ppermute | solution.py:43
  40.6 0.0 copy-done.4
  40.6 0.0 copy-done.10
  40.7 2.4 %cross.1.pair_hbm = f32[1,2560]{1,0:T(1,128)S(1)} custom-call(f32[8,2048]{1,0:T(8,128)S(1)} %copy-done.4, f32[8,512]{1,0:T(8,128)S(1)} %get-tuple-element.28.new_hbm, f32[1,2048]{1,0:T(1,128)S(1)} %copy-done.10), custom_call_target="tpu_custom_call" | custom-call | flops 1000 | bytes 1000 | tf_op jit(solution)/shard_map/cross/pallas_call | solution.py:549
  43.0 0.0 copy-done.1
  43.1 0.0 copy-done.7
  43.1 0.0 copy-done.8
  43.1 9.4 %mid.1.sum_hbm = f32[1024,128]{1,0:T(8,128)S(1)} custom-call(s32[16384]{0:T(1024)S(1)} %bitcast.32, s32[1024]{0:T(1024)S(1)} %bitcast.33, f32[1024,128]{1,0:T(8,128)S(1)} %get-tuple-element.26.pole_hbm, f32[968,121]{1,0:T(8,128)S(1)} %bitcast.26), custom_call_target="tpu_custom_call" | custom-call | flops 1000 | bytes 1000 | tf_op jit(solution)/shard_map/mid/pallas_call | solution.py:549
  52.5 0.0 copy-start
  52.5 0.8 %copy-done = f32[1024,128]{1,0:T(8,128)} copy-done((f32[1024,128]{1,0:T(8,128)}, f32[1024,128]{1,0:T(8,128)S(1)}, u32[]{:S(2)}) %copy-start) | copy-done | bytes 524312
  53.3 0.0 collective-permute-done.near_ref
  53.3 0.0 collective-permute-done.1.next_ref
  53.3 4.4 %all-to-all-done.1 = f32[128,1,2432]{2,1,0:T(1,128)} async-done(((f32[128,1,2432]{2,1,0:T(1,128)}), f32[128,1,2432]{2,1,0:T(1,128)}, u32[]{:S(2)}, u32[]{:S(2)}) %all-to-all-start.1) | async-done | bytes 1245216 | tf_op jit(solution)/shard_map/all_to_all | solution.py:614
  57.7 0.0 copy-done.3
  57.7 0.0 copy-done.5
  57.7 0.0 copy-done.6
  57.7 0.0 copy-done.11
  57.7 13.0 %last.1 = (f32[121,1024]{1,0:T(8,128)}, f32[20,128]{1,0:T(8,128)}) custom-call(s32[1]{0:T(128)} %bitcast.me_ref, s32[16384]{0:T(1024)S(1)} %bitcast.31, s32[1024]{0:T(1024)S(1)} %bitcast.34, s32[1024]{0:T(1024)S(1)} %bitcast.37, f32[2432,128]{1,0:T(8,128)} %bitcast.15.far_ref, f32[56,128]{1,0:T(8,128)S(1)} %collective-permute-done.near_ref, ...), custom_call_target="tpu_custom_call" | custom-call | flops 1000 | bytes 1000 | tf_op jit(solution)/shard_map/last/pallas_call | solution.py:549
Async XLA Ops:
  0.6 25.7 %copy-start.9 = (f32[121,3]{0,1:T(4,128)S(1)}, f32[121,3]{0,1:T(4,128)}, u32[]{:S(2)}) copy-start(f32[121,3]{0,1:T(4,128)} %param.19) | copy-start | bytes 4360
  0.6 25.7 %copy-start.12 = (f32[121]{0:T(128)S(1)}, f32[121]{0:T(128)}, u32[]{:S(2)}) copy-start(f32[121]{0:T(128)} %param.20) | copy-start | bytes 1456
  0.7 25.7 %copy-start.2 = (f32[8,121,121]{2,0,1:T(8,128)S(1)}, f32[8,121,121]{2,0,1:T(8,128)}, u32[]{:S(2)}) copy-start(f32[8,121,121]{2,0,1:T(8,128)} %param.22) | copy-start | bytes 1405540
  2.5 23.8 %all-to-all-start = ((f32[128,1,768]{2,1,0:T(1,128)}), f32[128,1,768]{2,1,0:T(1,128)S(1)}, u32[]{:S(2)}, u32[]{:S(2)}) async-start(f32[128,1,768]{2,1,0:T(1,128)} %bitcast.41), calls=%async_computation | async-start | bytes 786432 | tf_op jit(solution)/shard_map/all_to_all | solution.py:590
  29.5 11.1 %copy-start.4 = (f32[8,2048]{1,0:T(8,128)S(1)}, f32[8,2048]{1,0:T(8,128)}, u32[]{:S(2)}) copy-start(f32[8,2048]{1,0:T(8,128)} %get-tuple-element.27.stay_hbm) | copy-start | bytes 196612
  29.5 11.1 %copy-start.10 = (f32[1,2048]{1,0:T(1,128)S(1)}, f32[1,2048]{1,0:T(1,128)}, u32[]{:S(2)}) copy-start(f32[1,2048]{1,0:T(1,128)} %get-tuple-element.31.stay_pair_hbm) | copy-start | bytes 24580
  29.5 13.5 %copy-start.1 = (f32[8,121,121]{2,0,1:T(8,128)S(1)}, f32[8,121,121]{2,0,1:T(8,128)}, u32[]{:S(2)}) copy-start(f32[8,121,121]{2,0,1:T(8,128)} %param.21) | copy-start | bytes 1405540
  29.5 13.5 %copy-start.7 = (s32[16,8,128]{2,1,0:T(8,128)S(1)}, s32[16,8,128]{2,1,0:T(8,128)}, u32[]{:S(2)}) copy-start(s32[16,8,128]{2,1,0:T(8,128)} %get-tuple-element.25) | copy-start | bytes 196612
  29.5 13.5 %copy-start.8 = (s32[8,128]{1,0:T(8,128)S(1)}, s32[8,128]{1,0:T(8,128)}, u32[]{:S(2)}) copy-start(s32[8,128]{1,0:T(8,128)} %get-tuple-element.19) | copy-start | bytes 12292
  29.6 28.1 %all-to-all-start.1 = ((f32[128,1,2432]{2,1,0:T(1,128)}), f32[128,1,2432]{2,1,0:T(1,128)}, u32[]{:S(2)}, u32[]{:S(2)}) async-start(f32[128,1,2432]{2,1,0:T(1,128)} %bitcast.42), calls=%async_computation.1 | async-start | bytes 2490368 | tf_op jit(solution)/shard_map/all_to_all | solution.py:614
  36.8 20.9 %copy-start.3 = (f32[8,121,121]{2,0,1:T(8,128)S(1)}, f32[8,121,121]{2,0,1:T(8,128)}, u32[]{:S(2)}) copy-start(f32[8,121,121]{2,0,1:T(8,128)} %param.25) | copy-start | bytes 1405540
  36.8 20.9 %copy-start.5 = (f32[3,121,121]{2,1,0:T(8,128)S(1)}, f32[3,121,121]{2,1,0:T(8,128)}, u32[]{:S(2)}) copy-start(f32[3,121,121]{2,1,0:T(8,128)} %outer_hbm.1) | copy-start | bytes 527080
  36.9 20.8 %copy-start.6 = (s32[16,8,128]{2,1,0:T(8,128)S(1)}, s32[16,8,128]{2,1,0:T(8,128)}, u32[]{:S(2)}) copy-start(s32[16,8,128]{2,1,0:T(8,128)} %get-tuple-element.18) | copy-start | bytes 196612
  36.9 20.8 %copy-start.11 = (s32[8,128]{1,0:T(8,128)S(1)}, s32[8,128]{1,0:T(8,128)}, u32[]{:S(2)}) copy-start(s32[8,128]{1,0:T(8,128)} %get-tuple-element.20) | copy-start | bytes 12292
  36.9 16.4 %collective-permute-start = (f32[56,128]{1,0:T(8,128)S(1)}, f32[56,128]{1,0:T(8,128)S(1)}, u32[]{:S(2)}, u32[]{:S(2)}) collective-permute-start(f32[56,128]{1,0:T(8,128)S(1)} %get-tuple-element.23), channel_id=1, source_target_pairs={{0,1},{2,3},{4,5},{6,7},{8,9},{10,11},{12,13},{14,15},{16,17},{18,... | collective-permute-start | bytes 86024 | tf_op jit(solution)/shard_map/ppermute | solution.py:43
  38.1 15.2 %collective-permute-start.1 = (f32[56,128]{1,0:T(8,128)S(1)}, f32[56,128]{1,0:T(8,128)S(1)}, u32[]{:S(2)}, u32[]{:S(2)}) collective-permute-start(f32[56,128]{1,0:T(8,128)S(1)} %get-tuple-element.24), channel_id=1, source_target_pairs={{1,2},{3,4},{5,6},{7,8},{9,10},{11,12},{13,14},{15,16},{17,18},{19... | collective-permute-start | bytes 86024 | tf_op jit(solution)/shard_map/ppermute | solution.py:43
  52.5 0.8 %copy-start = (f32[1024,128]{1,0:T(8,128)}, f32[1024,128]{1,0:T(8,128)S(1)}, u32[]{:S(2)}) copy-start(f32[1024,128]{1,0:T(8,128)S(1)} %mid.1.sum_hbm) | copy-start | bytes 1572868

commit v8 on v7

--- a/solution.py
+++ b/solution.py
@@ -449,7 +449,7 @@
     copies[0].wait()
     load_ops(ops, both)
     copies[1].wait()
-    width = CELLS // 2
+    width = CELLS
     for lo in range(0, CELLS, width):
         premultiply(pole[lo : lo + width, :], both, table, lo, CELLS)
     copies[2].wait()
@@ -466,20 +466,19 @@
 
 
 def last_kernel(
-    me_ref, index_hbm, count_ref, place_ref, far_ref, near_ref, next_ref, ops_hbm, sum_hbm, inner_hbm, outer_hbm,
+    me_ref, index_hbm, count_ref, place_ref, far_ref, near_ref, next_ref, ops, sum_hbm, inner_hbm, outer_hbm,
     down_hbm, stay_hbm, new_hbm, stay_basis_hbm, new_basis_hbm, pair_hbm, local_ref, pot_ref,
-    index_ref, table, both, sums_ref, rows, coarse, ops, inner, outer, down, atoms_ref, basis_ref, pair, sems,
+    index_ref, table, both, sums_ref, rows, coarse, inner, outer, down, atoms_ref, basis_ref, pair, sems,
 ):
     copies = load(
-        sems, (ops_hbm, ops), (sum_hbm, sums_ref), (inner_hbm, inner), (outer_hbm, outer), (down_hbm, down),
+        sems, (sum_hbm, sums_ref), (inner_hbm, inner), (outer_hbm, outer), (down_hbm, down),
         (stay_hbm, atoms_ref.at[:, pl.ds(0, STAY)]), (new_hbm, atoms_ref.at[:, pl.ds(STAY, ARRIVE)]),
         (stay_basis_hbm, basis_ref.at[:, pl.ds(0, STAY)]), (new_basis_hbm, basis_ref.at[:, pl.ds(STAY, ARRIVE)]),
         (pair_hbm, pair), (index_hbm, index_ref),
     )
     table[OPS * REMOTE :, :] = jnp.zeros((8, LANES), f32)
-    copies[0].wait()
     load_ops(ops, both)
-    width = FAR_ROWS // 4
+    width = FAR_ROWS // 2
     for lo in range(0, FAR_ROWS, width):
         premultiply(far_ref[lo : lo + width, :], both, table, lo, REMOTE)
     premultiply(near_ref[...], both, table, FAR_ROWS, REMOTE)
@@ -495,7 +494,7 @@
     away = (jnp.abs(its_group - group) - 1 == which - MEMBERS) & (which >= MEMBERS)
     chosen = jnp.where(near | away, 1.0, 0.0)
     sums = lax.dot_general(chosen, coarse[...], NN, precision=lax.Precision.HIGHEST, preferred_element_type=f32)
-    for copy in copies[1:5]:
+    for copy in copies[0:4]:
         copy.wait()
     field = jnp.sum(inner[...] * sums[None, 0 : MEMBERS - 1, 0:COEF], axis=1)
     for o in range(GROUPS - 1):
@@ -513,7 +512,7 @@
     def store(r, g, total):
         rows[pl.ds(place_ref.at[pl.ds(r * LANES, LANES)][g], 1), :] = total
 
-    copies[10].wait()
+    copies[9].wait()
     for n in range(LIST, -1, -1):
         row_sums(
             index_ref, table, n, count_ref[n + 1], count_ref[n], lambda r, g: sums_ref[pl.ds(r * LANES + g, 1), :], store
@@ -526,7 +525,7 @@
     high = jnp.concatenate([high, jnp.zeros((LANES - COEF, CELLS), bf16)], axis=0)
     rest = jnp.concatenate([rest, jnp.zeros((LANES - COEF, CELLS), bf16)], axis=0)
     stacked = jnp.concatenate([high, rest], axis=0)
-    for copy in copies[5:10]:
+    for copy in copies[4:9]:
         copy.wait()
     wide = 512
     for lo in range(0, SLOTS, wide):
@@ -627,11 +626,11 @@
         own_index, counts, pole, by_row[0],
     )
     local, pot = call(
-        last_kernel, "last", [SM, HB, SM, SM] + [VM] * 3 + [HB] * 10, [(VM, (COEF, CELLS), f32), (VM, (SLOTS // LANES, LANES), f32)],
+        last_kernel, "last", [SM, HB, SM, SM] + [VM] * 4 + [HB] * 9, [(VM, (COEF, CELLS), f32), (VM, (SLOTS // LANES, LANES), f32)],
         [index_scratch, ((OPS * REMOTE + 8, LANES), f32), ((OPS * LANES, 3 * LANES), bf16), *[((CELLS, LANES), f32)] * 2, ((DEVICES, LANES), f32),
-         ops_shape, ((COEF, MEMBERS - 1, COEF), f32), ((GROUPS - 1, COEF, COEF), f32), ops_shape, ((8, SLOTS), f32),
+         ((COEF, MEMBERS - 1, COEF), f32), ((GROUPS - 1, COEF, COEF), f32), ops_shape, ((8, SLOTS), f32),
          ((LANES, SLOTS), f32), ((1, SLOTS), f32)],
-        [11],
+        [10],
         me, far_index, counts, place, far_rows, near_rows, next_rows, by_row[0], own_sum,
         far_in.transpose(1, 0, 2), far_out, by_row[2], stay_atoms, new_atoms, stay_basis, new_basis, pair,
     )

time: 71.4 us -> 71 us (level)
  no operation moved by 1% of the time
where the time goes in v8:
time: 71 us; the launch traced here: 70.6 us
  Pallas kernels  38.8 us (55%)
  starting transfers between devices  22.5 us (32%)
  waiting for transfers between devices  7.4 us (10%)
  between operations  1.02 us (1%)
  local copies, waits for them, and re-layouts  0.84 us (1%)
    pallas_call x6, Pallas kernels, call(): pl.pallas_call(kernel, name=name, in_specs=ins, out_specs=[spec for spec,...  38.8 us
    all_to_all x1, starting transfers between devices, on_device(): lax.all_to_all(outbound.reshape(DEVICES, 1, PIECE * LANES), AXES, split_a...  11.5 us
    all_to_all x1, starting transfers between devices, on_device(): lax.all_to_all(send.reshape(DEVICES, 1, BLOCK * LANES), AXES, split_axis=...  7.27 us
    all_to_all x1, waiting for transfers between devices, on_device(): lax.all_to_all(send.reshape(DEVICES, 1, BLOCK * LANES), AXES, split_axis=...  4.46 us
    ppermute x2, starting transfers between devices, swap(): return lax.ppermute(value, AXES, pairs + [(j, i) for i, j in pairs])  3.76 us
    all_to_all x1, waiting for transfers between devices, on_device(): lax.all_to_all(outbound.reshape(DEVICES, 1, PIECE * LANES), AXES, split_a...  2.93 us
  transfers between devices with their start and end apart: 4, of which 2 were waited for; matrix products, arithmetic and copies ran while one was open for 0% of the time, Pallas kernels for 30%

profile of v8, /device:TPU:1, one launch (start us, length us, event | category | flops | bytes accessed | tf_op | source)
XLA Modules:
  0.0 70.6 jit_solution(8193335558008283178)
XLA Ops:
  0.6 0.0 copy-start.9
  0.6 0.0 copy-start.12
  0.7 0.0 copy-start.2
  0.7 1.8 %pack.1 = f32[768,128]{1,0:T(8,128)} custom-call(s32[1]{0:T(128)} %bitcast.me_ref, s32[1,72,128]{2,1,0:T(8,128)} %bitcast.43, s32[16,128]{1,0:T(8,128)} %bitcast.44, f32[4,2048]{1,0:T(4,128)} %rows_hbm.3, s32[1,2048]{1,0:T(1,128)} %bitcast.46), custom_call_target="tpu_custom_call" | custom-call | flops 1000 | bytes 1000 | tf_op jit(solution)/shard_map/pack/pallas_call | solution.py:548
  2.5 11.5 %all-to-all-start = ((f32[128,1,768]{2,1,0:T(1,128)}), f32[128,1,768]{2,1,0:T(1,128)S(1)}, u32[]{:S(2)}, u32[]{:S(2)}) async-start(f32[128,1,768]{2,1,0:T(1,128)} %bitcast.41), calls=%async_computation | async-start | bytes 786432 | tf_op jit(solution)/shard_map/all_to_all | solution.py:589
  14.0 9.4 %early.1 = (f32[8,2048]{1,0:T(8,128)}, f32[128,2048]{1,0:T(8,128)}, f32[1024,128]{1,0:T(8,128)}, f32[1,2048]{1,0:T(1,128)}, s32[16,8,128]{2,1,0:T(8,128)}, /*ind...) custom-call(s32[1]{0:T(128)} %bitcast.me_ref, s32[1,2048]{1,0:T(1,128)} %bitcast.45, f32[4,2048]{1,0:T(4,128)} %rows_hbm.3, ...), custom_call_target="tpu_custom_call" | custom-call | flops 1000 | bytes 1000 | tf_op jit(solution)/shard_map/early/pallas_call | solution.py:548
  23.4 2.9 %all-to-all-done = f32[128,1,768]{2,1,0:T(1,128)S(1)} async-done(((f32[128,1,768]{2,1,0:T(1,128)}), f32[128,1,768]{2,1,0:T(1,128)S(1)}, u32[]{:S(2)}, u32[]{:S(2)}) %all-to-all-start) | async-done | bytes 393248 | tf_op jit(solution)/shard_map/all_to_all | solution.py:589
  26.3 0.0 copy-done.9
  26.3 0.0 copy-done.12
  26.4 0.0 copy-done.2
  26.4 3.1 %merge.1 = (f32[2432,128]{1,0:T(8,128)}, f32[56,128]{1,0:T(8,128)S(1)}, f32[56,128]{1,0:T(8,128)S(1)}, f32[1024,128]{1,0:T(8,128)S(1)}, f32[128,512]{1,0:T(8,128)S(1)}, /*index=5*/f32[8,512]{1,0:T(8,128)S(1)}) custom-call(s32[1]{0:T(128)} %bitcast.me_ref, f32[768,128]{1,0:T(8,128)S(1)} %bitcast.28, f32[3,121]{1,0:T(4,128)S(1)} %bitcast.36, ...), custom_call_target="tpu_custom_call" | custom-call | flops 1000 | bytes 1000 | tf_op jit(solution)/shard_map/merge/pallas_call | solution.py:548
  29.5 0.0 copy-start.4
  29.5 0.0 copy-start.10
  29.5 0.0 copy-start.1
  29.5 0.0 copy-start.7
  29.5 0.0 copy-start.8
  29.6 7.3 %all-to-all-start.1 = ((f32[128,1,2432]{2,1,0:T(1,128)}), f32[128,1,2432]{2,1,0:T(1,128)}, u32[]{:S(2)}, u32[]{:S(2)}) async-start(f32[128,1,2432]{2,1,0:T(1,128)} %bitcast.42), calls=%async_computation.1 | async-start | bytes 2490368 | tf_op jit(solution)/shard_map/all_to_all | solution.py:613
  36.8 0.0 copy-start.3
  36.8 0.0 copy-start.5
  36.9 0.0 copy-start.6
  36.9 0.0 copy-start.11
  36.9 1.2 %collective-permute-start = (f32[56,128]{1,0:T(8,128)S(1)}, f32[56,128]{1,0:T(8,128)S(1)}, u32[]{:S(2)}, u32[]{:S(2)}) collective-permute-start(f32[56,128]{1,0:T(8,128)S(1)} %get-tuple-element.23), channel_id=1, source_target_pairs={{0,1},{2,3},{4,5},{6,7},{8,9},{10,11},{12,13},{14,15},{16,17},{18,... | collective-permute-start | bytes 86024 | tf_op jit(solution)/shard_map/ppermute | solution.py:43
  38.1 2.5 %collective-permute-start.1 = (f32[56,128]{1,0:T(8,128)S(1)}, f32[56,128]{1,0:T(8,128)S(1)}, u32[]{:S(2)}, u32[]{:S(2)}) collective-permute-start(f32[56,128]{1,0:T(8,128)S(1)} %get-tuple-element.24), channel_id=1, source_target_pairs={{1,2},{3,4},{5,6},{7,8},{9,10},{11,12},{13,14},{15,16},{17,18},{19... | collective-permute-start | bytes 86024 | tf_op jit(solution)/shard_map/ppermute | solution.py:43
  40.6 0.0 copy-done.4
  40.6 0.0 copy-done.10
  40.7 2.4 %cross.1.pair_hbm = f32[1,2560]{1,0:T(1,128)S(1)} custom-call(f32[8,2048]{1,0:T(8,128)S(1)} %copy-done.4, f32[8,512]{1,0:T(8,128)S(1)} %get-tuple-element.28.new_hbm, f32[1,2048]{1,0:T(1,128)S(1)} %copy-done.10), custom_call_target="tpu_custom_call" | custom-call | flops 1000 | bytes 1000 | tf_op jit(solution)/shard_map/cross/pallas_call | solution.py:548
  43.0 0.0 copy-done.1
  43.1 0.0 copy-done.7
  43.1 0.0 copy-done.8
  43.1 9.4 %mid.1.sum_hbm = f32[1024,128]{1,0:T(8,128)S(1)} custom-call(s32[16384]{0:T(1024)S(1)} %bitcast.32, s32[1024]{0:T(1024)S(1)} %bitcast.33, f32[1024,128]{1,0:T(8,128)S(1)} %get-tuple-element.26.pole_hbm, f32[968,121]{1,0:T(8,128)S(1)} %bitcast.26), custom_call_target="tpu_custom_call" | custom-call | flops 1000 | bytes 1000 | tf_op jit(solution)/shard_map/mid/pallas_call | solution.py:548
  52.4 0.0 copy-start
  52.4 0.8 %copy-done = f32[1024,128]{1,0:T(8,128)} copy-done((f32[1024,128]{1,0:T(8,128)}, f32[1024,128]{1,0:T(8,128)S(1)}, u32[]{:S(2)}) %copy-start) | copy-done | bytes 524312
  53.2 0.0 collective-permute-done.near_ref
  53.2 0.0 collective-permute-done.1.next_ref
  53.2 4.5 %all-to-all-done.1 = f32[128,1,2432]{2,1,0:T(1,128)} async-done(((f32[128,1,2432]{2,1,0:T(1,128)}), f32[128,1,2432]{2,1,0:T(1,128)}, u32[]{:S(2)}, u32[]{:S(2)}) %all-to-all-start.1) | async-done | bytes 1245216 | tf_op jit(solution)/shard_map/all_to_all | solution.py:613
  57.7 0.0 copy-done.3
  57.7 0.0 copy-done.5
  57.7 0.0 copy-done.6
  57.7 0.0 copy-done.11
  57.7 12.8 %last.1 = (f32[121,1024]{1,0:T(8,128)}, f32[20,128]{1,0:T(8,128)}) custom-call(s32[1]{0:T(128)} %bitcast.me_ref, s32[16384]{0:T(1024)S(1)} %bitcast.31, s32[1024]{0:T(1024)S(1)} %bitcast.34, s32[1024]{0:T(1024)S(1)} %bitcast.37, f32[2432,128]{1,0:T(8,128)} %bitcast.15.far_ref, f32[56,128]{1,0:T(8,128)S(1)} %collective-permute-done.near_ref, ...), custom_call_target="tpu_custom_call" | custom-call | flops 1000 | bytes 1000 | tf_op jit(solution)/shard_map/last/pallas_call | solution.py:548
Async XLA Ops:
  0.6 25.7 %copy-start.9 = (f32[121,3]{0,1:T(4,128)S(1)}, f32[121,3]{0,1:T(4,128)}, u32[]{:S(2)}) copy-start(f32[121,3]{0,1:T(4,128)} %param.19) | copy-start | bytes 4360
  0.6 25.7 %copy-start.12 = (f32[121]{0:T(128)S(1)}, f32[121]{0:T(128)}, u32[]{:S(2)}) copy-start(f32[121]{0:T(128)} %param.20) | copy-start | bytes 1456
  0.7 25.7 %copy-start.2 = (f32[8,121,121]{2,0,1:T(8,128)S(1)}, f32[8,121,121]{2,0,1:T(8,128)}, u32[]{:S(2)}) copy-start(f32[8,121,121]{2,0,1:T(8,128)} %param.22) | copy-start | bytes 1405540
  2.5 23.8 %all-to-all-start = ((f32[128,1,768]{2,1,0:T(1,128)}), f32[128,1,768]{2,1,0:T(1,128)S(1)}, u32[]{:S(2)}, u32[]{:S(2)}) async-start(f32[128,1,768]{2,1,0:T(1,128)} %bitcast.41), calls=%async_computation | async-start | bytes 786432 | tf_op jit(solution)/shard_map/all_to_all | solution.py:589
  29.5 11.1 %copy-start.4 = (f32[8,2048]{1,0:T(8,128)S(1)}, f32[8,2048]{1,0:T(8,128)}, u32[]{:S(2)}) copy-start(f32[8,2048]{1,0:T(8,128)} %get-tuple-element.27.stay_hbm) | copy-start | bytes 196612
  29.5 11.1 %copy-start.10 = (f32[1,2048]{1,0:T(1,128)S(1)}, f32[1,2048]{1,0:T(1,128)}, u32[]{:S(2)}) copy-start(f32[1,2048]{1,0:T(1,128)} %get-tuple-element.31.stay_pair_hbm) | copy-start | bytes 24580
  29.5 13.5 %copy-start.1 = (f32[8,121,121]{2,0,1:T(8,128)S(1)}, f32[8,121,121]{2,0,1:T(8,128)}, u32[]{:S(2)}) copy-start(f32[8,121,121]{2,0,1:T(8,128)} %param.21) | copy-start | bytes 1405540
  29.5 13.5 %copy-start.7 = (s32[16,8,128]{2,1,0:T(8,128)S(1)}, s32[16,8,128]{2,1,0:T(8,128)}, u32[]{:S(2)}) copy-start(s32[16,8,128]{2,1,0:T(8,128)} %get-tuple-element.25) | copy-start | bytes 196612
  29.5 13.5 %copy-start.8 = (s32[8,128]{1,0:T(8,128)S(1)}, s32[8,128]{1,0:T(8,128)}, u32[]{:S(2)}) copy-start(s32[8,128]{1,0:T(8,128)} %get-tuple-element.19) | copy-start | bytes 12292
  29.6 28.1 %all-to-all-start.1 = ((f32[128,1,2432]{2,1,0:T(1,128)}), f32[128,1,2432]{2,1,0:T(1,128)}, u32[]{:S(2)}, u32[]{:S(2)}) async-start(f32[128,1,2432]{2,1,0:T(1,128)} %bitcast.42), calls=%async_computation.1 | async-start | bytes 2490368 | tf_op jit(solution)/shard_map/all_to_all | solution.py:613
  36.8 20.9 %copy-start.3 = (f32[8,121,121]{2,0,1:T(8,128)S(1)}, f32[8,121,121]{2,0,1:T(8,128)}, u32[]{:S(2)}) copy-start(f32[8,121,121]{2,0,1:T(8,128)} %param.25) | copy-start | bytes 1405540
  36.8 20.9 %copy-start.5 = (f32[3,121,121]{2,1,0:T(8,128)S(1)}, f32[3,121,121]{2,1,0:T(8,128)}, u32[]{:S(2)}) copy-start(f32[3,121,121]{2,1,0:T(8,128)} %outer_hbm.1) | copy-start | bytes 527080
  36.9 20.8 %copy-start.6 = (s32[16,8,128]{2,1,0:T(8,128)S(1)}, s32[16,8,128]{2,1,0:T(8,128)}, u32[]{:S(2)}) copy-start(s32[16,8,128]{2,1,0:T(8,128)} %get-tuple-element.18) | copy-start | bytes 196612
  36.9 20.8 %copy-start.11 = (s32[8,128]{1,0:T(8,128)S(1)}, s32[8,128]{1,0:T(8,128)}, u32[]{:S(2)}) copy-start(s32[8,128]{1,0:T(8,128)} %get-tuple-element.20) | copy-start | bytes 12292
  36.9 16.4 %collective-permute-start = (f32[56,128]{1,0:T(8,128)S(1)}, f32[56,128]{1,0:T(8,128)S(1)}, u32[]{:S(2)}, u32[]{:S(2)}) collective-permute-start(f32[56,128]{1,0:T(8,128)S(1)} %get-tuple-element.23), channel_id=1, source_target_pairs={{0,1},{2,3},{4,5},{6,7},{8,9},{10,11},{12,13},{14,15},{16,17},{18,... | collective-permute-start | bytes 86024 | tf_op jit(solution)/shard_map/ppermute | solution.py:43
  38.1 15.1 %collective-permute-start.1 = (f32[56,128]{1,0:T(8,128)S(1)}, f32[56,128]{1,0:T(8,128)S(1)}, u32[]{:S(2)}, u32[]{:S(2)}) collective-permute-start(f32[56,128]{1,0:T(8,128)S(1)} %get-tuple-element.24), channel_id=1, source_target_pairs={{1,2},{3,4},{5,6},{7,8},{9,10},{11,12},{13,14},{15,16},{17,18},{19... | collective-permute-start | bytes 86024 | tf_op jit(solution)/shard_map/ppermute | solution.py:43
  52.4 0.8 %copy-start = (f32[1024,128]{1,0:T(8,128)}, f32[1024,128]{1,0:T(8,128)S(1)}, u32[]{:S(2)}) copy-start(f32[1024,128]{1,0:T(8,128)S(1)} %mid.1.sum_hbm) | copy-start | bytes 1572868
